TPU v7x, 512 devices: a whole 4x8x8 slice. The times are simulated.
512 devices in a mesh: member: 16 (over z, core), tile: 32 (over y, x).
Axes of the slice: x: 4, y: 8, z: 8, core: 2. Of those that a mesh axis runs over, the one named last changes fastest.
Arguments:
- control: float32 [16, 96, 8, 4096], P('member', None, None, 'tile'), may hold values from -70 to 70
- members: bfloat16 [16, 96, 8, 4096], P('member', None, None, 'tile'), may hold values from -4 to 4
- obs_weight: float32 [96, 8, 4096], P(None, None, 'tile'), may hold values from 0.3 to 3
- innovation: float32 [96, 8, 4096], P(None, None, 'tile'), may hold values from -5 to 5
- scale_index: int32 [96], replicated, may hold values from 0 to 3
Outputs:
- increment: float32 [96, 8, 4096], P('member', None, 'tile')
- gradient: float32 [16, 96, 8, 4096], P('member', None, None, 'tile')
- cost_value: float32 [], replicated
- mean_square: float32 [], replicated
All inputs are finite; a program needn't handle non-finite values.
Results may differ from a plain program's by a relative error of at most 0.0003.
Values sent between devices are 32-bit elements; how exact they have to be, the bound alone decides.
No kernel may reach another device: no remote copies, remote signals or barrier semaphores. Data moves between devices by JAX's collectives and lax.ppermute only.
A program may use at most 64 MiB of HBM per device.

v0:
```python
import jax
import jax.numpy as jnp
from jax import lax
from jax.sharding import PartitionSpec as P

precise = lax.Precision.HIGHEST


def vertical_matrix(level_scale):
    levels = jnp.arange(level_scale.shape[0]).astype(jnp.float32)
    spacing = levels[:, None] - levels[None, :]
    spread = (
        level_scale[:, None] * level_scale[:, None] + level_scale[None, :] * level_scale[None, :]
    )
    return jnp.exp(-spacing * spacing / spread)


def lon_bands(level_scale, half_width):
    spread_lon = half_width * level_scale / 4.0
    inputs = jnp.arange(3 * half_width).astype(jnp.float32)[:, None]
    outputs = jnp.arange(half_width).astype(jnp.float32)[None, :]
    spacing = inputs - half_width - outputs
    distance = jnp.arange(-half_width, half_width + 1).astype(jnp.float32)
    squared = spread_lon[:, None] * spread_lon[:, None]
    norm_sum = jnp.sqrt(jnp.sum(jnp.exp(-distance[None, :] * distance[None, :] / squared), axis=1))
    weight = jnp.exp(
        -spacing[None]
        * spacing[None]
        / (2.0 * spread_lon[:, None, None] * spread_lon[:, None, None])
    )
    weight = jnp.where(jnp.abs(spacing)[None] <= half_width, weight, 0.0)
    return weight / norm_sum[:, None, None]


def lat_matrix(level_scale, lat_rows):
    spread_lat = lat_rows * level_scale / 8.0
    positions = jnp.arange(lat_rows).astype(jnp.float32)
    spacing = positions[:, None] - positions[None, :]
    distance = jnp.arange(-(lat_rows - 1), lat_rows).astype(jnp.float32)
    squared = spread_lat[:, None] * spread_lat[:, None]
    norm_sum = jnp.sqrt(jnp.sum(jnp.exp(-distance[None, :] * distance[None, :] / squared), axis=1))
    weight = jnp.exp(
        -spacing[None]
        * spacing[None]
        / (2.0 * spread_lat[:, None, None] * spread_lat[:, None, None])
    )
    return weight / norm_sum[:, None, None]


def apply_lon(blocks, banded):
    windows = jnp.concatenate([blocks[:, :, :-2], blocks[:, :, 1:-1], blocks[:, :, 2:]], axis=3)
    result = jnp.einsum("lakd,ldj->lakj", windows, banded, precision=precise)
    return result.reshape(result.shape[0], result.shape[1], -1)


def vertical_apply(matrix, values):
    return jnp.einsum("kq,qao->kao", matrix, values, precision=precise)


def lat_apply(matrix, values):
    return jnp.einsum("lab,lbo->lao", matrix, values, precision=precise)


def lon_filter(values, banded):
    half_width = banded.shape[2]
    levels, lat_rows, lon_cells = values.shape
    slab_field = lax.all_to_all(values, "tile", split_axis=0, concat_axis=2, tiled=True)
    slab_levels = slab_field.shape[0]
    section = lax.dynamic_slice_in_dim(banded, lax.axis_index("tile") * slab_levels, slab_levels, 0)
    blocks = slab_field.reshape(slab_levels, lat_rows, -1, half_width)
    blocks = jnp.concatenate([blocks[:, :, -1:], blocks, blocks[:, :, :1]], axis=2)
    return lax.all_to_all(
        apply_lon(blocks, section), "tile", split_axis=2, concat_axis=0, tiled=True
    )


def per_device(control, members, obs_weight, innovation, scale_index):
    level_scale = 1.0 + scale_index.astype(jnp.float32)
    levels, lat_rows, lon_cells = obs_weight.shape
    vertical = vertical_matrix(level_scale)
    banded = lon_bands(level_scale, lon_cells // 2)
    meridional = lat_matrix(level_scale, lat_rows)
    groups = lax.axis_size("member")
    tile_count = lax.axis_size("tile")
    inverse = 1.0 / jnp.sqrt(jnp.float32(groups - 1))
    cell_count = float(groups * levels * lat_rows * lon_cells * tile_count)
    control_one = control[0]
    member_one = members[0].astype(jnp.float32)
    alpha_field = lat_apply(meridional, lon_filter(vertical_apply(vertical, control_one), banded))
    member_term = member_one * alpha_field * inverse
    slab_levels = levels // groups
    first_level = lax.axis_index("member") * slab_levels
    weight_share = lax.dynamic_slice_in_dim(obs_weight, first_level, slab_levels, 0)
    innovation_share = lax.dynamic_slice_in_dim(innovation, first_level, slab_levels, 0)
    inc_total = lax.psum(member_term, "member")
    inc_share = lax.dynamic_slice_in_dim(inc_total, first_level, slab_levels, 0)
    misfit = obs_weight * inc_total - innovation
    control_sum = jnp.sum(control_one * control_one)
    misfit_sum = jnp.sum(0.5 * weight_share * inc_share * inc_share - innovation_share * inc_share)
    weighted = member_one * misfit * inverse
    adjoint_field = vertical_apply(vertical, lon_filter(lat_apply(meridional, weighted), banded))
    gradient = control_one + adjoint_field
    gradient_sum = jnp.sum(gradient * gradient)
    control_total, misfit_total = lax.psum((control_sum, misfit_sum), ("member", "tile"))
    gradient_total = lax.psum(gradient_sum, ("member", "tile"))
    cost_value = (0.5 * control_total + misfit_total) / cell_count
    mean_square = gradient_total / cell_count
    return (inc_share, gradient[None], cost_value, mean_square)


def solution(mesh):
    placed = (
        P("member", None, None, "tile"),
        P("member", None, None, "tile"),
        P(None, None, "tile"),
        P(None, None, "tile"),
        P(),
    )
    return jax.shard_map(
        per_device,
        mesh=mesh,
        in_specs=placed,
        out_specs=(P("member", None, "tile"), P("member", None, None, "tile"), P(), P()),
        check_vma=False,
    )
```

profile of v0, /device:TPU:1, one launch (start us, length us, event | category | flops | bytes accessed | tf_op | source)
XLA Modules:
  0.0 389.5 jit_solution(12140294566916616830)
XLA Ops:
  7.2 0.7 multiply_multiply_fusion.1
  7.8 1.5 fusion.21
  9.4 1.0 copy.42
  10.3 10.5 %all-to-all-start = ((f32[96,8,128]{2,1,0:T(8,128)}), f32[96,8,128]{2,1,0:T(8,128)S(1)}, u32[]{:S(2)}, u32[]{:S(2)}) async-start(f32[96,8,128]{2,1,0:T(8,128)} %copy.42), calls=%async_computation | async-start | bytes 786432 | tf_op jit(solution)/shard_map/all_to_all | solution.py:67
  20.9 0.1 fusion.47
  21.0 0.1 dynamic-slice.1
  21.1 0.1 dynamic-slice
  21.2 0.1 fusion.48
  21.3 0.1 subtract_multiply_fusion
  21.3 13.3 %all-to-all-done = f32[96,8,128]{2,1,0:T(8,128)S(1)} async-done(((f32[96,8,128]{2,1,0:T(8,128)}), f32[96,8,128]{2,1,0:T(8,128)S(1)}, u32[]{:S(2)}, u32[]{:S(2)}) %all-to-all-start) | async-done | bytes 393248 | tf_op jit(solution)/shard_map/all_to_all | solution.py:67
  34.7 0.1 copy.43
  34.7 0.2 reshape.179
  35.0 1.8 fusion.8
  36.8 5.9 %copy.53 = f32[3,8,64,64]{1,0,3,2:T(4,128)} copy(f32[3,8,64,64]{3,2,1,0:T(8,128)S(1)} %fusion.8) | data formatting | bytes 786432 | tf_op jit(solution)/shard_map/reshape | solution.py:53
  42.7 9.0 %reshape.186 = f32[32,1,3072]{2,1,0:T(1,128)} reshape(f32[4096,3,8]{2,1,0:T(4,128)} %bitcast.53) | data formatting | bytes 786432
  51.7 5.0 %all-to-all-start.1 = ((f32[32,1,3072]{2,1,0:T(1,128)}), f32[32,1,3072]{2,1,0:T(1,128)S(1)}, u32[]{:S(2)}, u32[]{:S(2)}) async-start(f32[32,1,3072]{2,1,0:T(1,128)} %reshape.186), calls=%async_computation.1 | async-start | bytes 786432 | tf_op jit(solution)/shard_map/all_to_all | solution.py:72
  56.7 0.0 all-reduce.3.cloned.1.call-start
  56.7 0.1 fusion.64
  56.8 0.1 negate_multiply_fusion.1
  56.9 12.6 %all-to-all-done.1 = f32[32,1,3072]{2,1,0:T(1,128)S(1)} async-done(((f32[32,1,3072]{2,1,0:T(1,128)}), f32[32,1,3072]{2,1,0:T(1,128)S(1)}, u32[]{:S(2)}, u32[]{:S(2)}) %all-to-all-start.1) | async-done | bytes 393248 | tf_op jit(solution)/shard_map/all_to_all | solution.py:72
  69.6 0.5 broadcast.108
  70.1 1.6 reduce
  71.6 6.8 %reshape.187 = f32[4096,3,8]{2,1,0:T(4,128)} reshape(f32[32,3072]{1,0:T(8,128)S(1)} %reduce) | data formatting | bytes 786432
  78.4 6.4 %copy.45 = f32[3,8,32,128]{3,1,0,2:T(8,128)S(1)} copy(f32[3,8,32,128]{1,0,3,2:T(4,128)} %bitcast.54) | data formatting | bytes 786432 | tf_op jit(solution)/shard_map/all_to_all | solution.py:72
  84.8 0.0 copy-done.3
  84.8 0.0 copy-start.1
  84.8 0.0 copy-start.2
  84.8 1.7 fusion.16
  86.5 0.0 all-reduce.3.cloned.1.call-update
  86.5 117.5 %all-reduce.3.cloned.1.call-done = f32[96,8,128]{2,1,0:T(8,128)} async-done(((f32[96,8,128]{2,1,0:T(8,128)}), f32[96,8,128]{2,1,0:T(8,128)}) %all-reduce.3.cloned.1.call-update) | async-done | bytes 393232 | tf_op jit(solution)/shard_map/psum | solution.py:95
  204.0 0.0 copy-done.2
  204.0 1.9 fusion.19
  206.0 22.9 %all_to_all.66 = f32[96,8,128]{2,1,0:T(8,128)S(1)} all-to-all(f32[96,8,128]{2,1,0:T(8,128)S(1)} %fusion.19), channel_id=1, replica_groups=mesh['member'=16,'tile'=32] {'tile'}, dimensions={0} | all-to-all | bytes 786432 | tf_op jit(solution)/shard_map/all_to_all | solution.py:67
  228.8 0.1 copy.46
  228.9 0.2 reshape.181
  229.1 1.8 fusion.1
  231.0 5.9 %copy.54 = f32[3,8,64,64]{1,0,3,2:T(4,128)} copy(f32[3,8,64,64]{3,2,1,0:T(8,128)S(1)} %fusion.1) | data formatting | bytes 786432 | tf_op jit(solution)/shard_map/reshape | solution.py:53
  236.9 9.0 %reshape.188 = f32[32,1,3072]{2,1,0:T(1,128)} reshape(f32[4096,3,8]{2,1,0:T(4,128)} %bitcast.55) | data formatting | bytes 786432
  245.9 5.0 %all-to-all-start.3 = ((f32[32,1,3072]{2,1,0:T(1,128)}), f32[32,1,3072]{2,1,0:T(1,128)S(1)}, u32[]{:S(2)}, u32[]{:S(2)}) async-start(f32[32,1,3072]{2,1,0:T(1,128)} %reshape.188), calls=%async_computation.3 | async-start | bytes 786432 | tf_op jit(solution)/shard_map/all_to_all | solution.py:72
  250.9 0.7 fusion.23
  251.6 1.9 fusion.55
  253.6 10.2 %all-to-all-done.3 = f32[32,1,3072]{2,1,0:T(1,128)S(1)} async-done(((f32[32,1,3072]{2,1,0:T(1,128)}), f32[32,1,3072]{2,1,0:T(1,128)S(1)}, u32[]{:S(2)}, u32[]{:S(2)}) %all-to-all-start.3) | async-done | bytes 393248 | tf_op jit(solution)/shard_map/all_to_all | solution.py:72
  263.8 1.6 reduce.1
  265.4 6.8 %reshape.189 = f32[4096,3,8]{2,1,0:T(4,128)} reshape(f32[32,3072]{1,0:T(8,128)S(1)} %reduce.1) | data formatting | bytes 786432
  272.1 6.3 %copy.56 = f32[3,8,32,128]{3,1,0,2:T(8,128)S(1)} copy(f32[3,8,32,128]{1,0,3,2:T(4,128)} %bitcast.56) | data formatting | bytes 786432 | tf_op jit(solution)/shard_map/all_to_all | solution.py:72
  278.5 1.3 multiply_reduce_fusion
  279.7 1.0 copy.51
  280.7 97.7 %all-reduce = (f32[]{:T(128)}, f32[]{:T(128)}, f32[]{:T(128)}) all-reduce(f32[]{:T(128)} %fusion.23, f32[]{:T(128)} %get-tuple-element.27, f32[]{:T(128)} %get-tuple-element.37), channel_id=1, replica_groups=mesh['member'=16,'tile'=32] {'member','tile'}, use_global_device_ids=true, to_apply=%region_4.5 | all-reduce | flops 3 | bytes 24 | tf_op jit(solution)/shard_map/psum | solution.py:104
  (14 shorter events, 0.1 us)
Async XLA Ops:
  10.3 24.3 %all-to-all-start = ((f32[96,8,128]{2,1,0:T(8,128)}), f32[96,8,128]{2,1,0:T(8,128)S(1)}, u32[]{:S(2)}, u32[]{:S(2)}) async-start(f32[96,8,128]{2,1,0:T(8,128)} %copy.42), calls=%async_computation | async-start | bytes 786432 | tf_op jit(solution)/shard_map/all_to_all | solution.py:67
  51.7 17.9 %all-to-all-start.1 = ((f32[32,1,3072]{2,1,0:T(1,128)}), f32[32,1,3072]{2,1,0:T(1,128)S(1)}, u32[]{:S(2)}, u32[]{:S(2)}) async-start(f32[32,1,3072]{2,1,0:T(1,128)} %reshape.186), calls=%async_computation.1 | async-start | bytes 786432 | tf_op jit(solution)/shard_map/all_to_all | solution.py:72
  56.7 147.4 %all-reduce.3.cloned.1.call-start = ((), (), s32[]{:S(2)}) async-start(), calls=%async_computation.4 | async-start | bytes 786432 | tf_op jit(solution)/shard_map/psum | solution.py:95
  78.4 6.4 %copy-start.3 = (bf16[1,96,8,128]{3,2,1,0:T(8,128)(2,1)S(1)}, bf16[1,96,8,128]{3,2,1,0:T(8,128)(2,1)}, u32[]{:S(2)}) copy-start(bf16[1,96,8,128]{3,2,1,0:T(8,128)(2,1)} %param.6) | copy-start | bytes 589828
  84.8 119.2 %copy-start.1 = (f32[96,8,128]{2,1,0:T(8,128)S(1)}, f32[96,8,128]{2,1,0:T(8,128)}, u32[]{:S(2)}) copy-start(f32[96,8,128]{2,1,0:T(8,128)} %param.8) | copy-start | bytes 1179652
  84.8 119.2 %copy-start.2 = (f32[96,8,128]{2,1,0:T(8,128)S(1)}, f32[96,8,128]{2,1,0:T(8,128)}, u32[]{:S(2)}) copy-start(f32[96,8,128]{2,1,0:T(8,128)} %param.7) | copy-start | bytes 1179652
  236.9 14.0 %copy-start = (f32[1,96,8,128]{3,2,1,0:T(8,128)S(1)}, f32[1,96,8,128]{3,2,1,0:T(8,128)}, u32[]{:S(2)}) copy-start(f32[1,96,8,128]{3,2,1,0:T(8,128)} %param.5) | copy-start | bytes 1179652
  245.9 17.9 %all-to-all-start.3 = ((f32[32,1,3072]{2,1,0:T(1,128)}), f32[32,1,3072]{2,1,0:T(1,128)S(1)}, u32[]{:S(2)}, u32[]{:S(2)}) async-start(f32[32,1,3072]{2,1,0:T(1,128)} %reshape.188), calls=%async_computation.3 | async-start | bytes 786432 | tf_op jit(solution)/shard_map/all_to_all | solution.py:72
Sparse Core Ops, SparseCore 0:
  86.7 117.3 all-reduce.2
where the time goes:
time: 391 us; the launch traced here: 389 us
  waiting for transfers between devices  154 us (39%)
  blocking collectives  121 us (31%)
  local copies, waits for them, and re-layouts  59.3 us (15%)
  starting transfers between devices  20.5 us (5%)
  between operations  18.4 us (5%)
  matrix products  9.98 us (3%)
  other arithmetic  6.94 us (2%)
    psum x1, waiting for transfers between devices, per_device(): inc_total = lax.psum(member_term, 'member')  118 us
    psum x1, blocking collectives, per_device(): lax.psum((control_sum, misfit_sum), ('member', 'tile'))  97.7 us
    unnamed x13, local copies, waits for them, and re-layouts  32.6 us
    all_to_all x1, blocking collectives, lon_filter(): lax.all_to_all(values, 'tile', split_axis=0, concat_axis=2, tiled=True)  22.9 us
    all_to_all x2, waiting for transfers between devices, lon_filter(): lax.all_to_all(apply_lon(blocks, section), 'tile', split_axis=2, concat_a...  22.8 us
    all_to_all x1, waiting for transfers between devices, lon_filter(): lax.all_to_all(values, 'tile', split_axis=0, concat_axis=2, tiled=True)  13.3 us
    all_to_all x3, local copies, waits for them, and re-layouts, lon_filter(): lax.all_to_all(apply_lon(blocks, section), 'tile', split_axis=2, concat_a...  13.2 us
    reshape x2, local copies, waits for them, and re-layouts, apply_lon(): return result.reshape(result.shape[0], result.shape[1], -1)  11.8 us
  transfers between devices with their start and end apart: 4, of which 4 were waited for; matrix products, arithmetic and copies ran while one was open for 1% of the time, Pallas kernels for 0%

commit v1 on v0

v1 whole, which is shorter than its diff:
```python
import functools

import jax
import jax.numpy as jnp
import numpy as np
from jax import lax
from jax.experimental import pallas as pl
from jax.experimental.pallas import tpu as pltpu
from jax.sharding import PartitionSpec as P

CLASSES = 4
VMEM_LIMIT = 48 * 1024 * 1024
f32, bf16 = jnp.float32, jnp.bfloat16


def vmem(count):
    return [pl.BlockSpec(memory_space=pltpu.VMEM)] * count


def smem():
    return pl.BlockSpec(memory_space=pltpu.SMEM)


def params():
    return pltpu.CompilerParams(vmem_limit_bytes=VMEM_LIMIT)


def split(value):
    high = value.astype(bf16)
    low = (value - high.astype(f32)).astype(bf16)
    return high, low


def dot(a, b):
    return jnp.dot(a, b, preferred_element_type=f32)


def left_product(high, low, value):
    vhigh, vlow = split(value)
    width = value.shape[1]
    both = dot(high, jnp.concatenate([vhigh, vlow], axis=1))
    return both[:, :width] + both[:, width:] + dot(low, vhigh)


def band_product(value, high, low):
    vhigh, vlow = split(value)
    return dot(vhigh, high) + dot(vlow, high) + dot(vhigh, low)


def lane_is_low(shape, half):
    return lax.broadcasted_iota(jnp.int32, shape, len(shape) - 1) < half


def pack_halves(x, to_right, to_left):
    half_levels, _, columns = to_right.shape
    half = columns // 2
    first = x[:half_levels]
    second = x[half_levels:]
    turned = pltpu.roll(second.reshape(-1, columns), half, 1).reshape(second.shape)
    low = lane_is_low(first.shape, half)
    to_right[...] = jnp.where(low, turned, first)
    to_left[...] = jnp.where(low, first, turned)


def unpack_halves(from_left, from_right):
    columns = from_left.shape[2]
    half = columns // 2
    low = lane_is_low(from_left.shape, half)
    first = jnp.where(low, from_right, from_left).reshape(-1, columns)
    second = pltpu.roll(jnp.where(low, from_left, from_right).reshape(-1, columns), half, 1)
    return jnp.concatenate([first, second], axis=0)


def pick_class(classes, all_ref, out_ref, rows, columns):
    for level in range(out_ref.shape[0] // rows):
        at = pl.multiple_of(classes[level] * columns, columns)
        out_ref[pl.ds(level * rows, rows), :] = all_ref[pl.ds(level * rows, rows), pl.ds(at, columns)]


def pack_kernel(x_ref, right_ref, left_ref):
    pack_halves(x_ref[...], right_ref, left_ref)


def class_scale(c):
    return 1.0 + float(c)


def prep_kernel(classes, col_ref, row_ref, x_ref, fh_ref, fl_ref, ah_ref, al_ref, bh_ref, bl_ref, y_ref, sum_ref, wide_ref, pat_ref):
    levels, lat, columns = x_ref.shape
    rows = levels * lat
    half = columns // 2
    scale_col = 1.0 + col_ref[...].astype(f32)
    scale_row = 1.0 + row_ref[...].astype(f32)
    k = lax.broadcasted_iota(jnp.int32, (levels, levels), 0).astype(f32)
    q = lax.broadcasted_iota(jnp.int32, (levels, levels), 1).astype(f32)
    spacing = k - q
    vertical = jnp.exp(-spacing * spacing / (scale_col * scale_col + scale_row * scale_row))
    which = lax.broadcasted_iota(jnp.int32, (levels, rows), 1) // lat
    spread = (which == lax.broadcasted_iota(jnp.int32, (levels, rows), 0)).astype(f32).astype(bf16)
    vh, vl = split(vertical)
    wide_ref[...] = dot(vh, spread) + dot(vl, spread)
    row8 = jnp.broadcast_to(row_ref[...].astype(f32), (8, levels)).astype(bf16)
    class_wide = dot(row8, spread)[:1]
    i = lax.broadcasted_iota(jnp.int32, (lat, rows), 0)
    j = lax.broadcasted_iota(jnp.int32, (lat, rows), 1) % lat
    gap = (i - j).astype(f32)
    own = jnp.zeros((lat, rows), f32)
    for c in range(CLASSES):
        rho = lat * class_scale(c) / 8.0
        e = np.arange(-(lat - 1), lat, dtype=np.float32)
        norm = float(np.sqrt(np.sum(np.exp(-e * e / np.float32(rho * rho)), dtype=np.float32)))
        pattern = jnp.exp(-gap * gap / (2.0 * rho * rho)) / norm
        pat_ref[c] = pattern
        own = jnp.where(class_wide == float(c), pattern, own)
    for pair in range(levels // 2):
        forward, adjoint = [], []
        for level in (2 * pair, 2 * pair + 1):
            line = wide_ref[pl.ds(level, 1), :]
            forward.append(line * pat_ref[classes[level]])
            adjoint.append(line * own)
        at = pl.ds(2 * pair * lat, 2 * lat)
        fh_ref[at, :], fl_ref[at, :] = split(jnp.concatenate(forward, axis=0))
        ah_ref[at, :], al_ref[at, :] = split(jnp.concatenate(adjoint, axis=0))
    d = lax.broadcasted_iota(jnp.int32, (2 * columns, columns), 0)
    out = lax.broadcasted_iota(jnp.int32, (2 * columns, columns), 1)
    place = jnp.where(d < columns, d, jnp.where(d < columns + half, d, d - 2 * columns))
    far = (place - out).astype(f32)
    inside = jnp.abs(far) <= half
    for c in range(CLASSES):
        sigma = half * class_scale(c) / 4.0
        e = np.arange(-half, half + 1, dtype=np.float32)
        norm = float(np.sqrt(np.sum(np.exp(-e * e / np.float32(sigma * sigma)), dtype=np.float32)))
        band = jnp.where(inside, jnp.exp(-far * far / (2.0 * sigma * sigma)) / norm, 0.0)
        at = pl.ds(c * columns, columns)
        bh_ref[:, at], bl_ref[:, at] = split(band)
    x = x_ref[...].reshape(rows, columns)
    sum_ref[...] = 0.5 * jnp.sum(x * x, axis=0, keepdims=True)
    y_ref[...] = left_product(fh_ref[...], fl_ref[...], x)


def forward_kernel(inverse, classes, fl_in, fr_in, y_ref, fh_ref, flo_ref, bh_ref, bl_ref, m_ref, out_ref, all_ref, picked_ref):
    levels, lat, columns = m_ref.shape
    halo = left_product(fh_ref[...], flo_ref[...], unpack_halves(fl_in[...], fr_in[...]))
    window = jnp.concatenate([y_ref[...], halo], axis=1)
    all_ref[...] = band_product(window, bh_ref[...], bl_ref[...])
    pick_class(classes, all_ref, picked_ref, lat, columns)
    out_ref[...] = m_ref[...].astype(f32) * picked_ref[...].reshape(levels, lat, columns) * inverse


def middle_kernel(got_ref, weight_ref, innovation_ref, sum_in, inc_ref, misfit_ref, sum_ref):
    inc = jnp.sum(got_ref[...], axis=0)
    weight, innovation = weight_ref[...], innovation_ref[...]
    inc_ref[...] = inc
    misfit_ref[...] = weight * inc - innovation
    cost = 0.5 * weight * inc * inc - innovation * inc
    sum_ref[...] = sum_in[...] + jnp.sum(cost.reshape(-1, cost.shape[2]), axis=0, keepdims=True)


def weight_kernel(inverse, m_ref, misfit_ref, w_ref, right_ref, left_ref):
    w = m_ref[...].astype(f32) * misfit_ref[...] * inverse
    w_ref[...] = w
    pack_halves(w, right_ref, left_ref)


def local_kernel(classes, w_ref, x_ref, bh_ref, bl_ref, ah_ref, al_ref, out_ref, all_ref, picked_ref):
    levels, lat, columns = w_ref.shape
    rows = levels * lat
    all_ref[...] = band_product(w_ref[...].reshape(rows, columns), bh_ref[:columns], bl_ref[:columns])
    pick_class(classes, all_ref, picked_ref, lat, columns)
    part = left_product(ah_ref[...], al_ref[...], picked_ref[...])
    out_ref[...] = x_ref[...] + part.reshape(levels, lat, columns)


def adjoint_kernel(classes, fl_in, fr_in, part_ref, bh_ref, bl_ref, ah_ref, al_ref, sum_in, grad_ref, sums_ref, all_ref, picked_ref):
    levels, lat, columns = part_ref.shape
    halo = unpack_halves(fl_in[...], fr_in[...])
    all_ref[...] = band_product(halo, bh_ref[columns:], bl_ref[columns:])
    pick_class(classes, all_ref, picked_ref, lat, columns)
    edge = left_product(ah_ref[...], al_ref[...], picked_ref[...])
    grad = part_ref[...] + edge.reshape(levels, lat, columns)
    grad_ref[...] = grad
    flat = grad.reshape(-1, columns)
    square = jnp.sum(flat * flat, axis=0, keepdims=True)
    sums = jnp.concatenate([square, sum_in[...]], axis=0)
    sums_ref[...] = jnp.broadcast_to(sums[None], sums_ref.shape)


def per_device(tiles, control, members, obs_weight, innovation, scale_index):
    x = control[0]
    member = members[0]
    levels, lat, columns = x.shape
    rows = levels * lat
    groups = lax.axis_size("member")
    share = levels // groups
    cells = float(groups * rows * columns * tiles)
    inverse = float(np.float32(1.0) / np.sqrt(np.float32(groups - 1)))
    shape = jax.ShapeDtypeStruct
    half_pack = shape((levels // 2, lat, columns), f32)
    field = shape((levels, lat, columns), f32)
    square = shape((rows, rows), bf16)
    band = shape((2 * columns, CLASSES * columns), bf16)
    line = shape((1, columns), f32)
    scratch = [pltpu.VMEM((rows, CLASSES * columns), f32), pltpu.VMEM((rows, columns), f32)]
    to_right = [(i, (i + 1) % tiles) for i in range(tiles)]
    to_left = [(i, (i - 1) % tiles) for i in range(tiles)]

    first_level = lax.axis_index("member") * share
    weight_share = lax.dynamic_slice_in_dim(obs_weight, first_level, share, 0)
    innovation_share = lax.dynamic_slice_in_dim(innovation, first_level, share, 0)

    right, left = pl.pallas_call(pack_kernel, out_shape=(half_pack, half_pack), in_specs=vmem(1), out_specs=tuple(vmem(2)), compiler_params=params(), name="pack_control")(x)
    from_left = lax.ppermute(right, "tile", to_right)
    from_right = lax.ppermute(left, "tile", to_left)
    fh, fl, ah, al, bh, bl, y, half_sum = pl.pallas_call(
        prep_kernel,
        out_shape=(square, square, square, square, band, band, shape((rows, columns), f32), line),
        in_specs=[smem()] + vmem(3),
        out_specs=tuple(vmem(8)),
        scratch_shapes=[pltpu.VMEM((levels, rows), f32), pltpu.VMEM((CLASSES, lat, rows), f32)],
        compiler_params=params(),
        cost_estimate=pl.CostEstimate(flops=6 * rows * rows * columns, bytes_accessed=6 * 1024 * 1024, transcendentals=300000),
        name="operators",
    )(scale_index, scale_index.reshape(levels, 1), scale_index.reshape(1, levels), x)
    term = pl.pallas_call(
        functools.partial(forward_kernel, inverse),
        out_shape=field,
        in_specs=[smem()] + vmem(8),
        out_specs=vmem(1)[0],
        scratch_shapes=scratch,
        compiler_params=params(),
        name="forward",
    )(scale_index, from_left, from_right, y, fh, fl, bh, bl, member)
    got = lax.all_to_all(term.reshape(groups, share, lat, columns), "member", 0, 0)
    inc, misfit_share, sums = pl.pallas_call(
        middle_kernel,
        out_shape=(shape((share, lat, columns), f32), shape((share, lat, columns), f32), line),
        in_specs=vmem(4),
        out_specs=tuple(vmem(3)),
        compiler_params=params(),
        name="middle",
    )(got, weight_share, innovation_share, half_sum)
    misfit = lax.all_gather(misfit_share, "member", axis=0, tiled=True)
    w, right, left = pl.pallas_call(
        functools.partial(weight_kernel, inverse),
        out_shape=(field, half_pack, half_pack),
        in_specs=vmem(2),
        out_specs=tuple(vmem(3)),
        compiler_params=params(),
        name="weighted",
    )(member, misfit)
    from_left = lax.ppermute(right, "tile", to_right)
    from_right = lax.ppermute(left, "tile", to_left)
    part = pl.pallas_call(
        local_kernel,
        out_shape=field,
        in_specs=[smem()] + vmem(6),
        out_specs=vmem(1)[0],
        scratch_shapes=scratch,
        compiler_params=params(),
        cost_estimate=pl.CostEstimate(flops=8 * rows * rows * columns, bytes_accessed=4 * 1024 * 1024, transcendentals=0),
        name="local",
    )(scale_index, w, x, bh, bl, ah, al)
    grad, sums = pl.pallas_call(
        adjoint_kernel,
        out_shape=(field, shape((groups, 2, columns), f32)),
        in_specs=[smem()] + vmem(8),
        out_specs=tuple(vmem(2)),
        scratch_shapes=scratch,
        compiler_params=params(),
        name="adjoint",
    )(scale_index, from_left, from_right, part, bh, bl, ah, al, sums)
    sums = jnp.sum(lax.all_to_all(sums, "member", 0, 0), axis=0)
    sums = jnp.broadcast_to(sums[None], (tiles,) + sums.shape)
    sums = jnp.sum(lax.all_to_all(sums, "tile", 0, 0), axis=(0, 2)) / cells
    return inc, grad[None], sums[1], sums[0]


def solution(mesh):
    placed = (
        P("member", None, None, "tile"),
        P("member", None, None, "tile"),
        P(None, None, "tile"),
        P(None, None, "tile"),
        P(),
    )
    return jax.shard_map(
        functools.partial(per_device, mesh.shape["tile"]),
        mesh=mesh,
        in_specs=placed,
        out_specs=(P("member", None, "tile"), P("member", None, None, "tile"), P(), P()),
        check_vma=False,
    )
```

time: 391 us -> 112 us (0.29)
  waiting for transfers between devices: 154 us -> 15.9 us
  blocking collectives: 121 us -> 46.7 us
  local copies, waits for them, and re-layouts: 59.3 us -> 5.5 us
  between operations: 18.4 us -> 0.76 us
  Pallas kernels: 0 us -> 11.7 us
  starting transfers between devices: 20.5 us -> 30.6 us
  matrix products: 9.98 us -> 0 us
  other arithmetic: 6.94 us -> 0.18 us
    psum x1 -> x0, waiting for transfers between devices: 118 us -> none  [per_device(): inc_total = lax.psum(member_term, 'member')]
    psum x1 -> x0, blocking collectives: 97.7 us -> none  [per_device(): lax.psum((control_sum, misfit_sum), ('member', 'tile'))]
    unnamed x13 -> x14, local copies, waits for them, and re-layouts: 32.6 us -> 3.39 us
    all_to_all x3 -> x1, waiting for transfers between devices: 36.2 us -> 13.9 us  [per_device(): lax.all_to_all(term.reshape(groups, share, lat, columns), 'member', 0, 0)]
    ppermute x0 -> x4, starting transfers between devices: none -> 19.2 us  [the longest x2 13.3 us: per_device(): from_right = lax.ppermute(left, 'tile', to_left)]
    all_gather x0 -> x1, blocking collectives: none -> 15.5 us  [per_device(): misfit = lax.all_gather(misfit_share, 'member', axis=0, tiled=True)]
    all_to_all x5 -> x0, local copies, waits for them, and re-layouts: 13.4 us -> none  [the longest x3 13.2 us: lon_filter(): lax.all_to_all(apply_lon(blocks, section), 'tile', split_axis=2, concat_a...]
    pallas_call x0 -> x7, Pallas kernels: none -> 11.7 us  [the longest x1 2.84 us: per_device(): pl.pallas_call(adjoint_kernel, out_shape=(field, shape((groups, 2, column...]
  transfers between devices with their start and end apart: 4 -> 5, of which waited for: 4 -> 3; matrix products, arithmetic and copies ran while one was open for 1% -> 1% of each run, Pallas kernels for 0% -> 4%
where the time goes in v1:
time: 112 us; the launch traced here: 111 us
  blocking collectives  46.7 us (42%)
  starting transfers between devices  30.6 us (27%)
  waiting for transfers between devices  15.9 us (14%)
  Pallas kernels  11.7 us (10%)
  local copies, waits for them, and re-layouts  5.5 us (5%)
    all_to_all x1, blocking collectives, per_device(): sums = jnp.sum(lax.all_to_all(sums, 'tile', 0, 0), axis=(0, 2)) / cells  18.2 us
    all_gather x1, blocking collectives, per_device(): misfit = lax.all_gather(misfit_share, 'member', axis=0, tiled=True)  15.5 us
    all_to_all x1, waiting for transfers between devices, per_device(): lax.all_to_all(term.reshape(groups, share, lat, columns), 'member', 0, 0)  13.9 us
    ppermute x2, starting transfers between devices, per_device(): from_right = lax.ppermute(left, 'tile', to_left)  13.3 us
    all_to_all x1, blocking collectives, per_device(): sums = jnp.sum(lax.all_to_all(sums, 'member', 0, 0), axis=0)  13 us
    all_to_all x1, starting transfers between devices, per_device(): lax.all_to_all(term.reshape(groups, share, lat, columns), 'member', 0, 0)  11.4 us
    ppermute x2, starting transfers between devices, per_device(): from_left = lax.ppermute(right, 'tile', to_right)  5.86 us
    unnamed x14, local copies, waits for them, and re-layouts  3.39 us
  transfers between devices with their start and end apart: 5, of which 3 were waited for; matrix products, arithmetic and copies ran while one was open for 1% of the time, Pallas kernels for 4%

profile of v1, /device:TPU:1, one launch (start us, length us, event | category | flops | bytes accessed | tf_op | source)
XLA Modules:
  0.0 111.4 jit_solution(12799792811547196438)
XLA Ops:
  0.6 0.0 copy-start
  0.6 1.0 copy-done
  1.6 0.0 copy-start.4
  1.6 0.9 pack_control.1
  2.5 3.9 %collective-permute-start = (f32[48,8,128]{2,1,0:T(8,128)}, f32[48,8,128]{2,1,0:T(8,128)S(1)}, u32[]{:S(2)}, u32[]{:S(2)}) collective-permute-start(f32[48,8,128]{2,1,0:T(8,128)} %get-tuple-element.22), channel_id=1, source_target_pairs={{0,1},{1,2},{2,3},{3,4},{4,5},{5,6},{6,7},{7,8},{8,9},{9,10},{10,1... | collective-permute-start | bytes 589832 | tf_op jit(solution)/shard_map/ppermute | solution.py:212
  6.4 6.1 %collective-permute-start.1 = (f32[48,8,128]{2,1,0:T(8,128)}, f32[48,8,128]{2,1,0:T(8,128)S(1)}, u32[]{:S(2)}, u32[]{:S(2)}) collective-permute-start(f32[48,8,128]{2,1,0:T(8,128)} %get-tuple-element.23), channel_id=1, source_target_pairs={{0,31},{1,0},{2,1},{3,2},{4,3},{5,4},{6,5},{7,6},{8,7},{9,8},{10,9... | collective-permute-start | bytes 589832 | tf_op jit(solution)/shard_map/ppermute | solution.py:213
  12.5 0.8 copy.12.col_ref
  13.3 0.0 copy-start.1
  13.3 1.0 copy-done.1
  14.3 0.0 copy-start.5
  14.3 0.7 copy-done.5
  15.0 2.1 %operators.1 = (bf16[768,768]{1,0:T(8,128)(2,1)S(1)}, bf16[768,768]{1,0:T(8,128)(2,1)S(1)}, bf16[768,768]{1,0:T(8,128)(2,1)S(1)}, bf16[768,768]{1,0:T(8,128)(2,1...) custom-call(s32[96]{0:T(128)S(1)} %copy-done.5, ...), custom_call_target="tpu_custom_call" | custom-call | flops 452984832 | bytes 6291456 | tf_op jit(solution)/shard_map/operators/pallas_call | solution.py:214
  17.0 0.0 collective-permute-done.fl_in
  17.0 0.0 collective-permute-done.1.fr_in
  17.1 0.0 copy-done.4
  17.1 2.0 %forward.1 = f32[96,8,128]{2,1,0:T(8,128)S(1)} custom-call(s32[96]{0:T(128)S(1)} %copy-done.5, f32[48,8,128]{2,1,0:T(8,128)S(1)} %collective-permute-done.fl_in, f32[48,8,128]{2,1,0:T(8,128)S(1)} %collective-permute-done.1.fr_in, f32[768,128]{1,0:T(8,128)S(1)} %get-tuple-element.24.y_ref, bf16[768,768]{1,0:T(8,128)(2,1)S(1)} %get-tuple-element.25.fh_ref, ...), custom_call_target="tpu_custom_call" | custom-call | tf_op jit(solution)/shard_map/forward/pallas_call | solution.py:224
  19.1 0.0 copy-start.3
  19.1 0.7 copy-done.3
  19.9 0.0 copy-start.2
  19.9 0.0 copy-start.6
  19.9 11.4 %all-to-all-start = ((f32[16,6,8,128]{3,2,1,0:T(8,128)}), f32[16,6,8,128]{3,2,1,0:T(8,128)}, u32[]{:S(2)}, u32[]{:S(2)}) async-start(f32[16,6,8,128]{3,2,1,0:T(8,128)} %bitcast.11), calls=%async_computation | async-start | bytes 786432 | tf_op jit(solution)/shard_map/all_to_all | solution.py:233
  31.3 0.8 constant_dynamic-slice_fusion
  32.0 13.9 %all-to-all-done.got_ref = f32[16,6,8,128]{3,2,1,0:T(8,128)} async-done(((f32[16,6,8,128]{3,2,1,0:T(8,128)}), f32[16,6,8,128]{3,2,1,0:T(8,128)}, u32[]{:S(2)}, u32[]{:S(2)}) %all-to-all-start) | async-done | bytes 393248 | tf_op jit(solution)/shard_map/all_to_all | solution.py:233
  45.9 1.6 %middle.1 = (f32[6,8,128]{2,1,0:T(8,128)}, f32[6,8,128]{2,1,0:T(8,128)S(1)}, f32[1,128]{1,0:T(1,128)S(1)}) custom-call(f32[16,6,8,128]{3,2,1,0:T(8,128)} %all-to-all-done.got_ref, f32[6,8,128]{2,1,0:T(8,128)S(1)} %get-tuple-element.43.weight_ref, f32[6,8,128]{2,1,0:T(8,128)S(1)} %get-tuple-element.42.innovation_ref, f32[1,128]{1,0:T(1,128)S(1)} %get-tuple-element.29.sum_in), custom_call_target="tpu_custom_call" | custom-call | tf_op jit(solution)/shard_map/middle/pallas_call | solution.py:234
  47.6 15.5 %all_gather.3.misfit_ref = f32[96,8,128]{2,1,0:T(8,128)S(1)} all-gather(f32[6,8,128]{2,1,0:T(8,128)S(1)} %get-tuple-element.31), channel_id=1, replica_groups=mesh['member'=16,'tile'=32] {'member'}, dimensions={0}, use_global_device_ids=true | all-gather | bytes 417792 | tf_op jit(solution)/shard_map/all_gather | solution.py:242
  63.1 0.1 weighted.1
  63.2 1.9 %collective-permute-start.2 = (f32[48,8,128]{2,1,0:T(8,128)S(1)}, f32[48,8,128]{2,1,0:T(8,128)S(1)}, u32[]{:S(2)}, u32[]{:S(2)}) collective-permute-start(f32[48,8,128]{2,1,0:T(8,128)S(1)} %get-tuple-element.32), channel_id=1, source_target_pairs={{0,1},{1,2},{2,3},{3,4},{4,5},{5,6},{6,7},{7,8},{8,9},{9,10},{10,1... | collective-permute-start | bytes 589832 | tf_op jit(solution)/shard_map/ppermute | solution.py:251
  65.2 7.3 %collective-permute-start.3 = (f32[48,8,128]{2,1,0:T(8,128)S(1)}, f32[48,8,128]{2,1,0:T(8,128)S(1)}, u32[]{:S(2)}, u32[]{:S(2)}) collective-permute-start(f32[48,8,128]{2,1,0:T(8,128)S(1)} %get-tuple-element.33), channel_id=1, source_target_pairs={{0,31},{1,0},{2,1},{3,2},{4,3},{5,4},{6,5},{7,6},{8,7},{9,8},{10,9... | collective-permute-start | bytes 589832 | tf_op jit(solution)/shard_map/ppermute | solution.py:252
  72.4 0.0 copy-done.2
  72.4 0.0 copy-done.6
  72.4 2.1 %local.1.part_ref = f32[96,8,128]{2,1,0:T(8,128)S(1)} custom-call(s32[96]{0:T(128)S(1)} %copy-done.6, f32[96,8,128]{2,1,0:T(8,128)S(1)} %get-tuple-element.34.w_ref, f32[96,8,128]{2,1,0:T(8,128)S(1)} %bitcast.10, bf16[256,512]{1,0:T(8,128)(2,1)S(1)} %get-tuple-element.27.bh_ref, bf16[256,512]{1,0:T(8,128)(2,1)S(1)} %get-tuple-element.28.bl_ref, ...), custom_call_target="tpu_custom_call" | custom-call | flops 603979776 | bytes 4194304 | tf_op jit(solution)/shard_map/local/pallas_call | solution.py:253
  74.5 1.1 collective-permute-done.2.fl_in
  75.6 1.0 collective-permute-done.3.fr_in
  76.5 2.8 %adjoint.1 = (f32[96,8,128]{2,1,0:T(8,128)}, f32[16,2,128]{2,1,0:T(2,128)S(1)}) custom-call(s32[96]{0:T(128)S(1)} %copy-done.6, f32[48,8,128]{2,1,0:T(8,128)S(1)} %collective-permute-done.2.fl_in, f32[48,8,128]{2,1,0:T(8,128)S(1)} %collective-permute-done.3.fr_in, f32[96,8,128]{2,1,0:T(8,128)S(1)} %local.1.part_ref, ...), custom_call_target="tpu_custom_call" | custom-call | tf_op jit(solution)/shard_map/adjoint/pallas_call | solution.py:263
  79.4 13.0 %all_to_all.15 = f32[16,2,128]{2,1,0:T(2,128)S(1)} all-to-all(f32[16,2,128]{2,1,0:T(2,128)S(1)} %get-tuple-element.39), channel_id=1, replica_groups=mesh['member'=16,'tile'=32] {'member'}, dimensions={0} | all-to-all | bytes 32768 | tf_op jit(solution)/shard_map/all_to_all | solution.py:272
  92.4 18.2 %all_to_all.16 = f32[32,2,128]{2,1,0:T(2,128)S(1)} all-to-all(f32[32,2,128]{2,1,0:T(2,128)S(1)} %broadcast_in_dim.10), channel_id=1, replica_groups=mesh['member'=16,'tile'=32] {'tile'}, dimensions={0} | all-to-all | bytes 65536 | tf_op jit(solution)/shard_map/all_to_all | solution.py:274
  110.7 0.1 reduce_sum.19
  110.8 0.6 fusion
  (3 shorter events, 0.0 us)
Async XLA Ops:
  0.6 1.0 copy-start
  1.6 15.4 %copy-start.4 = (bf16[1,96,8,128]{3,2,1,0:T(8,128)(2,1)S(1)}, bf16[1,96,8,128]{3,2,1,0:T(8,128)(2,1)}, u32[]{:S(2)}) copy-start(bf16[1,96,8,128]{3,2,1,0:T(8,128)(2,1)} %param.6) | copy-start | bytes 589828
  2.5 14.5 %collective-permute-start = (f32[48,8,128]{2,1,0:T(8,128)}, f32[48,8,128]{2,1,0:T(8,128)S(1)}, u32[]{:S(2)}, u32[]{:S(2)}) collective-permute-start(f32[48,8,128]{2,1,0:T(8,128)} %get-tuple-element.22), channel_id=1, source_target_pairs={{0,1},{1,2},{2,3},{3,4},{4,5},{5,6},{6,7},{7,8},{8,9},{9,10},{10,1... | collective-permute-start | bytes 589832 | tf_op jit(solution)/shard_map/ppermute | solution.py:212
  6.4 10.6 %collective-permute-start.1 = (f32[48,8,128]{2,1,0:T(8,128)}, f32[48,8,128]{2,1,0:T(8,128)S(1)}, u32[]{:S(2)}, u32[]{:S(2)}) collective-permute-start(f32[48,8,128]{2,1,0:T(8,128)} %get-tuple-element.23), channel_id=1, source_target_pairs={{0,31},{1,0},{2,1},{3,2},{4,3},{5,4},{6,5},{7,6},{8,7},{9,8},{10,9... | collective-permute-start | bytes 589832 | tf_op jit(solution)/shard_map/ppermute | solution.py:213
  13.3 1.0 copy-start.1
  14.3 0.7 copy-start.5
  19.1 0.7 copy-start.3
  19.9 52.6 %copy-start.2 = (f32[1,96,8,128]{3,2,1,0:T(8,128)S(1)}, f32[1,96,8,128]{3,2,1,0:T(8,128)}, u32[]{:S(2)}) copy-start(f32[1,96,8,128]{3,2,1,0:T(8,128)} %param.5) | copy-start | bytes 1179652
  19.9 52.6 %copy-start.6 = (s32[96]{0:T(128)S(1)}, s32[96]{0:T(128)}, u32[]{:S(2)}) copy-start(s32[96]{0:T(128)} %classes.7) | copy-start | bytes 1156
  19.9 26.1 %all-to-all-start = ((f32[16,6,8,128]{3,2,1,0:T(8,128)}), f32[16,6,8,128]{3,2,1,0:T(8,128)}, u32[]{:S(2)}, u32[]{:S(2)}) async-start(f32[16,6,8,128]{3,2,1,0:T(8,128)} %bitcast.11), calls=%async_computation | async-start | bytes 786432 | tf_op jit(solution)/shard_map/all_to_all | solution.py:233
  63.2 12.4 %collective-permute-start.2 = (f32[48,8,128]{2,1,0:T(8,128)S(1)}, f32[48,8,128]{2,1,0:T(8,128)S(1)}, u32[]{:S(2)}, u32[]{:S(2)}) collective-permute-start(f32[48,8,128]{2,1,0:T(8,128)S(1)} %get-tuple-element.32), channel_id=1, source_target_pairs={{0,1},{1,2},{2,3},{3,4},{4,5},{5,6},{6,7},{7,8},{8,9},{9,10},{10,1... | collective-permute-start | bytes 589832 | tf_op jit(solution)/shard_map/ppermute | solution.py:251
  65.2 11.4 %collective-permute-start.3 = (f32[48,8,128]{2,1,0:T(8,128)S(1)}, f32[48,8,128]{2,1,0:T(8,128)S(1)}, u32[]{:S(2)}, u32[]{:S(2)}) collective-permute-start(f32[48,8,128]{2,1,0:T(8,128)S(1)} %get-tuple-element.33), channel_id=1, source_target_pairs={{0,31},{1,0},{2,1},{3,2},{4,3},{5,4},{6,5},{7,6},{8,7},{9,8},{10,9... | collective-permute-start | bytes 589832 | tf_op jit(solution)/shard_map/ppermute | solution.py:252

commit v2 on v1

v2 whole, which is shorter than its diff:
```python
import functools

import jax
import jax.numpy as jnp
import numpy as np
from jax import lax
from jax.experimental import pallas as pl
from jax.experimental.pallas import tpu as pltpu
from jax.sharding import PartitionSpec as P

CLASSES = 4
PARTS = 4
VMEM_LIMIT = 48 * 1024 * 1024
f32, bf16 = jnp.float32, jnp.bfloat16


def vmem(count):
    return [pl.BlockSpec(memory_space=pltpu.VMEM)] * count


def smem():
    return pl.BlockSpec(memory_space=pltpu.SMEM)


def params():
    return pltpu.CompilerParams(vmem_limit_bytes=VMEM_LIMIT)


def split(value):
    high = value.astype(bf16)
    low = (value - high.astype(f32)).astype(bf16)
    return high, low


def dot(a, b):
    return jnp.dot(a, b, preferred_element_type=f32)


def left_product(high, low, value):
    vhigh, vlow = split(value)
    width = value.shape[1]
    both = dot(high, jnp.concatenate([vhigh, vlow], axis=1))
    return both[:, :width] + both[:, width:] + dot(low, vhigh)


def class_product(value, hot_ref, band):
    width = value.shape[1]
    high, low = split(value)
    highs = jnp.concatenate([high * hot_ref[c] for c in range(CLASSES)], axis=1)
    lows = jnp.concatenate([low * hot_ref[c] for c in range(CLASSES)], axis=1)
    both = dot(highs, band)
    return both[:, :width] + both[:, width:] + dot(lows, band[:, :width])


def lane_is_low(shape, half):
    return lax.broadcasted_iota(jnp.int32, shape, len(shape) - 1) < half


def lane_swaps(shape, half):
    upper = lax.broadcasted_iota(jnp.int32, shape, len(shape) - 1) // half
    return (upper + lax.axis_index("tile")) % 2 == 0


def pack_halves(first, second, near_ref, far_ref, at):
    columns = first.shape[2]
    half = columns // 2
    turned = pltpu.roll(second.reshape(-1, columns), half, 1).reshape(second.shape)
    swap = lane_swaps(first.shape, half)
    near_ref[at] = jnp.where(swap, turned, first)
    far_ref[at] = jnp.where(swap, first, turned)


def unpack_halves(near, far):
    columns = near.shape[2]
    half = columns // 2
    swap = lane_swaps(near.shape, half)
    first = jnp.where(swap, near, far).reshape(-1, columns)
    second = pltpu.roll(jnp.where(swap, far, near).reshape(-1, columns), half, 1)
    return jnp.concatenate([first, second], axis=0)


def pack_kernel(x_hbm, far_ref, near_ref, x_ref, sems):
    half_levels = near_ref.shape[0]
    size = half_levels // PARTS
    copies = []
    for part in range(PARTS):
        for side in range(2):
            at = pl.ds(side * half_levels + part * size, size)
            copy = pltpu.make_async_copy(x_hbm.at[at], x_ref.at[at], sems.at[part, side])
            copy.start()
            copies.append(copy)
    for part in range(PARTS):
        copies[2 * part].wait()
        copies[2 * part + 1].wait()
        at = pl.ds(part * size, size)
        pack_halves(x_ref[at], x_ref[pl.ds(half_levels + part * size, size)], near_ref, far_ref, at)


def class_scale(c):
    return 1.0 + float(c)


def operators_kernel(
    classes, x_hbm, weight_hbm, innovation_hbm,
    fh_ref, fl_ref, ah_ref, al_ref, own_ref, halo_ref, hot_ref, y_ref, sum_ref, weight_ref, innovation_ref,
    wide_ref, pat_ref, class_ref, x_ref, sems,
):
    levels, lat, columns = x_ref.shape
    rows = levels * lat
    half = columns // 2
    share = weight_ref.shape[0]
    mine = pl.ds(lax.axis_index("member") * share, share)
    weight_copy = pltpu.make_async_copy(weight_hbm.at[mine], weight_ref, sems.at[0])
    innovation_copy = pltpu.make_async_copy(innovation_hbm.at[mine], innovation_ref, sems.at[1])
    x_copy = pltpu.make_async_copy(x_hbm, x_ref, sems.at[2])
    x_copy.start()
    weight_copy.start()
    innovation_copy.start()
    for level in range(levels):
        class_ref[pl.ds(level, 1), :] = jnp.full((1, columns), classes[level].astype(f32), f32)
    class_lines = class_ref[...]
    class_rows = jnp.broadcast_to(class_lines[:, None, :], (levels, lat, columns)).reshape(rows, columns)
    for c in range(CLASSES):
        hot_ref[c] = (class_rows == float(c)).astype(f32).astype(bf16)
    k = lax.broadcasted_iota(jnp.int32, (levels, levels), 0)
    q = lax.broadcasted_iota(jnp.int32, (levels, levels), 1)
    class_col = class_lines[:, :levels]
    class_row = jnp.sum(jnp.where(k == q, class_col, 0.0), axis=0, keepdims=True)
    scale_col = 1.0 + class_col
    scale_row = 1.0 + class_row
    spacing = (k - q).astype(f32)
    vertical = jnp.exp(-spacing * spacing / (scale_col * scale_col + scale_row * scale_row))
    which = lax.broadcasted_iota(jnp.int32, (levels, rows), 1) // lat
    spread = (which == lax.broadcasted_iota(jnp.int32, (levels, rows), 0)).astype(f32).astype(bf16)
    vh, vl = split(vertical)
    wide_ref[...] = dot(vh, spread) + dot(vl, spread)
    class_wide = dot(jnp.broadcast_to(class_row, (8, levels)).astype(bf16), spread)[:1]
    i = lax.broadcasted_iota(jnp.int32, (lat, rows), 0)
    j = lax.broadcasted_iota(jnp.int32, (lat, rows), 1) % lat
    gap = (i - j).astype(f32)
    by_column = jnp.zeros((lat, rows), f32)
    for c in range(CLASSES):
        rho = lat * class_scale(c) / 8.0
        e = np.arange(-(lat - 1), lat, dtype=np.float32)
        norm = float(np.sqrt(np.sum(np.exp(-e * e / np.float32(rho * rho)), dtype=np.float32)))
        pattern = jnp.exp(-gap * gap / (2.0 * rho * rho)) / norm
        pat_ref[c] = pattern
        by_column = jnp.where(class_wide == float(c), pattern, by_column)
    for pair in range(levels // 2):
        forward, adjoint = [], []
        for level in (2 * pair, 2 * pair + 1):
            line = wide_ref[pl.ds(level, 1), :]
            forward.append(line * pat_ref[classes[level]])
            adjoint.append(line * by_column)
        at = pl.ds(2 * pair * lat, 2 * lat)
        fh_ref[at, :], fl_ref[at, :] = split(jnp.concatenate(forward, axis=0))
        ah_ref[at, :], al_ref[at, :] = split(jnp.concatenate(adjoint, axis=0))
    d = lax.broadcasted_iota(jnp.int32, (columns, columns), 0)
    out = lax.broadcasted_iota(jnp.int32, (columns, columns), 1)
    for ref, place in ((own_ref, d), (halo_ref, jnp.where(d < half, d + columns, d - columns))):
        far = (place - out).astype(f32)
        inside = jnp.abs(far) <= half
        for c in range(CLASSES):
            sigma = half * class_scale(c) / 4.0
            e = np.arange(-half, half + 1, dtype=np.float32)
            norm = float(np.sqrt(np.sum(np.exp(-e * e / np.float32(sigma * sigma)), dtype=np.float32)))
            band = jnp.where(inside, jnp.exp(-far * far / (2.0 * sigma * sigma)) / norm, 0.0)
            at = pl.ds(c * columns, columns)
            ref[at, :columns], ref[at, columns:] = split(band)
    x_copy.wait()
    x = x_ref[...].reshape(rows, columns)
    sum_ref[...] = 0.5 * jnp.sum(x * x, axis=0, keepdims=True)
    y_ref[...] = class_product(left_product(fh_ref[...], fl_ref[...], x), hot_ref, own_ref[...])
    weight_copy.wait()
    innovation_copy.wait()


def forward_kernel(inverse, far_ref, near_ref, y_ref, fh_ref, flo_ref, halo_ref, hot_ref, m_ref, out_ref):
    levels, lat, columns = m_ref.shape
    halo = left_product(fh_ref[...], flo_ref[...], unpack_halves(near_ref[...], far_ref[...]))
    alpha = y_ref[...] + class_product(halo, hot_ref, halo_ref[...])
    out_ref[...] = m_ref[...].astype(f32) * alpha.reshape(levels, lat, columns) * inverse


def middle_kernel(got_ref, weight_ref, innovation_ref, sum_in, inc_ref, misfit_ref, sum_ref):
    inc = jnp.sum(got_ref[...], axis=0)
    weight, innovation = weight_ref[...], innovation_ref[...]
    inc_ref[...] = inc
    misfit_ref[...] = weight * inc - innovation
    cost = 0.5 * weight * inc * inc - innovation * inc
    sum_ref[...] = sum_in[...] + jnp.sum(cost.reshape(-1, cost.shape[2]), axis=0, keepdims=True)


def weight_kernel(inverse, m_ref, misfit_ref, w_ref, far_ref, near_ref):
    w = m_ref[...].astype(f32) * misfit_ref[...] * inverse
    w_ref[...] = w
    half_levels = near_ref.shape[0]
    pack_halves(w[:half_levels], w[half_levels:], near_ref, far_ref, slice(None))


def local_kernel(w_ref, x_ref, own_ref, hot_ref, ah_ref, al_ref, out_ref):
    levels, lat, columns = w_ref.shape
    rows = levels * lat
    filtered = class_product(w_ref[...].reshape(rows, columns), hot_ref, own_ref[...])
    part = left_product(ah_ref[...], al_ref[...], filtered)
    out_ref[...] = x_ref[...] + part.reshape(levels, lat, columns)


def adjoint_kernel(far_ref, near_ref, part_ref, halo_ref, hot_ref, ah_ref, al_ref, sum_in, grad_ref, sums_ref):
    levels, lat, columns = part_ref.shape
    half = columns // 2
    filtered = class_product(unpack_halves(near_ref[...], far_ref[...]), hot_ref, halo_ref[...])
    edge = left_product(ah_ref[...], al_ref[...], filtered)
    grad = part_ref[...] + edge.reshape(levels, lat, columns)
    grad_ref[...] = grad
    flat = grad.reshape(-1, columns)
    square = jnp.sum(flat * flat, axis=0, keepdims=True)
    cost = sum_in[...]
    row = jnp.where(lane_is_low(square.shape, half), square + pltpu.roll(square, half, 1), cost + pltpu.roll(cost, half, 1))
    sums_ref[...] = jnp.broadcast_to(row[None], sums_ref.shape)


def per_device(tiles, control, members, obs_weight, innovation, scale_index):
    x = control[0]
    x_hbm, weight_hbm, innovation_hbm = [pltpu.with_memory_space_constraint(v, pltpu.HBM) for v in (x, obs_weight, innovation)]
    member = members[0]
    levels, lat, columns = x.shape
    rows = levels * lat
    groups = lax.axis_size("member")
    share = levels // groups
    cells = float(groups * rows * columns * tiles)
    inverse = float(np.float32(1.0) / np.sqrt(np.float32(groups - 1)))
    half_pack = pltpu.VMEM((levels // 2, lat, columns), f32)
    field = pltpu.VMEM((levels, lat, columns), f32)
    part = pltpu.VMEM((share, lat, columns), f32)
    square = pltpu.VMEM((rows, rows), bf16)
    band = pltpu.VMEM((CLASSES * columns, 2 * columns), bf16)
    line = pltpu.VMEM((1, columns), f32)
    near_pairs = [(i, i ^ 1) for i in range(tiles)]
    far_pairs = [(i, (((i - 1) % tiles ^ 1) + 1) % tiles) for i in range(tiles)]
    hbm = [pl.BlockSpec(memory_space=pltpu.HBM)]

    far, near = pl.pallas_call(
        pack_kernel,
        out_shape=(half_pack, half_pack),
        in_specs=hbm,
        out_specs=tuple(vmem(2)),
        scratch_shapes=[pltpu.VMEM((levels, lat, columns), f32), pltpu.SemaphoreType.DMA((PARTS, 2))],
        compiler_params=params(),
        name="pack_control",
    )(x_hbm)
    far = lax.ppermute(far, "tile", far_pairs)
    near = lax.ppermute(near, "tile", near_pairs)
    fh, fl, ah, al, own, halo, hot, y, half_sum, weight_share, innovation_share = pl.pallas_call(
        operators_kernel,
        out_shape=(square, square, square, square, band, band, pltpu.VMEM((CLASSES, rows, columns), bf16), pltpu.VMEM((rows, columns), f32), line, part, part),
        in_specs=[smem()] + hbm * 3,
        out_specs=tuple(vmem(11)),
        scratch_shapes=[
            pltpu.VMEM((levels, rows), f32),
            pltpu.VMEM((CLASSES, lat, rows), f32),
            pltpu.VMEM((levels, columns), f32),
            pltpu.VMEM((levels, lat, columns), f32),
            pltpu.SemaphoreType.DMA((3,)),
        ],
        compiler_params=params(),
        cost_estimate=pl.CostEstimate(flops=6 * rows * rows * columns, bytes_accessed=6 * 1024 * 1024, transcendentals=300000),
        name="operators",
    )(scale_index, x_hbm, weight_hbm, innovation_hbm)
    term = pl.pallas_call(
        functools.partial(forward_kernel, inverse),
        out_shape=field,
        in_specs=vmem(8),
        out_specs=vmem(1)[0],
        compiler_params=params(),
        name="forward",
    )(far, near, y, fh, fl, halo, hot, member)
    got = lax.all_to_all(term.reshape(groups, share, lat, columns), "member", 0, 0)
    inc, misfit_share, sums = pl.pallas_call(
        middle_kernel,
        out_shape=(part, part, line),
        in_specs=vmem(4),
        out_specs=tuple(vmem(3)),
        compiler_params=params(),
        name="middle",
    )(got, weight_share, innovation_share, half_sum)
    misfit = lax.all_gather(misfit_share, "member", axis=0, tiled=True)
    w, far, near = pl.pallas_call(
        functools.partial(weight_kernel, inverse),
        out_shape=(field, half_pack, half_pack),
        in_specs=vmem(2),
        out_specs=tuple(vmem(3)),
        compiler_params=params(),
        name="weighted",
    )(member, misfit)
    far = lax.ppermute(far, "tile", far_pairs)
    near = lax.ppermute(near, "tile", near_pairs)
    inner = pl.pallas_call(
        local_kernel,
        out_shape=field,
        in_specs=vmem(6),
        out_specs=vmem(1)[0],
        compiler_params=params(),
        cost_estimate=pl.CostEstimate(flops=8 * rows * rows * columns, bytes_accessed=4 * 1024 * 1024, transcendentals=0),
        name="local",
    )(w, x, own, hot, ah, al)
    grad, sums = pl.pallas_call(
        adjoint_kernel,
        out_shape=(field, pltpu.VMEM((groups, 1, columns), f32)),
        in_specs=vmem(8),
        out_specs=tuple(vmem(2)),
        compiler_params=params(),
        name="adjoint",
    )(far, near, inner, halo, hot, ah, al, sums)
    sums = jnp.sum(lax.all_to_all(sums, "member", 0, 0), axis=0)
    sums = jnp.broadcast_to(sums[None], (tiles,) + sums.shape)
    sums = jnp.sum(lax.all_to_all(sums, "tile", 0, 0), axis=0)
    sums = jnp.sum(sums.reshape(2, columns // 2), axis=1) / cells
    return inc, grad[None], sums[1], sums[0]


def solution(mesh):
    placed = (
        P("member", None, None, "tile"),
        P("member", None, None, "tile"),
        P(None, None, "tile"),
        P(None, None, "tile"),
        P(),
    )
    return jax.shard_map(
        functools.partial(per_device, mesh.shape["tile"]),
        mesh=mesh,
        in_specs=placed,
        out_specs=(P("member", None, "tile"), P("member", None, None, "tile"), P(), P()),
        check_vma=False,
    )
```

time: 112 us -> 103 us (0.920)
  starting transfers between devices: 30.6 us -> 21.5 us
  blocking collectives: 46.7 us -> 54.9 us
  local copies, waits for them, and re-layouts: 5.5 us -> 2.65 us
  waiting for transfers between devices: 15.9 us -> 13.4 us
  Pallas kernels: 11.7 us -> 9.27 us
    all_to_all x1, blocking collectives: 18.2 us -> 26.7 us  [per_device(): lax.all_to_all(term.reshape(groups, share, lat, columns), 'member', 0, 0)]
    all_to_all x1, waiting for transfers between devices: 13.9 us -> 7.07 us  [per_device(): sums = jnp.sum(lax.all_to_all(sums, 'tile', 0, 0), axis=0)]
    all_to_all x1, starting transfers between devices: 11.4 us -> 6.19 us  [per_device(): sums = jnp.sum(lax.all_to_all(sums, 'tile', 0, 0), axis=0)]
    ppermute x4, waiting for transfers between devices: 2.02 us -> 6.34 us  [the longest x2 5.1 us: per_device(): far = lax.ppermute(far, 'tile', far_pairs)]
    ppermute x4, starting transfers between devices: 19.2 us -> 15.3 us  [the longest x2 11.4 us: per_device(): far = lax.ppermute(far, 'tile', far_pairs)]
    unnamed x14 -> x6, local copies, waits for them, and re-layouts: 3.39 us -> 1.37 us
    pallas_call x5, Pallas kernels: 9.51 us -> 7.94 us  [the longest x1 4.16 us: per_device(): pl.pallas_call(operators_kernel, out_shape=(square, square, square, squar...]
  transfers between devices with their start and end apart: 5 -> 5, of which waited for: 3 -> 3; matrix products, arithmetic and copies ran while one was open for 1% -> 1% of each run, Pallas kernels for 4% -> 5%
where the time goes in v2:
time: 103 us
  blocking collectives  54.9 us (53%)
  starting transfers between devices  21.5 us (21%)
  waiting for transfers between devices  13.4 us (13%)
  Pallas kernels  9.27 us (9%)
  local copies, waits for them, and re-layouts  2.65 us (3%)
    all_to_all x1, blocking collectives, per_device(): lax.all_to_all(term.reshape(groups, share, lat, columns), 'member', 0, 0)  26.7 us
    all_gather x1, blocking collectives, per_device(): misfit = lax.all_gather(misfit_share, 'member', axis=0, tiled=True)  15.5 us
    all_to_all x1, blocking collectives, per_device(): sums = jnp.sum(lax.all_to_all(sums, 'member', 0, 0), axis=0)  12.7 us
    ppermute x2, starting transfers between devices, per_device(): far = lax.ppermute(far, 'tile', far_pairs)  11.4 us
    all_to_all x1, waiting for transfers between devices, per_device(): sums = jnp.sum(lax.all_to_all(sums, 'tile', 0, 0), axis=0)  7.07 us
    all_to_all x1, starting transfers between devices, per_device(): sums = jnp.sum(lax.all_to_all(sums, 'tile', 0, 0), axis=0)  6.19 us
    ppermute x2, waiting for transfers between devices, per_device(): far = lax.ppermute(far, 'tile', far_pairs)  5.1 us
    pallas_call x1, Pallas kernels, per_device(): pl.pallas_call(operators_kernel, out_shape=(square, square, square, squar...  4.16 us
  transfers between devices with their start and end apart: 5, of which 3 were waited for; matrix products, arithmetic and copies ran while one was open for 1% of the time, Pallas kernels for 5%

profile of v2, /device:TPU:1, one launch (start us, length us, event | category | flops | bytes accessed | tf_op | source)
XLA Modules:
  0.0 102.6 jit_solution(435887402827611638)
XLA Ops:
  0.6 0.0 copy-start.1
  0.6 1.3 %pack_control.1 = (f32[48,8,128]{2,1,0:T(8,128)S(1)}, f32[48,8,128]{2,1,0:T(8,128)S(1)}) custom-call(f32[96,8,128]{2,1,0:T(8,128)} %bitcast.8), custom_call_target="tpu_custom_call" | custom-call | tf_op jit(solution)/shard_map/pack_control/pallas_call | solution.py:243
  1.9 8.1 %collective-permute-start = (f32[48,8,128]{2,1,0:T(8,128)S(1)}, f32[48,8,128]{2,1,0:T(8,128)S(1)}, u32[]{:S(2)}, u32[]{:S(2)}) collective-permute-start(f32[48,8,128]{2,1,0:T(8,128)S(1)} %get-tuple-element.25), channel_id=1, source_target_pairs={{0,31},{1,2},{2,1},{3,4},{4,3},{5,6},{6,5},{7,8},{8,7},{9,10},{10,... | collective-permute-start | bytes 589832 | tf_op jit(solution)/shard_map/ppermute | solution.py:252
  10.0 1.9 %collective-permute-start.1 = (f32[48,8,128]{2,1,0:T(8,128)S(1)}, f32[48,8,128]{2,1,0:T(8,128)S(1)}, u32[]{:S(2)}, u32[]{:S(2)}) collective-permute-start(f32[48,8,128]{2,1,0:T(8,128)S(1)} %get-tuple-element.26), channel_id=1, source_target_pairs={{0,1},{1,0},{2,3},{3,2},{4,5},{5,4},{6,7},{7,6},{8,9},{9,8},{10,11... | collective-permute-start | bytes 589832 | tf_op jit(solution)/shard_map/ppermute | solution.py:253
  12.0 4.2 %operators.1 = (bf16[768,768]{1,0:T(8,128)(2,1)S(1)}, bf16[768,768]{1,0:T(8,128)(2,1)S(1)}, bf16[768,768]{1,0:T(8,128)(2,1)S(1)}, bf16[768,768]{1,0:T(8,128)(2,1...) custom-call(s32[96]{0:T(128)} %classes.1, ...), custom_call_target="tpu_custom_call" | custom-call | flops 452984832 | bytes 6291456 | tf_op jit(solution)/shard_map/operators/pallas_call | solution.py:254
  16.1 0.0 collective-permute-done.far_ref
  16.1 1.2 %collective-permute-done.1.near_ref = f32[48,8,128]{2,1,0:T(8,128)S(1)} collective-permute-done((f32[48,8,128]{2,1,0:T(8,128)S(1)}, f32[48,8,128]{2,1,0:T(8,128)S(1)}, u32[]{:S(2)}, u32[]{:S(2)}) %collective-permute-start.1) | collective-permute-done | bytes 196640 | tf_op jit(solution)/shard_map/ppermute | solution.py:253
  17.4 0.0 copy-done.1
  17.4 1.2 %forward.1 = f32[96,8,128]{2,1,0:T(8,128)S(1)} custom-call(f32[48,8,128]{2,1,0:T(8,128)S(1)} %collective-permute-done.far_ref, f32[48,8,128]{2,1,0:T(8,128)S(1)} %collective-permute-done.1.near_ref, f32[768,128]{1,0:T(8,128)S(1)} %get-tuple-element.27.y_ref, bf16[768,768]{1,0:T(8,128)(2,1)S(1)} %get-tuple-element.28.fh_ref, ...), custom_call_target="tpu_custom_call" | custom-call | tf_op jit(solution)/shard_map/forward/pallas_call | solution.py:270
  18.6 0.0 copy-start
  18.6 26.7 %all_to_all.15.got_ref = f32[16,6,8,128]{3,2,1,0:T(8,128)S(1)} all-to-all(f32[16,6,8,128]{3,2,1,0:T(8,128)S(1)} %bitcast.11), channel_id=1, replica_groups=mesh['member'=16,'tile'=32] {'member'}, dimensions={0} | all-to-all | bytes 786432 | tf_op jit(solution)/shard_map/all_to_all | solution.py:278
  45.3 15.5 %all_gather.3.misfit_ref = f32[96,8,128]{2,1,0:T(8,128)S(1)} all-gather(f32[6,8,128]{2,1,0:T(8,128)S(1)} %get-tuple-element.36), channel_id=1, replica_groups=mesh['member'=16,'tile'=32] {'member'}, dimensions={0}, use_global_device_ids=true | all-gather | bytes 417792 | tf_op jit(solution)/shard_map/all_gather | solution.py:287
  60.9 0.1 weighted.1
  61.0 3.3 %collective-permute-start.2 = (f32[48,8,128]{2,1,0:T(8,128)S(1)}, f32[48,8,128]{2,1,0:T(8,128)S(1)}, u32[]{:S(2)}, u32[]{:S(2)}) collective-permute-start(f32[48,8,128]{2,1,0:T(8,128)S(1)} %get-tuple-element.37), channel_id=1, source_target_pairs={{0,31},{1,2},{2,1},{3,4},{4,3},{5,6},{6,5},{7,8},{8,7},{9,10},{10,... | collective-permute-start | bytes 589832 | tf_op jit(solution)/shard_map/ppermute | solution.py:296
  64.3 1.9 %collective-permute-start.3 = (f32[48,8,128]{2,1,0:T(8,128)S(1)}, f32[48,8,128]{2,1,0:T(8,128)S(1)}, u32[]{:S(2)}, u32[]{:S(2)}) collective-permute-start(f32[48,8,128]{2,1,0:T(8,128)S(1)} %get-tuple-element.38), channel_id=1, source_target_pairs={{0,1},{1,0},{2,3},{3,2},{4,5},{5,4},{6,7},{7,6},{8,9},{9,8},{10,11... | collective-permute-start | bytes 589832 | tf_op jit(solution)/shard_map/ppermute | solution.py:297
  66.2 0.0 copy-done
  66.3 1.2 %local.1.part_ref = f32[96,8,128]{2,1,0:T(8,128)S(1)} custom-call(f32[96,8,128]{2,1,0:T(8,128)S(1)} %get-tuple-element.39.w_ref, f32[96,8,128]{2,1,0:T(8,128)S(1)} %bitcast.10, bf16[512,256]{1,0:T(8,128)(2,1)S(1)} %get-tuple-element.40.own_ref, bf16[4,768,128]{2,1,0:T(8,128)(2,1)S(1)} %get-tuple-element.31.hot_ref, ...), custom_call_target="tpu_custom_call" | custom-call | flops 603979776 | bytes 4194304 | tf_op jit(solution)/shard_map/local/pallas_call | solution.py:298
  67.5 5.1 %collective-permute-done.2.far_ref = f32[48,8,128]{2,1,0:T(8,128)S(1)} collective-permute-done((f32[48,8,128]{2,1,0:T(8,128)S(1)}, f32[48,8,128]{2,1,0:T(8,128)S(1)}, u32[]{:S(2)}, u32[]{:S(2)}) %collective-permute-start.2) | collective-permute-done | bytes 196640 | tf_op jit(solution)/shard_map/ppermute | solution.py:296
  72.6 0.0 collective-permute-done.3.near_ref
  72.6 1.3 %adjoint.1 = (f32[96,8,128]{2,1,0:T(8,128)S(1)}, f32[16,1,128]{2,1,0:T(1,128)S(1)}) custom-call(f32[48,8,128]{2,1,0:T(8,128)S(1)} %collective-permute-done.2.far_ref, f32[48,8,128]{2,1,0:T(8,128)S(1)} %collective-permute-done.3.near_ref, f32[96,8,128]{2,1,0:T(8,128)S(1)} %local.1.part_ref, bf16[512,256]{1,0:T(8,128)(2,1)S(1)} %get-tuple-element.30.halo_ref, ...), custom_call_target="tpu_custom_call" | custom-call | tf_op jit(solution)/shard_map/adjoint/pallas_call | solution.py:307
  73.8 12.7 %all_to_all.16 = f32[16,1,128]{2,1,0:T(1,128)S(1)} all-to-all(f32[16,1,128]{2,1,0:T(1,128)S(1)} %get-tuple-element.45), channel_id=1, replica_groups=mesh['member'=16,'tile'=32] {'member'}, dimensions={0} | all-to-all | bytes 16384 | tf_op jit(solution)/shard_map/all_to_all | solution.py:315
  86.6 0.6 broadcast_in_dim.10
  87.2 6.2 %all-to-all-start.2 = ((f32[32,1,128]{2,1,0:T(1,128)}), f32[32,1,128]{2,1,0:T(1,128)S(1)}, u32[]{:S(2)}, u32[]{:S(2)}) async-start(f32[32,1,128]{2,1,0:T(1,128)} %broadcast_in_dim.10), calls=%async_computation.2 | async-start | bytes 32768 | tf_op jit(solution)/shard_map/all_to_all | solution.py:317
  93.4 0.6 copy.10
  94.0 0.7 copy.11
  94.7 7.1 %all-to-all-done.2 = f32[32,1,128]{2,1,0:T(1,128)S(1)} async-done(((f32[32,1,128]{2,1,0:T(1,128)}), f32[32,1,128]{2,1,0:T(1,128)S(1)}, u32[]{:S(2)}, u32[]{:S(2)}) %all-to-all-start.2) | async-done | bytes 16416 | tf_op jit(solution)/shard_map/all_to_all | solution.py:317
  101.8 0.1 reshape.22
  101.9 0.1 reduce_sum.29
  102.0 0.6 fusion
  (4 shorter events, 0.1 us)
Async XLA Ops:
  0.6 16.8 %copy-start.1 = (bf16[1,96,8,128]{3,2,1,0:T(8,128)(2,1)S(1)}, bf16[1,96,8,128]{3,2,1,0:T(8,128)(2,1)}, u32[]{:S(2)}) copy-start(bf16[1,96,8,128]{3,2,1,0:T(8,128)(2,1)} %param.6) | copy-start | bytes 589828
  1.9 14.2 %collective-permute-start = (f32[48,8,128]{2,1,0:T(8,128)S(1)}, f32[48,8,128]{2,1,0:T(8,128)S(1)}, u32[]{:S(2)}, u32[]{:S(2)}) collective-permute-start(f32[48,8,128]{2,1,0:T(8,128)S(1)} %get-tuple-element.25), channel_id=1, source_target_pairs={{0,31},{1,2},{2,1},{3,4},{4,3},{5,6},{6,5},{7,8},{8,7},{9,10},{10,... | collective-permute-start | bytes 589832 | tf_op jit(solution)/shard_map/ppermute | solution.py:252
  10.0 7.3 %collective-permute-start.1 = (f32[48,8,128]{2,1,0:T(8,128)S(1)}, f32[48,8,128]{2,1,0:T(8,128)S(1)}, u32[]{:S(2)}, u32[]{:S(2)}) collective-permute-start(f32[48,8,128]{2,1,0:T(8,128)S(1)} %get-tuple-element.26), channel_id=1, source_target_pairs={{0,1},{1,0},{2,3},{3,2},{4,5},{5,4},{6,7},{7,6},{8,9},{9,8},{10,11... | collective-permute-start | bytes 589832 | tf_op jit(solution)/shard_map/ppermute | solution.py:253
  18.6 47.6 %copy-start = (f32[1,96,8,128]{3,2,1,0:T(8,128)S(1)}, f32[1,96,8,128]{3,2,1,0:T(8,128)}, u32[]{:S(2)}) copy-start(f32[1,96,8,128]{3,2,1,0:T(8,128)} %param.5) | copy-start | bytes 1179652
  61.0 11.6 %collective-permute-start.2 = (f32[48,8,128]{2,1,0:T(8,128)S(1)}, f32[48,8,128]{2,1,0:T(8,128)S(1)}, u32[]{:S(2)}, u32[]{:S(2)}) collective-permute-start(f32[48,8,128]{2,1,0:T(8,128)S(1)} %get-tuple-element.37), channel_id=1, source_target_pairs={{0,31},{1,2},{2,1},{3,4},{4,3},{5,6},{6,5},{7,8},{8,7},{9,10},{10,... | collective-permute-start | bytes 589832 | tf_op jit(solution)/shard_map/ppermute | solution.py:296
  64.3 8.2 %collective-permute-start.3 = (f32[48,8,128]{2,1,0:T(8,128)S(1)}, f32[48,8,128]{2,1,0:T(8,128)S(1)}, u32[]{:S(2)}, u32[]{:S(2)}) collective-permute-start(f32[48,8,128]{2,1,0:T(8,128)S(1)} %get-tuple-element.38), channel_id=1, source_target_pairs={{0,1},{1,0},{2,3},{3,2},{4,5},{5,4},{6,7},{7,6},{8,9},{9,8},{10,11... | collective-permute-start | bytes 589832 | tf_op jit(solution)/shard_map/ppermute | solution.py:297
  87.2 14.6 %all-to-all-start.2 = ((f32[32,1,128]{2,1,0:T(1,128)}), f32[32,1,128]{2,1,0:T(1,128)S(1)}, u32[]{:S(2)}, u32[]{:S(2)}) async-start(f32[32,1,128]{2,1,0:T(1,128)} %broadcast_in_dim.10), calls=%async_computation.2 | async-start | bytes 32768 | tf_op jit(solution)/shard_map/all_to_all | solution.py:317

commit v3 on v2

--- a/solution.py
+++ b/solution.py
@@ -101,9 +101,9 @@
 
 
 def operators_kernel(
-    classes, x_hbm, weight_hbm, innovation_hbm,
-    fh_ref, fl_ref, ah_ref, al_ref, own_ref, halo_ref, hot_ref, y_ref, sum_ref, weight_ref, innovation_ref,
-    wide_ref, pat_ref, class_ref, x_ref, sems,
+    classes, x_ref, weight_hbm, innovation_hbm,
+    fh_ref, fl_ref, wide_ref, mix_ref, own_ref, halo_ref, hot_ref, y_ref, sum_ref, weight_ref, innovation_ref,
+    class_ref, class_rows_ref, sems,
 ):
     levels, lat, columns = x_ref.shape
     rows = levels * lat
@@ -112,14 +112,13 @@
     mine = pl.ds(lax.axis_index("member") * share, share)
     weight_copy = pltpu.make_async_copy(weight_hbm.at[mine], weight_ref, sems.at[0])
     innovation_copy = pltpu.make_async_copy(innovation_hbm.at[mine], innovation_ref, sems.at[1])
-    x_copy = pltpu.make_async_copy(x_hbm, x_ref, sems.at[2])
-    x_copy.start()
     weight_copy.start()
     innovation_copy.start()
     for level in range(levels):
         class_ref[pl.ds(level, 1), :] = jnp.full((1, columns), classes[level].astype(f32), f32)
     class_lines = class_ref[...]
     class_rows = jnp.broadcast_to(class_lines[:, None, :], (levels, lat, columns)).reshape(rows, columns)
+    class_rows_ref[...] = class_rows
     for c in range(CLASSES):
         hot_ref[c] = (class_rows == float(c)).astype(f32).astype(bf16)
     k = lax.broadcasted_iota(jnp.int32, (levels, levels), 0)
@@ -130,31 +129,33 @@
     scale_row = 1.0 + class_row
     spacing = (k - q).astype(f32)
     vertical = jnp.exp(-spacing * spacing / (scale_col * scale_col + scale_row * scale_row))
-    which = lax.broadcasted_iota(jnp.int32, (levels, rows), 1) // lat
-    spread = (which == lax.broadcasted_iota(jnp.int32, (levels, rows), 0)).astype(f32).astype(bf16)
+    ahead = lax.broadcasted_iota(jnp.int32, (levels, rows), 1) - lat * lax.broadcasted_iota(jnp.int32, (levels, rows), 0)
+    spread = ((ahead >= 0) & (ahead < lat)).astype(f32).astype(bf16)
     vh, vl = split(vertical)
     wide_ref[...] = dot(vh, spread) + dot(vl, spread)
     class_wide = dot(jnp.broadcast_to(class_row, (8, levels)).astype(bf16), spread)[:1]
     i = lax.broadcasted_iota(jnp.int32, (lat, rows), 0)
-    j = lax.broadcasted_iota(jnp.int32, (lat, rows), 1) % lat
+    j = lax.broadcasted_iota(jnp.int32, (lat, rows), 1) & (lat - 1)
     gap = (i - j).astype(f32)
-    by_column = jnp.zeros((lat, rows), f32)
+    patterns = []
+    mix = jnp.zeros((lat, rows), f32)
     for c in range(CLASSES):
         rho = lat * class_scale(c) / 8.0
         e = np.arange(-(lat - 1), lat, dtype=np.float32)
         norm = float(np.sqrt(np.sum(np.exp(-e * e / np.float32(rho * rho)), dtype=np.float32)))
-        pattern = jnp.exp(-gap * gap / (2.0 * rho * rho)) / norm
-        pat_ref[c] = pattern
-        by_column = jnp.where(class_wide == float(c), pattern, by_column)
+        patterns.append(jnp.exp(-gap * gap / (2.0 * rho * rho)) / norm)
+        mix = jnp.where(class_wide == float(c), patterns[c], mix)
+    mix_ref[...] = mix
     for pair in range(levels // 2):
-        forward, adjoint = [], []
+        both = []
         for level in (2 * pair, 2 * pair + 1):
-            line = wide_ref[pl.ds(level, 1), :]
-            forward.append(line * pat_ref[classes[level]])
-            adjoint.append(line * by_column)
+            kind = class_rows_ref[pl.ds(level * lat, lat), :1]
+            pattern = patterns[CLASSES - 1]
+            for c in range(CLASSES - 1):
+                pattern = jnp.where(kind == float(c), patterns[c], pattern)
+            both.append(wide_ref[pl.ds(level, 1), :] * pattern)
         at = pl.ds(2 * pair * lat, 2 * lat)
-        fh_ref[at, :], fl_ref[at, :] = split(jnp.concatenate(forward, axis=0))
-        ah_ref[at, :], al_ref[at, :] = split(jnp.concatenate(adjoint, axis=0))
+        fh_ref[at, :], fl_ref[at, :] = split(jnp.concatenate(both, axis=0))
     d = lax.broadcasted_iota(jnp.int32, (columns, columns), 0)
     out = lax.broadcasted_iota(jnp.int32, (columns, columns), 1)
     for ref, place in ((own_ref, d), (halo_ref, jnp.where(d < half, d + columns, d - columns))):
@@ -167,7 +168,6 @@
             band = jnp.where(inside, jnp.exp(-far * far / (2.0 * sigma * sigma)) / norm, 0.0)
             at = pl.ds(c * columns, columns)
             ref[at, :columns], ref[at, columns:] = split(band)
-    x_copy.wait()
     x = x_ref[...].reshape(rows, columns)
     sum_ref[...] = 0.5 * jnp.sum(x * x, axis=0, keepdims=True)
     y_ref[...] = class_product(left_product(fh_ref[...], fl_ref[...], x), hot_ref, own_ref[...])
@@ -175,32 +175,50 @@
     innovation_copy.wait()
 
 
-def forward_kernel(inverse, far_ref, near_ref, y_ref, fh_ref, flo_ref, halo_ref, hot_ref, m_ref, out_ref):
+def forward_kernel(inverse, far_ref, near_ref, y_ref, fh_ref, flo_ref, halo_ref, hot_ref, m_ref, mine_ref, other_ref):
     levels, lat, columns = m_ref.shape
     halo = left_product(fh_ref[...], flo_ref[...], unpack_halves(near_ref[...], far_ref[...]))
     alpha = y_ref[...] + class_product(halo, hot_ref, halo_ref[...])
-    out_ref[...] = m_ref[...].astype(f32) * alpha.reshape(levels, lat, columns) * inverse
+    term = m_ref[...].astype(f32) * alpha.reshape(levels, lat, columns) * inverse
+    chips, share = mine_ref.shape[:2]
+    term = term.reshape(chips, 2, share, lat, columns)
+    even = lax.axis_index("member") % 2 == 0
+    mine_ref[...] = jnp.where(even, term[:, 0], term[:, 1])
+    other_ref[...] = jnp.where(even, term[:, 1], term[:, 0])
+
+
+def add_kernel(a_ref, b_ref, out_ref):
+    out_ref[...] = a_ref[...] + b_ref[...]
 
 
 def middle_kernel(got_ref, weight_ref, innovation_ref, sum_in, inc_ref, misfit_ref, sum_ref):
     inc = jnp.sum(got_ref[...], axis=0)
     weight, innovation = weight_ref[...], innovation_ref[...]
     inc_ref[...] = inc
-    misfit_ref[...] = weight * inc - innovation
+    misfit_ref[...] = jnp.broadcast_to((weight * inc - innovation)[None], misfit_ref.shape)
     cost = 0.5 * weight * inc * inc - innovation * inc
     sum_ref[...] = sum_in[...] + jnp.sum(cost.reshape(-1, cost.shape[2]), axis=0, keepdims=True)
 
 
-def weight_kernel(inverse, m_ref, misfit_ref, w_ref, far_ref, near_ref):
-    w = m_ref[...].astype(f32) * misfit_ref[...] * inverse
+def weight_kernel(inverse, m_ref, mine_ref, other_ref, w_ref, far_ref, near_ref):
+    levels, lat, columns = m_ref.shape
+    mine, other = mine_ref[...], other_ref[...]
+    even = lax.axis_index("member") % 2 == 0
+    misfit = jnp.stack([jnp.where(even, mine, other), jnp.where(even, other, mine)], axis=1)
+    w = m_ref[...].astype(f32) * misfit.reshape(levels, lat, columns) * inverse
     w_ref[...] = w
     half_levels = near_ref.shape[0]
     pack_halves(w[:half_levels], w[half_levels:], near_ref, far_ref, slice(None))
 
 
-def local_kernel(w_ref, x_ref, own_ref, hot_ref, ah_ref, al_ref, out_ref):
+def local_kernel(w_ref, x_ref, own_ref, hot_ref, wide_ref, mix_ref, out_ref, ah_ref, al_ref):
     levels, lat, columns = w_ref.shape
     rows = levels * lat
+    mix = mix_ref[...]
+    for pair in range(levels // 2):
+        both = [wide_ref[pl.ds(level, 1), :] * mix for level in (2 * pair, 2 * pair + 1)]
+        at = pl.ds(2 * pair * lat, 2 * lat)
+        ah_ref[at, :], al_ref[at, :] = split(jnp.concatenate(both, axis=0))
     filtered = class_product(w_ref[...].reshape(rows, columns), hot_ref, own_ref[...])
     part = left_product(ah_ref[...], al_ref[...], filtered)
     out_ref[...] = x_ref[...] + part.reshape(levels, lat, columns)
@@ -222,7 +240,8 @@
 
 def per_device(tiles, control, members, obs_weight, innovation, scale_index):
     x = control[0]
-    x_hbm, weight_hbm, innovation_hbm = [pltpu.with_memory_space_constraint(v, pltpu.HBM) for v in (x, obs_weight, innovation)]
+    in_hbm = (x, obs_weight, innovation, scale_index)
+    x_hbm, weight_hbm, innovation_hbm, classes = [pltpu.with_memory_space_constraint(v, pltpu.HBM) for v in in_hbm]
     member = members[0]
     levels, lat, columns = x.shape
     rows = levels * lat
@@ -236,74 +255,78 @@
     square = pltpu.VMEM((rows, rows), bf16)
     band = pltpu.VMEM((CLASSES * columns, 2 * columns), bf16)
     line = pltpu.VMEM((1, columns), f32)
+    chips = [list(range(core, groups, 2)) for core in range(2)]
+    partners = [(i, i ^ 1) for i in range(groups)]
     near_pairs = [(i, i ^ 1) for i in range(tiles)]
     far_pairs = [(i, (((i - 1) % tiles ^ 1) + 1) % tiles) for i in range(tiles)]
     hbm = [pl.BlockSpec(memory_space=pltpu.HBM)]
 
-    far, near = pl.pallas_call(
+    far, near, x_near = pl.pallas_call(
         pack_kernel,
-        out_shape=(half_pack, half_pack),
+        out_shape=(half_pack, half_pack, field),
         in_specs=hbm,
-        out_specs=tuple(vmem(2)),
-        scratch_shapes=[pltpu.VMEM((levels, lat, columns), f32), pltpu.SemaphoreType.DMA((PARTS, 2))],
+        out_specs=tuple(vmem(3)),
+        scratch_shapes=[pltpu.SemaphoreType.DMA((PARTS, 2))],
         compiler_params=params(),
         name="pack_control",
     )(x_hbm)
     far = lax.ppermute(far, "tile", far_pairs)
     near = lax.ppermute(near, "tile", near_pairs)
-    fh, fl, ah, al, own, halo, hot, y, half_sum, weight_share, innovation_share = pl.pallas_call(
+    fh, fl, wide, mix, own, halo, hot, y, half_sum, weight_share, innovation_share = pl.pallas_call(
         operators_kernel,
-        out_shape=(square, square, square, square, band, band, pltpu.VMEM((CLASSES, rows, columns), bf16), pltpu.VMEM((rows, columns), f32), line, part, part),
-        in_specs=[smem()] + hbm * 3,
+        out_shape=(square, square, pltpu.VMEM((levels, rows), f32), pltpu.VMEM((lat, rows), f32), band, band, pltpu.VMEM((CLASSES, rows, columns), bf16), pltpu.VMEM((rows, columns), f32), line, part, part),
+        in_specs=[smem()] + vmem(1) + hbm * 2,
         out_specs=tuple(vmem(11)),
         scratch_shapes=[
-            pltpu.VMEM((levels, rows), f32),
-            pltpu.VMEM((CLASSES, lat, rows), f32),
             pltpu.VMEM((levels, columns), f32),
-            pltpu.VMEM((levels, lat, columns), f32),
-            pltpu.SemaphoreType.DMA((3,)),
+            pltpu.VMEM((rows, columns), f32),
+            pltpu.SemaphoreType.DMA((2,)),
         ],
         compiler_params=params(),
         cost_estimate=pl.CostEstimate(flops=6 * rows * rows * columns, bytes_accessed=6 * 1024 * 1024, transcendentals=300000),
         name="operators",
-    )(scale_index, x_hbm, weight_hbm, innovation_hbm)
-    term = pl.pallas_call(
+    )(classes, x_near, weight_hbm, innovation_hbm)
+    half_term = pltpu.VMEM((groups // 2, share, lat, columns), f32)
+    mine, other = pl.pallas_call(
         functools.partial(forward_kernel, inverse),
-        out_shape=field,
+        out_shape=(half_term, half_term),
         in_specs=vmem(8),
-        out_specs=vmem(1)[0],
+        out_specs=tuple(vmem(2)),
         compiler_params=params(),
         name="forward",
     )(far, near, y, fh, fl, halo, hot, member)
-    got = lax.all_to_all(term.reshape(groups, share, lat, columns), "member", 0, 0)
+    other = lax.ppermute(other, "member", partners)
+    both = pl.pallas_call(add_kernel, out_shape=half_term, in_specs=vmem(2), out_specs=vmem(1)[0], compiler_params=params(), name="add_cores")(mine, other)
+    got = lax.all_to_all(both, "member", 0, 0, axis_index_groups=chips)
     inc, misfit_share, sums = pl.pallas_call(
         middle_kernel,
-        out_shape=(part, part, line),
+        out_shape=(part, pltpu.VMEM((groups // 2, share, lat, columns), f32), line),
         in_specs=vmem(4),
         out_specs=tuple(vmem(3)),
         compiler_params=params(),
         name="middle",
     )(got, weight_share, innovation_share, half_sum)
-    misfit = lax.all_gather(misfit_share, "member", axis=0, tiled=True)
+    misfit_mine = lax.all_to_all(misfit_share, "member", 0, 0, axis_index_groups=chips)
+    misfit_other = lax.ppermute(misfit_mine, "member", partners)
     w, far, near = pl.pallas_call(
         functools.partial(weight_kernel, inverse),
         out_shape=(field, half_pack, half_pack),
-        in_specs=vmem(2),
+        in_specs=vmem(3),
         out_specs=tuple(vmem(3)),
         compiler_params=params(),
         name="weighted",
-    )(member, misfit)
+    )(member, misfit_mine, misfit_other)
     far = lax.ppermute(far, "tile", far_pairs)
     near = lax.ppermute(near, "tile", near_pairs)
-    inner = pl.pallas_call(
+    inner, ah, al = pl.pallas_call(
         local_kernel,
-        out_shape=field,
+        out_shape=(field, square, square),
         in_specs=vmem(6),
-        out_specs=vmem(1)[0],
+        out_specs=tuple(vmem(3)),
         compiler_params=params(),
         cost_estimate=pl.CostEstimate(flops=8 * rows * rows * columns, bytes_accessed=4 * 1024 * 1024, transcendentals=0),
         name="local",
-    )(w, x, own, hot, ah, al)
+    )(w, x, own, hot, wide, mix)
     grad, sums = pl.pallas_call(
         adjoint_kernel,
         out_shape=(field, pltpu.VMEM((groups, 1, columns), f32)),

time: 103 us -> 100 us (0.971)
  blocking collectives: 54.9 us -> 40.8 us
  starting transfers between devices: 21.5 us -> 30.5 us
  waiting for transfers between devices: 13.4 us -> 15.8 us
    all_gather x1 -> x0, blocking collectives: 15.5 us -> none  [per_device(): misfit = lax.all_gather(misfit_share, 'member', axis=0, tiled=True)]
    ppermute x0 -> x2, starting transfers between devices: none -> 9.08 us  [the longest x1 4.75 us: per_device(): misfit_other = lax.ppermute(misfit_mine, 'member', partners)]
    all_to_all x1 -> x2, blocking collectives: 26.7 us -> 30.2 us  [the longest x1 18.8 us: per_device(): got = lax.all_to_all(both, 'member', 0, 0, axis_index_groups=chips)]
    ppermute x0 -> x2, waiting for transfers between devices: none -> 2.1 us  [the longest x1 1.05 us: per_device(): other = lax.ppermute(other, 'member', partners)]
    all_to_all x1, blocking collectives: 12.7 us -> 10.6 us  [per_device(): sums = jnp.sum(lax.all_to_all(sums, 'member', 0, 0), axis=0)]
    pallas_call x5 -> x6, Pallas kernels: 7.87 us -> 7.54 us  [the longest x1 3.76 us: per_device(): pl.pallas_call(operators_kernel, out_shape=(square, square, pltpu.VMEM((l...]
  transfers between devices with their start and end apart: 5 -> 7, of which waited for: 3 -> 5; matrix products, arithmetic and copies ran while one was open for 1% -> 1% of each run, Pallas kernels for 5% -> 5%
where the time goes in v3:
time: 100 us; the launch traced here: 99.7 us
  blocking collectives  40.8 us (41%)
  starting transfers between devices  30.5 us (30%)
  waiting for transfers between devices  15.8 us (16%)
  Pallas kernels  8.98 us (9%)
  local copies, waits for them, and re-layouts  2.65 us (3%)
    all_to_all x1, blocking collectives, per_device(): got = lax.all_to_all(both, 'member', 0, 0, axis_index_groups=chips)  18.8 us
    ppermute x2, starting transfers between devices, per_device(): far = lax.ppermute(far, 'tile', far_pairs)  11.4 us
    all_to_all x1, blocking collectives, per_device(): lax.all_to_all(misfit_share, 'member', 0, 0, axis_index_groups=chips)  11.3 us
    all_to_all x1, blocking collectives, per_device(): sums = jnp.sum(lax.all_to_all(sums, 'member', 0, 0), axis=0)  10.6 us
    all_to_all x1, waiting for transfers between devices, per_device(): sums = jnp.sum(lax.all_to_all(sums, 'tile', 0, 0), axis=0)  7.24 us
    all_to_all x1, starting transfers between devices, per_device(): sums = jnp.sum(lax.all_to_all(sums, 'tile', 0, 0), axis=0)  6.19 us
    ppermute x2, waiting for transfers between devices, per_device(): far = lax.ppermute(far, 'tile', far_pairs)  4.84 us
    ppermute x1, starting transfers between devices, per_device(): misfit_other = lax.ppermute(misfit_mine, 'member', partners)  4.75 us
  transfers between devices with their start and end apart: 7, of which 5 were waited for; matrix products, arithmetic and copies ran while one was open for 1% of the time, Pallas kernels for 5%

profile of v3, /device:TPU:1, one launch (start us, length us, event | category | flops | bytes accessed | tf_op | source)
XLA Modules:
  0.0 99.7 jit_solution(327044902850898244)
XLA Ops:
  0.6 0.0 copy-start
  0.6 1.3 %pack_control.1 = (f32[48,8,128]{2,1,0:T(8,128)S(1)}, f32[48,8,128]{2,1,0:T(8,128)S(1)}, f32[96,8,128]{2,1,0:T(8,128)S(1)}) custom-call(f32[96,8,128]{2,1,0:T(8,128)} %bitcast.9), custom_call_target="tpu_custom_call" | custom-call | tf_op jit(solution)/shard_map/pack_control/pallas_call | solution.py:264
  1.9 8.1 %collective-permute-start = (f32[48,8,128]{2,1,0:T(8,128)S(1)}, f32[48,8,128]{2,1,0:T(8,128)S(1)}, u32[]{:S(2)}, u32[]{:S(2)}) collective-permute-start(f32[48,8,128]{2,1,0:T(8,128)S(1)} %get-tuple-element.31), channel_id=1, source_target_pairs={{0,31},{1,2},{2,1},{3,4},{4,3},{5,6},{6,5},{7,8},{8,7},{9,10},{10,... | collective-permute-start | bytes 589832 | tf_op jit(solution)/shard_map/ppermute | solution.py:273
  10.0 1.9 %collective-permute-start.1 = (f32[48,8,128]{2,1,0:T(8,128)S(1)}, f32[48,8,128]{2,1,0:T(8,128)S(1)}, u32[]{:S(2)}, u32[]{:S(2)}) collective-permute-start(f32[48,8,128]{2,1,0:T(8,128)S(1)} %get-tuple-element.32), channel_id=1, source_target_pairs={{0,1},{1,0},{2,3},{3,2},{4,5},{5,4},{6,7},{7,6},{8,9},{9,8},{10,11... | collective-permute-start | bytes 589832 | tf_op jit(solution)/shard_map/ppermute | solution.py:274
  12.0 3.8 %operators.1 = (bf16[768,768]{1,0:T(8,128)(2,1)S(1)}, bf16[768,768]{1,0:T(8,128)(2,1)S(1)}, f32[96,768]{1,0:T(8,128)S(1)}, f32[8,768]{1,0:T(8,128)S(1)}, bf16[51...) custom-call(s32[96]{0:T(128)} %classes.1, ...), custom_call_target="tpu_custom_call" | custom-call | flops 452984832 | bytes 6291456 | tf_op jit(solution)/shard_map/operators/pallas_call | solution.py:275
  15.7 0.0 collective-permute-done.far_ref
  15.7 1.6 %collective-permute-done.1.near_ref = f32[48,8,128]{2,1,0:T(8,128)S(1)} collective-permute-done((f32[48,8,128]{2,1,0:T(8,128)S(1)}, f32[48,8,128]{2,1,0:T(8,128)S(1)}, u32[]{:S(2)}, u32[]{:S(2)}) %collective-permute-start.1) | collective-permute-done | bytes 196640 | tf_op jit(solution)/shard_map/ppermute | solution.py:274
  17.4 0.0 copy-done
  17.4 1.2 %forward.1 = (f32[8,6,8,128]{3,2,1,0:T(8,128)S(1)}, f32[8,6,8,128]{3,2,1,0:T(8,128)S(1)}) custom-call(f32[48,8,128]{2,1,0:T(8,128)S(1)} %collective-permute-done.far_ref, f32[48,8,128]{2,1,0:T(8,128)S(1)} %collective-permute-done.1.near_ref, f32[768,128]{1,0:T(8,128)S(1)} %get-tuple-element.34.y_ref, bf16[768,768]{1,0:T(8,128)(2,1)S(1)} %get-tuple-element.35.fh_ref, ...), custom_call_target="tpu_custom_call" | custom-call | tf_op jit(solution)/shard_map/forward/pallas_call | solution.py:290
  18.6 0.0 copy-start.1
  18.6 4.3 %collective-permute-start.2 = (f32[8,6,8,128]{3,2,1,0:T(8,128)S(1)}, f32[8,6,8,128]{3,2,1,0:T(8,128)S(1)}, u32[]{:S(2)}, u32[]{:S(2)}) collective-permute-start(f32[8,6,8,128]{3,2,1,0:T(8,128)S(1)} %get-tuple-element.40), channel_id=1, source_target_pairs={{0,32},{32,0},{64,96},{96,64},{128,160},{160,128},{192,224},{224,1... | collective-permute-start | bytes 589832 | tf_op jit(solution)/shard_map/ppermute | solution.py:298
  23.0 1.0 %collective-permute-done.2.b_ref = f32[8,6,8,128]{3,2,1,0:T(8,128)S(1)} collective-permute-done((f32[8,6,8,128]{3,2,1,0:T(8,128)S(1)}, f32[8,6,8,128]{3,2,1,0:T(8,128)S(1)}, u32[]{:S(2)}, u32[]{:S(2)}) %collective-permute-start.2) | collective-permute-done | bytes 196640 | tf_op jit(solution)/shard_map/ppermute | solution.py:298
  24.1 18.8 %all_to_all.20.got_ref = f32[8,6,8,128]{3,2,1,0:T(8,128)S(1)} all-to-all(f32[8,6,8,128]{3,2,1,0:T(8,128)S(1)} %add_cores.1), channel_id=1, replica_groups={{0,64,128,192,256,320,384,448},{32,96,160,224,288,352,416,480},{1,65,12..., dimensions={0} | all-to-all | bytes 393216 | tf_op jit(solution)/shard_map/all_to_all | solution.py:300
  42.9 11.3 %all_to_all.21.mine_ref = f32[8,6,8,128]{3,2,1,0:T(8,128)S(1)} all-to-all(f32[8,6,8,128]{3,2,1,0:T(8,128)S(1)} %get-tuple-element.45), channel_id=1, replica_groups={{0,64,128,192,256,320,384,448},{32,96,160,224,288,352,416,480},{1,65,12..., dimensions={0} | all-to-all | bytes 393216 | tf_op jit(solution)/shard_map/all_to_all | solution.py:309
  54.3 4.7 %collective-permute-start.3 = (f32[8,6,8,128]{3,2,1,0:T(8,128)S(1)}, f32[8,6,8,128]{3,2,1,0:T(8,128)S(1)}, u32[]{:S(2)}, u32[]{:S(2)}) collective-permute-start(f32[8,6,8,128]{3,2,1,0:T(8,128)S(1)} %all_to_all.21.mine_ref), channel_id=1, source_target_pairs={{0,32},{32,0},{64,96},{96,64},{128,160},{160,128},{192,224},{224,1... | collective-permute-start | bytes 589832 | tf_op jit(solution)/shard_map/ppermute | solution.py:310
  59.0 1.0 %collective-permute-done.3.other_ref = f32[8,6,8,128]{3,2,1,0:T(8,128)S(1)} collective-permute-done((f32[8,6,8,128]{3,2,1,0:T(8,128)S(1)}, f32[8,6,8,128]{3,2,1,0:T(8,128)S(1)}, u32[]{:S(2)}, u32[]{:S(2)}) %collective-permute-start.3) | collective-permute-done | bytes 196640 | tf_op jit(solution)/shard_map/ppermute | solution.py:310
  60.1 0.1 weighted.1
  60.2 3.3 %collective-permute-start.4 = (f32[48,8,128]{2,1,0:T(8,128)S(1)}, f32[48,8,128]{2,1,0:T(8,128)S(1)}, u32[]{:S(2)}, u32[]{:S(2)}) collective-permute-start(f32[48,8,128]{2,1,0:T(8,128)S(1)} %get-tuple-element.46), channel_id=1, source_target_pairs={{0,31},{1,2},{2,1},{3,4},{4,3},{5,6},{6,5},{7,8},{8,7},{9,10},{10,... | collective-permute-start | bytes 589832 | tf_op jit(solution)/shard_map/ppermute | solution.py:319
  63.5 1.9 %collective-permute-start.5 = (f32[48,8,128]{2,1,0:T(8,128)S(1)}, f32[48,8,128]{2,1,0:T(8,128)S(1)}, u32[]{:S(2)}, u32[]{:S(2)}) collective-permute-start(f32[48,8,128]{2,1,0:T(8,128)S(1)} %get-tuple-element.47), channel_id=1, source_target_pairs={{0,1},{1,0},{2,3},{3,2},{4,5},{5,4},{6,7},{7,6},{8,9},{9,8},{10,11... | collective-permute-start | bytes 589832 | tf_op jit(solution)/shard_map/ppermute | solution.py:320
  65.5 0.0 copy-done.1
  65.5 1.2 %local.1 = (f32[96,8,128]{2,1,0:T(8,128)S(1)}, bf16[768,768]{1,0:T(8,128)(2,1)S(1)}, bf16[768,768]{1,0:T(8,128)(2,1)S(1)}) custom-call(f32[96,8,128]{2,1,0:T(8,128)S(1)} %get-tuple-element.48.w_ref, f32[96,8,128]{2,1,0:T(8,128)S(1)} %bitcast.10, bf16[512,256]{1,0:T(8,128)(2,1)S(1)} %get-tuple-element.49.own_ref, ...), custom_call_target="tpu_custom_call" | custom-call | flops 603979776 | bytes 4194304 | tf_op jit(solution)/shard_map/local/pallas_call | solution.py:321
  66.7 4.8 %collective-permute-done.4.far_ref = f32[48,8,128]{2,1,0:T(8,128)S(1)} collective-permute-done((f32[48,8,128]{2,1,0:T(8,128)S(1)}, f32[48,8,128]{2,1,0:T(8,128)S(1)}, u32[]{:S(2)}, u32[]{:S(2)}) %collective-permute-start.4) | collective-permute-done | bytes 196640 | tf_op jit(solution)/shard_map/ppermute | solution.py:319
  71.5 0.0 collective-permute-done.5.near_ref
  71.5 1.3 %adjoint.1 = (f32[96,8,128]{2,1,0:T(8,128)S(1)}, f32[16,1,128]{2,1,0:T(1,128)S(1)}) custom-call(f32[48,8,128]{2,1,0:T(8,128)S(1)} %collective-permute-done.4.far_ref, f32[48,8,128]{2,1,0:T(8,128)S(1)} %collective-permute-done.5.near_ref, f32[96,8,128]{2,1,0:T(8,128)S(1)} %get-tuple-element.52.part_ref, bf16[512,256]{1,0:T(8,128)(2,1)S(1)} %get-tuple-element.37.halo_ref, ...), custom_call_target="tpu_custom_call" | custom-call | tf_op jit(solution)/shard_map/adjoint/pallas_call | solution.py:330
  72.8 10.6 %all_to_all.22 = f32[16,1,128]{2,1,0:T(1,128)S(1)} all-to-all(f32[16,1,128]{2,1,0:T(1,128)S(1)} %get-tuple-element.57), channel_id=1, replica_groups=mesh['member'=16,'tile'=32] {'member'}, dimensions={0} | all-to-all | bytes 16384 | tf_op jit(solution)/shard_map/all_to_all | solution.py:338
  83.5 0.6 broadcast_in_dim.10
  84.1 6.2 %all-to-all-start.3 = ((f32[32,1,128]{2,1,0:T(1,128)}), f32[32,1,128]{2,1,0:T(1,128)S(1)}, u32[]{:S(2)}, u32[]{:S(2)}) async-start(f32[32,1,128]{2,1,0:T(1,128)} %broadcast_in_dim.10), calls=%async_computation.3 | async-start | bytes 32768 | tf_op jit(solution)/shard_map/all_to_all | solution.py:340
  90.3 0.6 copy.10
  90.9 0.7 copy.11
  91.7 7.2 %all-to-all-done.3 = f32[32,1,128]{2,1,0:T(1,128)S(1)} async-done(((f32[32,1,128]{2,1,0:T(1,128)}), f32[32,1,128]{2,1,0:T(1,128)S(1)}, u32[]{:S(2)}, u32[]{:S(2)}) %all-to-all-start.3) | async-done | bytes 16416 | tf_op jit(solution)/shard_map/all_to_all | solution.py:340
  98.9 0.1 reshape.18
  99.0 0.1 reduce_sum.29
  99.1 0.6 fusion
  (5 shorter events, 0.1 us)
Async XLA Ops:
  0.6 16.8 %copy-start = (bf16[1,96,8,128]{3,2,1,0:T(8,128)(2,1)S(1)}, bf16[1,96,8,128]{3,2,1,0:T(8,128)(2,1)}, u32[]{:S(2)}) copy-start(bf16[1,96,8,128]{3,2,1,0:T(8,128)(2,1)} %param.6) | copy-start | bytes 589828
  1.9 13.8 %collective-permute-start = (f32[48,8,128]{2,1,0:T(8,128)S(1)}, f32[48,8,128]{2,1,0:T(8,128)S(1)}, u32[]{:S(2)}, u32[]{:S(2)}) collective-permute-start(f32[48,8,128]{2,1,0:T(8,128)S(1)} %get-tuple-element.31), channel_id=1, source_target_pairs={{0,31},{1,2},{2,1},{3,4},{4,3},{5,6},{6,5},{7,8},{8,7},{9,10},{10,... | collective-permute-start | bytes 589832 | tf_op jit(solution)/shard_map/ppermute | solution.py:273
  10.0 7.3 %collective-permute-start.1 = (f32[48,8,128]{2,1,0:T(8,128)S(1)}, f32[48,8,128]{2,1,0:T(8,128)S(1)}, u32[]{:S(2)}, u32[]{:S(2)}) collective-permute-start(f32[48,8,128]{2,1,0:T(8,128)S(1)} %get-tuple-element.32), channel_id=1, source_target_pairs={{0,1},{1,0},{2,3},{3,2},{4,5},{5,4},{6,7},{7,6},{8,9},{9,8},{10,11... | collective-permute-start | bytes 589832 | tf_op jit(solution)/shard_map/ppermute | solution.py:274
  18.6 46.8 %copy-start.1 = (f32[1,96,8,128]{3,2,1,0:T(8,128)S(1)}, f32[1,96,8,128]{3,2,1,0:T(8,128)}, u32[]{:S(2)}) copy-start(f32[1,96,8,128]{3,2,1,0:T(8,128)} %param.5) | copy-start | bytes 1179652
  18.6 5.4 %collective-permute-start.2 = (f32[8,6,8,128]{3,2,1,0:T(8,128)S(1)}, f32[8,6,8,128]{3,2,1,0:T(8,128)S(1)}, u32[]{:S(2)}, u32[]{:S(2)}) collective-permute-start(f32[8,6,8,128]{3,2,1,0:T(8,128)S(1)} %get-tuple-element.40), channel_id=1, source_target_pairs={{0,32},{32,0},{64,96},{96,64},{128,160},{160,128},{192,224},{224,1... | collective-permute-start | bytes 589832 | tf_op jit(solution)/shard_map/ppermute | solution.py:298
  54.3 5.8 %collective-permute-start.3 = (f32[8,6,8,128]{3,2,1,0:T(8,128)S(1)}, f32[8,6,8,128]{3,2,1,0:T(8,128)S(1)}, u32[]{:S(2)}, u32[]{:S(2)}) collective-permute-start(f32[8,6,8,128]{3,2,1,0:T(8,128)S(1)} %all_to_all.21.mine_ref), channel_id=1, source_target_pairs={{0,32},{32,0},{64,96},{96,64},{128,160},{160,128},{192,224},{224,1... | collective-permute-start | bytes 589832 | tf_op jit(solution)/shard_map/ppermute | solution.py:310
  60.2 11.3 %collective-permute-start.4 = (f32[48,8,128]{2,1,0:T(8,128)S(1)}, f32[48,8,128]{2,1,0:T(8,128)S(1)}, u32[]{:S(2)}, u32[]{:S(2)}) collective-permute-start(f32[48,8,128]{2,1,0:T(8,128)S(1)} %get-tuple-element.46), channel_id=1, source_target_pairs={{0,31},{1,2},{2,1},{3,4},{4,3},{5,6},{6,5},{7,8},{8,7},{9,10},{10,... | collective-permute-start | bytes 589832 | tf_op jit(solution)/shard_map/ppermute | solution.py:319
  63.5 8.0 %collective-permute-start.5 = (f32[48,8,128]{2,1,0:T(8,128)S(1)}, f32[48,8,128]{2,1,0:T(8,128)S(1)}, u32[]{:S(2)}, u32[]{:S(2)}) collective-permute-start(f32[48,8,128]{2,1,0:T(8,128)S(1)} %get-tuple-element.47), channel_id=1, source_target_pairs={{0,1},{1,0},{2,3},{3,2},{4,5},{5,4},{6,7},{7,6},{8,9},{9,8},{10,11... | collective-permute-start | bytes 589832 | tf_op jit(solution)/shard_map/ppermute | solution.py:320
  84.1 14.8 %all-to-all-start.3 = ((f32[32,1,128]{2,1,0:T(1,128)}), f32[32,1,128]{2,1,0:T(1,128)S(1)}, u32[]{:S(2)}, u32[]{:S(2)}) async-start(f32[32,1,128]{2,1,0:T(1,128)} %broadcast_in_dim.10), calls=%async_computation.3 | async-start | bytes 32768 | tf_op jit(solution)/shard_map/all_to_all | solution.py:340

commit v4 on v3

--- a/solution.py
+++ b/solution.py
@@ -187,8 +187,8 @@
     other_ref[...] = jnp.where(even, term[:, 1], term[:, 0])
 
 
-def add_kernel(a_ref, b_ref, out_ref):
-    out_ref[...] = a_ref[...] + b_ref[...]
+def add_kernel(mine_ref, sent_ref, out_ref):
+    out_ref[...] = mine_ref[...] + sent_ref[1 - lax.axis_index("member") % 2]
 
 
 def middle_kernel(got_ref, weight_ref, innovation_ref, sum_in, inc_ref, misfit_ref, sum_ref):
@@ -200,11 +200,9 @@
     sum_ref[...] = sum_in[...] + jnp.sum(cost.reshape(-1, cost.shape[2]), axis=0, keepdims=True)
 
 
-def weight_kernel(inverse, m_ref, mine_ref, other_ref, w_ref, far_ref, near_ref):
+def weight_kernel(inverse, m_ref, both_ref, w_ref, far_ref, near_ref):
     levels, lat, columns = m_ref.shape
-    mine, other = mine_ref[...], other_ref[...]
-    even = lax.axis_index("member") % 2 == 0
-    misfit = jnp.stack([jnp.where(even, mine, other), jnp.where(even, other, mine)], axis=1)
+    misfit = jnp.stack([both_ref[0], both_ref[1]], axis=1)
     w = m_ref[...].astype(f32) * misfit.reshape(levels, lat, columns) * inverse
     w_ref[...] = w
     half_levels = near_ref.shape[0]
@@ -256,7 +254,7 @@
     band = pltpu.VMEM((CLASSES * columns, 2 * columns), bf16)
     line = pltpu.VMEM((1, columns), f32)
     chips = [list(range(core, groups, 2)) for core in range(2)]
-    partners = [(i, i ^ 1) for i in range(groups)]
+    cores = [[i, i + 1] for i in range(0, groups, 2)]
     near_pairs = [(i, i ^ 1) for i in range(tiles)]
     far_pairs = [(i, (((i - 1) % tiles ^ 1) + 1) % tiles) for i in range(tiles)]
     hbm = [pl.BlockSpec(memory_space=pltpu.HBM)]
@@ -295,8 +293,8 @@
         compiler_params=params(),
         name="forward",
     )(far, near, y, fh, fl, halo, hot, member)
-    other = lax.ppermute(other, "member", partners)
-    both = pl.pallas_call(add_kernel, out_shape=half_term, in_specs=vmem(2), out_specs=vmem(1)[0], compiler_params=params(), name="add_cores")(mine, other)
+    sent = lax.all_gather(other, "member", axis_index_groups=cores)
+    both = pl.pallas_call(add_kernel, out_shape=half_term, in_specs=vmem(2), out_specs=vmem(1)[0], compiler_params=params(), name="add_cores")(mine, sent)
     got = lax.all_to_all(both, "member", 0, 0, axis_index_groups=chips)
     inc, misfit_share, sums = pl.pallas_call(
         middle_kernel,
@@ -307,15 +305,15 @@
         name="middle",
     )(got, weight_share, innovation_share, half_sum)
     misfit_mine = lax.all_to_all(misfit_share, "member", 0, 0, axis_index_groups=chips)
-    misfit_other = lax.ppermute(misfit_mine, "member", partners)
+    misfit = lax.all_gather(misfit_mine, "member", axis_index_groups=cores)
     w, far, near = pl.pallas_call(
         functools.partial(weight_kernel, inverse),
         out_shape=(field, half_pack, half_pack),
-        in_specs=vmem(3),
+        in_specs=vmem(2),
         out_specs=tuple(vmem(3)),
         compiler_params=params(),
         name="weighted",
-    )(member, misfit_mine, misfit_other)
+    )(member, misfit)
     far = lax.ppermute(far, "tile", far_pairs)
     near = lax.ppermute(near, "tile", near_pairs)
     inner, ah, al = pl.pallas_call(

time: 100 us -> 97.5 us (0.975)
  starting transfers between devices: 30.5 us -> 21.5 us
  blocking collectives: 40.8 us -> 49.5 us
  waiting for transfers between devices: 15.8 us -> 13.6 us
    ppermute x2 -> x0, starting transfers between devices: 9.08 us -> none  [the longest x1 4.75 us: per_device(): misfit_other = lax.ppermute(misfit_mine, 'member', partners)]
    all_gather x0 -> x2, blocking collectives: none -> 8.56 us  [the longest x1 4.56 us: per_device(): misfit = lax.all_gather(misfit_mine, 'member', axis_index_groups=cores)]
    ppermute x2 -> x0, waiting for transfers between devices: 2.1 us -> none  [the longest x1 1.05 us: per_device(): other = lax.ppermute(other, 'member', partners)]
  transfers between devices with their start and end apart: 7 -> 5, of which waited for: 5 -> 3; matrix products, arithmetic and copies ran while one was open for 1% -> 1% of each run, Pallas kernels for 5% -> 5%
where the time goes in v4:
time: 97.5 us; the launch traced here: 97.1 us
  blocking collectives  49.5 us (51%)
  starting transfers between devices  21.5 us (22%)
  waiting for transfers between devices  13.6 us (14%)
  Pallas kernels  8.95 us (9%)
  local copies, waits for them, and re-layouts  2.64 us (3%)
    all_to_all x1, blocking collectives, per_device(): got = lax.all_to_all(both, 'member', 0, 0, axis_index_groups=chips)  19 us
    ppermute x2, starting transfers between devices, per_device(): far = lax.ppermute(far, 'tile', far_pairs)  11.4 us
    all_to_all x1, blocking collectives, per_device(): lax.all_to_all(misfit_share, 'member', 0, 0, axis_index_groups=chips)  11.3 us
    all_to_all x1, blocking collectives, per_device(): sums = jnp.sum(lax.all_to_all(sums, 'member', 0, 0), axis=0)  10.6 us
    all_to_all x1, waiting for transfers between devices, per_device(): sums = jnp.sum(lax.all_to_all(sums, 'tile', 0, 0), axis=0)  7.07 us
    all_to_all x1, starting transfers between devices, per_device(): sums = jnp.sum(lax.all_to_all(sums, 'tile', 0, 0), axis=0)  6.19 us
    ppermute x2, waiting for transfers between devices, per_device(): far = lax.ppermute(far, 'tile', far_pairs)  4.85 us
    all_gather x1, blocking collectives, per_device(): misfit = lax.all_gather(misfit_mine, 'member', axis_index_groups=cores)  4.56 us
  transfers between devices with their start and end apart: 5, of which 3 were waited for; matrix products, arithmetic and copies ran while one was open for 1% of the time, Pallas kernels for 5%

profile of v4, /device:TPU:1, one launch (start us, length us, event | category | flops | bytes accessed | tf_op | source)
XLA Modules:
  0.0 97.1 jit_solution(12590821764182873040)
XLA Ops:
  0.6 0.0 copy-start
  0.6 1.3 %pack_control.1 = (f32[48,8,128]{2,1,0:T(8,128)S(1)}, f32[48,8,128]{2,1,0:T(8,128)S(1)}, f32[96,8,128]{2,1,0:T(8,128)S(1)}) custom-call(f32[96,8,128]{2,1,0:T(8,128)} %bitcast.13), custom_call_target="tpu_custom_call" | custom-call | tf_op jit(solution)/shard_map/pack_control/pallas_call | solution.py:262
  1.9 8.1 %collective-permute-start = (f32[48,8,128]{2,1,0:T(8,128)S(1)}, f32[48,8,128]{2,1,0:T(8,128)S(1)}, u32[]{:S(2)}, u32[]{:S(2)}) collective-permute-start(f32[48,8,128]{2,1,0:T(8,128)S(1)} %get-tuple-element.31), channel_id=1, source_target_pairs={{0,31},{1,2},{2,1},{3,4},{4,3},{5,6},{6,5},{7,8},{8,7},{9,10},{10,... | collective-permute-start | bytes 589832 | tf_op jit(solution)/shard_map/ppermute | solution.py:271
  10.0 1.9 %collective-permute-start.1 = (f32[48,8,128]{2,1,0:T(8,128)S(1)}, f32[48,8,128]{2,1,0:T(8,128)S(1)}, u32[]{:S(2)}, u32[]{:S(2)}) collective-permute-start(f32[48,8,128]{2,1,0:T(8,128)S(1)} %get-tuple-element.32), channel_id=1, source_target_pairs={{0,1},{1,0},{2,3},{3,2},{4,5},{5,4},{6,7},{7,6},{8,9},{9,8},{10,11... | collective-permute-start | bytes 589832 | tf_op jit(solution)/shard_map/ppermute | solution.py:272
  12.0 3.8 %operators.1 = (bf16[768,768]{1,0:T(8,128)(2,1)S(1)}, bf16[768,768]{1,0:T(8,128)(2,1)S(1)}, f32[96,768]{1,0:T(8,128)S(1)}, f32[8,768]{1,0:T(8,128)S(1)}, bf16[51...) custom-call(s32[96]{0:T(128)} %classes.1, ...), custom_call_target="tpu_custom_call" | custom-call | flops 452984832 | bytes 6291456 | tf_op jit(solution)/shard_map/operators/pallas_call | solution.py:273
  15.7 0.0 collective-permute-done.far_ref
  15.7 1.6 %collective-permute-done.1.near_ref = f32[48,8,128]{2,1,0:T(8,128)S(1)} collective-permute-done((f32[48,8,128]{2,1,0:T(8,128)S(1)}, f32[48,8,128]{2,1,0:T(8,128)S(1)}, u32[]{:S(2)}, u32[]{:S(2)}) %collective-permute-start.1) | collective-permute-done | bytes 196640 | tf_op jit(solution)/shard_map/ppermute | solution.py:272
  17.4 0.0 copy-done
  17.4 1.2 %forward.1 = (f32[8,6,8,128]{3,2,1,0:T(8,128)S(1)}, f32[8,6,8,128]{3,2,1,0:T(8,128)S(1)}) custom-call(f32[48,8,128]{2,1,0:T(8,128)S(1)} %collective-permute-done.far_ref, f32[48,8,128]{2,1,0:T(8,128)S(1)} %collective-permute-done.1.near_ref, f32[768,128]{1,0:T(8,128)S(1)} %get-tuple-element.34.y_ref, bf16[768,768]{1,0:T(8,128)(2,1)S(1)} %get-tuple-element.35.fh_ref, ...), custom_call_target="tpu_custom_call" | custom-call | tf_op jit(solution)/shard_map/forward/pallas_call | solution.py:288
  18.6 4.0 %all-gather = f32[16,6,8,128]{3,2,1,0:T(8,128)S(1)} all-gather(f32[8,6,8,128]{3,2,1,0:T(8,128)S(1)} %get-tuple-element.40), channel_id=2, replica_groups={{0,32},{64,96},{128,160},{192,224},{256,288},{320,352},{384,416},{448,4..., dimensions={0}, use_global_device_ids=true | all-gather | bytes 589824 | tf_op jit(solution)/shard_map/all_gather | solution.py:296
  22.7 0.0 copy-start.1
  22.7 19.0 %all_to_all.20.got_ref = f32[8,6,8,128]{3,2,1,0:T(8,128)S(1)} all-to-all(f32[8,6,8,128]{3,2,1,0:T(8,128)S(1)} %add_cores.1), channel_id=1, replica_groups={{0,64,128,192,256,320,384,448},{32,96,160,224,288,352,416,480},{1,65,12..., dimensions={0} | all-to-all | bytes 393216 | tf_op jit(solution)/shard_map/all_to_all | solution.py:298
  41.7 11.3 %all_to_all.21 = f32[8,6,8,128]{3,2,1,0:T(8,128)S(1)} all-to-all(f32[8,6,8,128]{3,2,1,0:T(8,128)S(1)} %get-tuple-element.45), channel_id=1, replica_groups={{0,64,128,192,256,320,384,448},{32,96,160,224,288,352,416,480},{1,65,12..., dimensions={0} | all-to-all | bytes 393216 | tf_op jit(solution)/shard_map/all_to_all | solution.py:307
  53.0 4.6 %all-gather.1 = f32[16,6,8,128]{3,2,1,0:T(8,128)S(1)} all-gather(f32[8,6,8,128]{3,2,1,0:T(8,128)S(1)} %all_to_all.21), channel_id=3, replica_groups={{0,32},{64,96},{128,160},{192,224},{256,288},{320,352},{384,416},{448,4..., dimensions={0}, use_global_device_ids=true | all-gather | bytes 589824 | tf_op jit(solution)/shard_map/all_gather | solution.py:308
  57.6 0.1 weighted.1
  57.7 3.3 %collective-permute-start.2 = (f32[48,8,128]{2,1,0:T(8,128)S(1)}, f32[48,8,128]{2,1,0:T(8,128)S(1)}, u32[]{:S(2)}, u32[]{:S(2)}) collective-permute-start(f32[48,8,128]{2,1,0:T(8,128)S(1)} %get-tuple-element.46), channel_id=1, source_target_pairs={{0,31},{1,2},{2,1},{3,4},{4,3},{5,6},{6,5},{7,8},{8,7},{9,10},{10,... | collective-permute-start | bytes 589832 | tf_op jit(solution)/shard_map/ppermute | solution.py:317
  61.0 1.9 %collective-permute-start.3 = (f32[48,8,128]{2,1,0:T(8,128)S(1)}, f32[48,8,128]{2,1,0:T(8,128)S(1)}, u32[]{:S(2)}, u32[]{:S(2)}) collective-permute-start(f32[48,8,128]{2,1,0:T(8,128)S(1)} %get-tuple-element.47), channel_id=1, source_target_pairs={{0,1},{1,0},{2,3},{3,2},{4,5},{5,4},{6,7},{7,6},{8,9},{9,8},{10,11... | collective-permute-start | bytes 589832 | tf_op jit(solution)/shard_map/ppermute | solution.py:318
  62.9 0.0 copy-done.1
  62.9 1.2 %local.1 = (f32[96,8,128]{2,1,0:T(8,128)S(1)}, bf16[768,768]{1,0:T(8,128)(2,1)S(1)}, bf16[768,768]{1,0:T(8,128)(2,1)S(1)}) custom-call(f32[96,8,128]{2,1,0:T(8,128)S(1)} %get-tuple-element.48.w_ref, f32[96,8,128]{2,1,0:T(8,128)S(1)} %bitcast.14, bf16[512,256]{1,0:T(8,128)(2,1)S(1)} %get-tuple-element.49.own_ref, ...), custom_call_target="tpu_custom_call" | custom-call | flops 603979776 | bytes 4194304 | tf_op jit(solution)/shard_map/local/pallas_call | solution.py:319
  64.2 4.8 %collective-permute-done.2.far_ref = f32[48,8,128]{2,1,0:T(8,128)S(1)} collective-permute-done((f32[48,8,128]{2,1,0:T(8,128)S(1)}, f32[48,8,128]{2,1,0:T(8,128)S(1)}, u32[]{:S(2)}, u32[]{:S(2)}) %collective-permute-start.2) | collective-permute-done | bytes 196640 | tf_op jit(solution)/shard_map/ppermute | solution.py:317
  69.0 0.0 collective-permute-done.3.near_ref
  69.0 1.3 %adjoint.1 = (f32[96,8,128]{2,1,0:T(8,128)S(1)}, f32[16,1,128]{2,1,0:T(1,128)S(1)}) custom-call(f32[48,8,128]{2,1,0:T(8,128)S(1)} %collective-permute-done.2.far_ref, f32[48,8,128]{2,1,0:T(8,128)S(1)} %collective-permute-done.3.near_ref, f32[96,8,128]{2,1,0:T(8,128)S(1)} %get-tuple-element.52.part_ref, bf16[512,256]{1,0:T(8,128)(2,1)S(1)} %get-tuple-element.37.halo_ref, ...), custom_call_target="tpu_custom_call" | custom-call | tf_op jit(solution)/shard_map/adjoint/pallas_call | solution.py:328
  70.3 10.6 %all_to_all.22 = f32[16,1,128]{2,1,0:T(1,128)S(1)} all-to-all(f32[16,1,128]{2,1,0:T(1,128)S(1)} %get-tuple-element.57), channel_id=1, replica_groups=mesh['member'=16,'tile'=32] {'member'}, dimensions={0} | all-to-all | bytes 16384 | tf_op jit(solution)/shard_map/all_to_all | solution.py:336
  81.0 0.6 broadcast_in_dim.10
  81.6 6.2 %all-to-all-start.3 = ((f32[32,1,128]{2,1,0:T(1,128)}), f32[32,1,128]{2,1,0:T(1,128)S(1)}, u32[]{:S(2)}, u32[]{:S(2)}) async-start(f32[32,1,128]{2,1,0:T(1,128)} %broadcast_in_dim.10), calls=%async_computation.3 | async-start | bytes 32768 | tf_op jit(solution)/shard_map/all_to_all | solution.py:338
  87.8 0.6 copy.10
  88.4 0.7 copy.11
  89.2 7.1 %all-to-all-done.3 = f32[32,1,128]{2,1,0:T(1,128)S(1)} async-done(((f32[32,1,128]{2,1,0:T(1,128)}), f32[32,1,128]{2,1,0:T(1,128)S(1)}, u32[]{:S(2)}, u32[]{:S(2)}) %all-to-all-start.3) | async-done | bytes 16416 | tf_op jit(solution)/shard_map/all_to_all | solution.py:338
  96.3 0.1 reshape.18
  96.3 0.1 reduce_sum.29
  96.5 0.6 fusion
  (5 shorter events, 0.1 us)
Async XLA Ops:
  0.6 16.8 %copy-start = (bf16[1,96,8,128]{3,2,1,0:T(8,128)(2,1)S(1)}, bf16[1,96,8,128]{3,2,1,0:T(8,128)(2,1)}, u32[]{:S(2)}) copy-start(bf16[1,96,8,128]{3,2,1,0:T(8,128)(2,1)} %param.6) | copy-start | bytes 589828
  1.9 13.8 %collective-permute-start = (f32[48,8,128]{2,1,0:T(8,128)S(1)}, f32[48,8,128]{2,1,0:T(8,128)S(1)}, u32[]{:S(2)}, u32[]{:S(2)}) collective-permute-start(f32[48,8,128]{2,1,0:T(8,128)S(1)} %get-tuple-element.31), channel_id=1, source_target_pairs={{0,31},{1,2},{2,1},{3,4},{4,3},{5,6},{6,5},{7,8},{8,7},{9,10},{10,... | collective-permute-start | bytes 589832 | tf_op jit(solution)/shard_map/ppermute | solution.py:271
  10.0 7.3 %collective-permute-start.1 = (f32[48,8,128]{2,1,0:T(8,128)S(1)}, f32[48,8,128]{2,1,0:T(8,128)S(1)}, u32[]{:S(2)}, u32[]{:S(2)}) collective-permute-start(f32[48,8,128]{2,1,0:T(8,128)S(1)} %get-tuple-element.32), channel_id=1, source_target_pairs={{0,1},{1,0},{2,3},{3,2},{4,5},{5,4},{6,7},{7,6},{8,9},{9,8},{10,11... | collective-permute-start | bytes 589832 | tf_op jit(solution)/shard_map/ppermute | solution.py:272
  22.7 40.3 %copy-start.1 = (f32[1,96,8,128]{3,2,1,0:T(8,128)S(1)}, f32[1,96,8,128]{3,2,1,0:T(8,128)}, u32[]{:S(2)}) copy-start(f32[1,96,8,128]{3,2,1,0:T(8,128)} %param.5) | copy-start | bytes 1179652
  57.7 11.3 %collective-permute-start.2 = (f32[48,8,128]{2,1,0:T(8,128)S(1)}, f32[48,8,128]{2,1,0:T(8,128)S(1)}, u32[]{:S(2)}, u32[]{:S(2)}) collective-permute-start(f32[48,8,128]{2,1,0:T(8,128)S(1)} %get-tuple-element.46), channel_id=1, source_target_pairs={{0,31},{1,2},{2,1},{3,4},{4,3},{5,6},{6,5},{7,8},{8,7},{9,10},{10,... | collective-permute-start | bytes 589832 | tf_op jit(solution)/shard_map/ppermute | solution.py:317
  61.0 8.0 %collective-permute-start.3 = (f32[48,8,128]{2,1,0:T(8,128)S(1)}, f32[48,8,128]{2,1,0:T(8,128)S(1)}, u32[]{:S(2)}, u32[]{:S(2)}) collective-permute-start(f32[48,8,128]{2,1,0:T(8,128)S(1)} %get-tuple-element.47), channel_id=1, source_target_pairs={{0,1},{1,0},{2,3},{3,2},{4,5},{5,4},{6,7},{7,6},{8,9},{9,8},{10,11... | collective-permute-start | bytes 589832 | tf_op jit(solution)/shard_map/ppermute | solution.py:318
  81.6 14.6 %all-to-all-start.3 = ((f32[32,1,128]{2,1,0:T(1,128)}), f32[32,1,128]{2,1,0:T(1,128)S(1)}, u32[]{:S(2)}, u32[]{:S(2)}) async-start(f32[32,1,128]{2,1,0:T(1,128)} %broadcast_in_dim.10), calls=%async_computation.3 | async-start | bytes 32768 | tf_op jit(solution)/shard_map/all_to_all | solution.py:338

commit v5 on v4

--- a/solution.py
+++ b/solution.py
@@ -9,17 +9,13 @@
 from jax.sharding import PartitionSpec as P
 
 CLASSES = 4
-PARTS = 4
+PARTS = 2
 VMEM_LIMIT = 48 * 1024 * 1024
 f32, bf16 = jnp.float32, jnp.bfloat16
 
 
 def vmem(count):
     return [pl.BlockSpec(memory_space=pltpu.VMEM)] * count
-
-
-def smem():
-    return pl.BlockSpec(memory_space=pltpu.SMEM)
 
 
 def params():
@@ -101,19 +97,50 @@
 
 
 def operators_kernel(
-    classes, x_ref, weight_hbm, innovation_hbm,
+    classes_hbm, x_ref, weight_hbm, innovation_hbm,
     fh_ref, fl_ref, wide_ref, mix_ref, own_ref, halo_ref, hot_ref, y_ref, sum_ref, weight_ref, innovation_ref,
-    class_ref, class_rows_ref, sems,
+    classes, class_ref, class_rows_ref, sems,
 ):
     levels, lat, columns = x_ref.shape
     rows = levels * lat
     half = columns // 2
     share = weight_ref.shape[0]
     mine = pl.ds(lax.axis_index("member") * share, share)
-    weight_copy = pltpu.make_async_copy(weight_hbm.at[mine], weight_ref, sems.at[0])
-    innovation_copy = pltpu.make_async_copy(innovation_hbm.at[mine], innovation_ref, sems.at[1])
+    class_copy = pltpu.make_async_copy(classes_hbm, classes, sems.at[0])
+    weight_copy = pltpu.make_async_copy(weight_hbm.at[mine], weight_ref, sems.at[1])
+    innovation_copy = pltpu.make_async_copy(innovation_hbm.at[mine], innovation_ref, sems.at[2])
+    class_copy.start()
     weight_copy.start()
     innovation_copy.start()
+    d = lax.broadcasted_iota(jnp.int32, (columns, columns), 0)
+    out = lax.broadcasted_iota(jnp.int32, (columns, columns), 1)
+    for ref, place in ((own_ref, d), (halo_ref, jnp.where(d < half, d + columns, d - columns))):
+        far = (place - out).astype(f32)
+        inside = jnp.abs(far) <= half
+        for c in range(CLASSES):
+            sigma = half * class_scale(c) / 4.0
+            e = np.arange(-half, half + 1, dtype=np.float32)
+            norm = float(np.sqrt(np.sum(np.exp(-e * e / np.float32(sigma * sigma)), dtype=np.float32)))
+            band = jnp.where(inside, jnp.exp(-far * far / (2.0 * sigma * sigma)) / norm, 0.0)
+            at = pl.ds(c * columns, columns)
+            ref[at, :columns], ref[at, columns:] = split(band)
+    i = lax.broadcasted_iota(jnp.int32, (lat, rows), 0)
+    j = lax.broadcasted_iota(jnp.int32, (lat, rows), 1) & (lat - 1)
+    gap = (i - j).astype(f32)
+    patterns = []
+    for c in range(CLASSES):
+        rho = lat * class_scale(c) / 8.0
+        e = np.arange(-(lat - 1), lat, dtype=np.float32)
+        norm = float(np.sqrt(np.sum(np.exp(-e * e / np.float32(rho * rho)), dtype=np.float32)))
+        patterns.append(jnp.exp(-gap * gap / (2.0 * rho * rho)) / norm)
+    ahead = lax.broadcasted_iota(jnp.int32, (levels, rows), 1) - lat * lax.broadcasted_iota(jnp.int32, (levels, rows), 0)
+    spread = ((ahead >= 0) & (ahead < lat)).astype(f32).astype(bf16)
+    k = lax.broadcasted_iota(jnp.int32, (levels, levels), 0)
+    q = lax.broadcasted_iota(jnp.int32, (levels, levels), 1)
+    spacing = (k - q).astype(f32)
+    x = x_ref[...].reshape(rows, columns)
+    sum_ref[...] = 0.5 * jnp.sum(x * x, axis=0, keepdims=True)
+    class_copy.wait()
     for level in range(levels):
         class_ref[pl.ds(level, 1), :] = jnp.full((1, columns), classes[level].astype(f32), f32)
     class_lines = class_ref[...]
@@ -121,29 +148,16 @@
     class_rows_ref[...] = class_rows
     for c in range(CLASSES):
         hot_ref[c] = (class_rows == float(c)).astype(f32).astype(bf16)
-    k = lax.broadcasted_iota(jnp.int32, (levels, levels), 0)
-    q = lax.broadcasted_iota(jnp.int32, (levels, levels), 1)
     class_col = class_lines[:, :levels]
     class_row = jnp.sum(jnp.where(k == q, class_col, 0.0), axis=0, keepdims=True)
     scale_col = 1.0 + class_col
     scale_row = 1.0 + class_row
-    spacing = (k - q).astype(f32)
     vertical = jnp.exp(-spacing * spacing / (scale_col * scale_col + scale_row * scale_row))
-    ahead = lax.broadcasted_iota(jnp.int32, (levels, rows), 1) - lat * lax.broadcasted_iota(jnp.int32, (levels, rows), 0)
-    spread = ((ahead >= 0) & (ahead < lat)).astype(f32).astype(bf16)
     vh, vl = split(vertical)
     wide_ref[...] = dot(vh, spread) + dot(vl, spread)
     class_wide = dot(jnp.broadcast_to(class_row, (8, levels)).astype(bf16), spread)[:1]
-    i = lax.broadcasted_iota(jnp.int32, (lat, rows), 0)
-    j = lax.broadcasted_iota(jnp.int32, (lat, rows), 1) & (lat - 1)
-    gap = (i - j).astype(f32)
-    patterns = []
     mix = jnp.zeros((lat, rows), f32)
     for c in range(CLASSES):
-        rho = lat * class_scale(c) / 8.0
-        e = np.arange(-(lat - 1), lat, dtype=np.float32)
-        norm = float(np.sqrt(np.sum(np.exp(-e * e / np.float32(rho * rho)), dtype=np.float32)))
-        patterns.append(jnp.exp(-gap * gap / (2.0 * rho * rho)) / norm)
         mix = jnp.where(class_wide == float(c), patterns[c], mix)
     mix_ref[...] = mix
     for pair in range(levels // 2):
@@ -156,20 +170,6 @@
             both.append(wide_ref[pl.ds(level, 1), :] * pattern)
         at = pl.ds(2 * pair * lat, 2 * lat)
         fh_ref[at, :], fl_ref[at, :] = split(jnp.concatenate(both, axis=0))
-    d = lax.broadcasted_iota(jnp.int32, (columns, columns), 0)
-    out = lax.broadcasted_iota(jnp.int32, (columns, columns), 1)
-    for ref, place in ((own_ref, d), (halo_ref, jnp.where(d < half, d + columns, d - columns))):
-        far = (place - out).astype(f32)
-        inside = jnp.abs(far) <= half
-        for c in range(CLASSES):
-            sigma = half * class_scale(c) / 4.0
-            e = np.arange(-half, half + 1, dtype=np.float32)
-            norm = float(np.sqrt(np.sum(np.exp(-e * e / np.float32(sigma * sigma)), dtype=np.float32)))
-            band = jnp.where(inside, jnp.exp(-far * far / (2.0 * sigma * sigma)) / norm, 0.0)
-            at = pl.ds(c * columns, columns)
-            ref[at, :columns], ref[at, columns:] = split(band)
-    x = x_ref[...].reshape(rows, columns)
-    sum_ref[...] = 0.5 * jnp.sum(x * x, axis=0, keepdims=True)
     y_ref[...] = class_product(left_product(fh_ref[...], fl_ref[...], x), hot_ref, own_ref[...])
     weight_copy.wait()
     innovation_copy.wait()
@@ -209,9 +209,10 @@
     pack_halves(w[:half_levels], w[half_levels:], near_ref, far_ref, slice(None))
 
 
-def local_kernel(w_ref, x_ref, own_ref, hot_ref, wide_ref, mix_ref, out_ref, ah_ref, al_ref):
+def local_kernel(w_ref, x_ref, own_ref, hot_ref, wide_ref, mix_ref, inc_ref, out_ref, ah_ref, al_ref, inc_out):
     levels, lat, columns = w_ref.shape
     rows = levels * lat
+    inc_out[...] = inc_ref[...]
     mix = mix_ref[...]
     for pair in range(levels // 2):
         both = [wide_ref[pl.ds(level, 1), :] * mix for level in (2 * pair, 2 * pair + 1)]
@@ -234,6 +235,13 @@
     cost = sum_in[...]
     row = jnp.where(lane_is_low(square.shape, half), square + pltpu.roll(square, half, 1), cost + pltpu.roll(cost, half, 1))
     sums_ref[...] = jnp.broadcast_to(row[None], sums_ref.shape)
+
+
+def finish_kernel(cells, got_ref, square_ref, cost_ref):
+    row = jnp.sum(got_ref[...], axis=0)
+    low = lane_is_low(row.shape, row.shape[1] // 2)
+    square_ref[...] = jnp.sum(jnp.where(low, row, 0.0), axis=1, keepdims=True) / cells
+    cost_ref[...] = jnp.sum(jnp.where(low, 0.0, row), axis=1, keepdims=True) / cells
 
 
 def per_device(tiles, control, members, obs_weight, innovation, scale_index):
@@ -273,12 +281,13 @@
     fh, fl, wide, mix, own, halo, hot, y, half_sum, weight_share, innovation_share = pl.pallas_call(
         operators_kernel,
         out_shape=(square, square, pltpu.VMEM((levels, rows), f32), pltpu.VMEM((lat, rows), f32), band, band, pltpu.VMEM((CLASSES, rows, columns), bf16), pltpu.VMEM((rows, columns), f32), line, part, part),
-        in_specs=[smem()] + vmem(1) + hbm * 2,
+        in_specs=hbm + vmem(1) + hbm * 2,
         out_specs=tuple(vmem(11)),
         scratch_shapes=[
+            pltpu.SMEM((levels,), jnp.int32),
             pltpu.VMEM((levels, columns), f32),
             pltpu.VMEM((rows, columns), f32),
-            pltpu.SemaphoreType.DMA((2,)),
+            pltpu.SemaphoreType.DMA((3,)),
         ],
         compiler_params=params(),
         cost_estimate=pl.CostEstimate(flops=6 * rows * rows * columns, bytes_accessed=6 * 1024 * 1024, transcendentals=300000),
@@ -316,15 +325,15 @@
     )(member, misfit)
     far = lax.ppermute(far, "tile", far_pairs)
     near = lax.ppermute(near, "tile", near_pairs)
-    inner, ah, al = pl.pallas_call(
+    inner, ah, al, inc = pl.pallas_call(
         local_kernel,
-        out_shape=(field, square, square),
-        in_specs=vmem(6),
-        out_specs=tuple(vmem(3)),
+        out_shape=(field, square, square, jax.ShapeDtypeStruct(inc.shape, f32)),
+        in_specs=vmem(7),
+        out_specs=tuple(vmem(4)),
         compiler_params=params(),
         cost_estimate=pl.CostEstimate(flops=8 * rows * rows * columns, bytes_accessed=4 * 1024 * 1024, transcendentals=0),
         name="local",
-    )(w, x, own, hot, wide, mix)
+    )(w, x, own, hot, wide, mix, inc)
     grad, sums = pl.pallas_call(
         adjoint_kernel,
         out_shape=(field, pltpu.VMEM((groups, 1, columns), f32)),
@@ -335,9 +344,16 @@
     )(far, near, inner, halo, hot, ah, al, sums)
     sums = jnp.sum(lax.all_to_all(sums, "member", 0, 0), axis=0)
     sums = jnp.broadcast_to(sums[None], (tiles,) + sums.shape)
-    sums = jnp.sum(lax.all_to_all(sums, "tile", 0, 0), axis=0)
-    sums = jnp.sum(sums.reshape(2, columns // 2), axis=1) / cells
-    return inc, grad[None], sums[1], sums[0]
+    one = jax.ShapeDtypeStruct((1, 1), f32)
+    square_mean, cost = pl.pallas_call(
+        functools.partial(finish_kernel, cells),
+        out_shape=(one, one),
+        in_specs=vmem(1),
+        out_specs=tuple(vmem(2)),
+        compiler_params=params(),
+        name="finish",
+    )(lax.all_to_all(sums, "tile", 0, 0))
+    return inc, grad[None], cost.reshape(()), square_mean.reshape(())
 
 
 def solution(mesh):

time: 97.5 us -> 97.2 us (level)
  local copies, waits for them, and re-layouts: 2.64 us -> 1.38 us
    pallas_call x1 -> x2, Pallas kernels: 1.21 us -> 2.36 us  [the longest x1 1.74 us: per_device(): pl.pallas_call(local_kernel, out_shape=(field, square, square, jax.ShapeD...]
where the time goes in v5:
time: 97.2 us; the launch traced here: 96.8 us
  blocking collectives  49.5 us (51%)
  starting transfers between devices  21.5 us (22%)
  waiting for transfers between devices  14.5 us (15%)
  Pallas kernels  9.18 us (9%)
  local copies, waits for them, and re-layouts  1.38 us (1%)
    all_to_all x1, blocking collectives, per_device(): got = lax.all_to_all(both, 'member', 0, 0, axis_index_groups=chips)  19 us
    ppermute x2, starting transfers between devices, per_device(): far = lax.ppermute(far, 'tile', far_pairs)  11.4 us
    all_to_all x1, blocking collectives, per_device(): lax.all_to_all(misfit_share, 'member', 0, 0, axis_index_groups=chips)  11.3 us
    all_to_all x1, blocking collectives, per_device(): sums = jnp.sum(lax.all_to_all(sums, 'member', 0, 0), axis=0)  10.6 us
    all_to_all x1, waiting for transfers between devices, per_device(): lax.all_to_all(sums, 'tile', 0, 0)  7.68 us
    all_to_all x1, starting transfers between devices, per_device(): lax.all_to_all(sums, 'tile', 0, 0)  6.19 us
    all_gather x1, blocking collectives, per_device(): misfit = lax.all_gather(misfit_mine, 'member', axis_index_groups=cores)  4.56 us
    ppermute x2, waiting for transfers between devices, per_device(): far = lax.ppermute(far, 'tile', far_pairs)  4.33 us
  transfers between devices with their start and end apart: 5, of which 3 were waited for; matrix products, arithmetic and copies ran while one was open for 1% of the time, Pallas kernels for 5%

profile of v5, /device:TPU:1, one launch (start us, length us, event | category | flops | bytes accessed | tf_op | source)
XLA Modules:
  0.0 96.8 jit_solution(11280950556517594382)
XLA Ops:
  0.6 0.0 copy-start
  0.6 1.2 %pack_control.1 = (f32[48,8,128]{2,1,0:T(8,128)S(1)}, f32[48,8,128]{2,1,0:T(8,128)S(1)}, f32[96,8,128]{2,1,0:T(8,128)S(1)}) custom-call(f32[96,8,128]{2,1,0:T(8,128)} %bitcast.12), custom_call_target="tpu_custom_call" | custom-call | tf_op jit(solution)/shard_map/pack_control/pallas_call | solution.py:270
  1.9 8.1 %collective-permute-start = (f32[48,8,128]{2,1,0:T(8,128)S(1)}, f32[48,8,128]{2,1,0:T(8,128)S(1)}, u32[]{:S(2)}, u32[]{:S(2)}) collective-permute-start(f32[48,8,128]{2,1,0:T(8,128)S(1)} %get-tuple-element.34), channel_id=1, source_target_pairs={{0,31},{1,2},{2,1},{3,4},{4,3},{5,6},{6,5},{7,8},{8,7},{9,10},{10,... | collective-permute-start | bytes 589832 | tf_op jit(solution)/shard_map/ppermute | solution.py:279
  10.0 1.9 %collective-permute-start.1 = (f32[48,8,128]{2,1,0:T(8,128)S(1)}, f32[48,8,128]{2,1,0:T(8,128)S(1)}, u32[]{:S(2)}, u32[]{:S(2)}) collective-permute-start(f32[48,8,128]{2,1,0:T(8,128)S(1)} %get-tuple-element.35), channel_id=1, source_target_pairs={{0,1},{1,0},{2,3},{3,2},{4,5},{5,4},{6,7},{7,6},{8,9},{9,8},{10,11... | collective-permute-start | bytes 589832 | tf_op jit(solution)/shard_map/ppermute | solution.py:280
  11.9 2.9 %operators.1 = (bf16[768,768]{1,0:T(8,128)(2,1)S(1)}, bf16[768,768]{1,0:T(8,128)(2,1)S(1)}, f32[96,768]{1,0:T(8,128)S(1)}, f32[8,768]{1,0:T(8,128)S(1)}, bf16[51...) custom-call(s32[96]{0:T(128)} %classes_hbm.1, ...), custom_call_target="tpu_custom_call" | custom-call | flops 452984832 | bytes 6291456 | tf_op jit(solution)/shard_map/operators/pallas_call | solution.py:281
  14.8 0.0 collective-permute-done.far_ref
  14.9 2.5 %collective-permute-done.1.near_ref = f32[48,8,128]{2,1,0:T(8,128)S(1)} collective-permute-done((f32[48,8,128]{2,1,0:T(8,128)S(1)}, f32[48,8,128]{2,1,0:T(8,128)S(1)}, u32[]{:S(2)}, u32[]{:S(2)}) %collective-permute-start.1) | collective-permute-done | bytes 196640 | tf_op jit(solution)/shard_map/ppermute | solution.py:280
  17.3 0.0 copy-done
  17.3 1.2 %forward.1 = (f32[8,6,8,128]{3,2,1,0:T(8,128)S(1)}, f32[8,6,8,128]{3,2,1,0:T(8,128)S(1)}) custom-call(f32[48,8,128]{2,1,0:T(8,128)S(1)} %collective-permute-done.far_ref, f32[48,8,128]{2,1,0:T(8,128)S(1)} %collective-permute-done.1.near_ref, f32[768,128]{1,0:T(8,128)S(1)} %get-tuple-element.37.y_ref, bf16[768,768]{1,0:T(8,128)(2,1)S(1)} %get-tuple-element.38.fh_ref, ...), custom_call_target="tpu_custom_call" | custom-call | tf_op jit(solution)/shard_map/forward/pallas_call | solution.py:297
  18.6 4.0 %all-gather = f32[16,6,8,128]{3,2,1,0:T(8,128)S(1)} all-gather(f32[8,6,8,128]{3,2,1,0:T(8,128)S(1)} %get-tuple-element.43), channel_id=2, replica_groups={{0,32},{64,96},{128,160},{192,224},{256,288},{320,352},{384,416},{448,4..., dimensions={0}, use_global_device_ids=true | all-gather | bytes 589824 | tf_op jit(solution)/shard_map/all_gather | solution.py:305
  22.6 0.0 copy-start.1
  22.6 19.0 %all_to_all.20.got_ref = f32[8,6,8,128]{3,2,1,0:T(8,128)S(1)} all-to-all(f32[8,6,8,128]{3,2,1,0:T(8,128)S(1)} %add_cores.1), channel_id=1, replica_groups={{0,64,128,192,256,320,384,448},{32,96,160,224,288,352,416,480},{1,65,12..., dimensions={0} | all-to-all | bytes 393216 | tf_op jit(solution)/shard_map/all_to_all | solution.py:307
  41.6 11.3 %all_to_all.21 = f32[8,6,8,128]{3,2,1,0:T(8,128)S(1)} all-to-all(f32[8,6,8,128]{3,2,1,0:T(8,128)S(1)} %get-tuple-element.47), channel_id=1, replica_groups={{0,64,128,192,256,320,384,448},{32,96,160,224,288,352,416,480},{1,65,12..., dimensions={0} | all-to-all | bytes 393216 | tf_op jit(solution)/shard_map/all_to_all | solution.py:316
  52.9 4.6 %all-gather.1 = f32[16,6,8,128]{3,2,1,0:T(8,128)S(1)} all-gather(f32[8,6,8,128]{3,2,1,0:T(8,128)S(1)} %all_to_all.21), channel_id=3, replica_groups={{0,32},{64,96},{128,160},{192,224},{256,288},{320,352},{384,416},{448,4..., dimensions={0}, use_global_device_ids=true | all-gather | bytes 589824 | tf_op jit(solution)/shard_map/all_gather | solution.py:317
  57.5 0.1 weighted.1
  57.6 3.3 %collective-permute-start.2 = (f32[48,8,128]{2,1,0:T(8,128)S(1)}, f32[48,8,128]{2,1,0:T(8,128)S(1)}, u32[]{:S(2)}, u32[]{:S(2)}) collective-permute-start(f32[48,8,128]{2,1,0:T(8,128)S(1)} %get-tuple-element.54), channel_id=1, source_target_pairs={{0,31},{1,2},{2,1},{3,4},{4,3},{5,6},{6,5},{7,8},{8,7},{9,10},{10,... | collective-permute-start | bytes 589832 | tf_op jit(solution)/shard_map/ppermute | solution.py:326
  60.9 1.9 %collective-permute-start.3 = (f32[48,8,128]{2,1,0:T(8,128)S(1)}, f32[48,8,128]{2,1,0:T(8,128)S(1)}, u32[]{:S(2)}, u32[]{:S(2)}) collective-permute-start(f32[48,8,128]{2,1,0:T(8,128)S(1)} %get-tuple-element.55), channel_id=1, source_target_pairs={{0,1},{1,0},{2,3},{3,2},{4,5},{5,4},{6,7},{7,6},{8,9},{9,8},{10,11... | collective-permute-start | bytes 589832 | tf_op jit(solution)/shard_map/ppermute | solution.py:327
  62.9 0.0 copy-done.1
  62.9 1.7 %local.1 = (f32[96,8,128]{2,1,0:T(8,128)S(1)}, bf16[768,768]{1,0:T(8,128)(2,1)S(1)}, bf16[768,768]{1,0:T(8,128)(2,1)S(1)}, f32[6,8,128]{2,1,0:T(8,128)}) custom-call(f32[96,8,128]{2,1,0:T(8,128)S(1)} %get-tuple-element.48.w_ref, f32[96,8,128]{2,1,0:T(8,128)S(1)} %bitcast.13, bf16[512,256]{1,0:T(8,128)(2,1)S(1)} %get-tuple-element.49.own_ref, ...), custom_call_target="tpu_custom_call" | custom-call | flops 603979776 | bytes 4194304 | tf_op jit(solution)/shard_map/local/pallas_call | solution.py:328
  64.6 4.3 %collective-permute-done.2.far_ref = f32[48,8,128]{2,1,0:T(8,128)S(1)} collective-permute-done((f32[48,8,128]{2,1,0:T(8,128)S(1)}, f32[48,8,128]{2,1,0:T(8,128)S(1)}, u32[]{:S(2)}, u32[]{:S(2)}) %collective-permute-start.2) | collective-permute-done | bytes 196640 | tf_op jit(solution)/shard_map/ppermute | solution.py:326
  68.9 0.0 collective-permute-done.3.near_ref
  68.9 1.3 %adjoint.1 = (f32[96,8,128]{2,1,0:T(8,128)S(1)}, f32[16,1,128]{2,1,0:T(1,128)S(1)}) custom-call(f32[48,8,128]{2,1,0:T(8,128)S(1)} %collective-permute-done.2.far_ref, f32[48,8,128]{2,1,0:T(8,128)S(1)} %collective-permute-done.3.near_ref, f32[96,8,128]{2,1,0:T(8,128)S(1)} %get-tuple-element.56.part_ref, bf16[512,256]{1,0:T(8,128)(2,1)S(1)} %get-tuple-element.40.halo_ref, ...), custom_call_target="tpu_custom_call" | custom-call | tf_op jit(solution)/shard_map/adjoint/pallas_call | solution.py:337
  70.2 10.6 %all_to_all.22 = f32[16,1,128]{2,1,0:T(1,128)S(1)} all-to-all(f32[16,1,128]{2,1,0:T(1,128)S(1)} %get-tuple-element.61), channel_id=1, replica_groups=mesh['member'=16,'tile'=32] {'member'}, dimensions={0} | all-to-all | bytes 16384 | tf_op jit(solution)/shard_map/all_to_all | solution.py:345
  80.9 0.6 broadcast_in_dim.10
  81.5 6.2 %all-to-all-start.3 = ((f32[32,1,128]{2,1,0:T(1,128)}), f32[32,1,128]{2,1,0:T(1,128)S(1)}, u32[]{:S(2)}, u32[]{:S(2)}) async-start(f32[32,1,128]{2,1,0:T(1,128)} %broadcast_in_dim.10), calls=%async_computation.3 | async-start | bytes 32768 | tf_op jit(solution)/shard_map/all_to_all | solution.py:355
  87.7 0.7 copy.9
  88.5 7.7 %all-to-all-done.3.got_ref = f32[32,1,128]{2,1,0:T(1,128)S(1)} async-done(((f32[32,1,128]{2,1,0:T(1,128)}), f32[32,1,128]{2,1,0:T(1,128)S(1)}, u32[]{:S(2)}, u32[]{:S(2)}) %all-to-all-start.3) | async-done | bytes 16416 | tf_op jit(solution)/shard_map/all_to_all | solution.py:355
  96.1 0.6 finish.1
  (3 shorter events, 0.1 us)
Async XLA Ops:
  0.6 16.7 %copy-start = (bf16[1,96,8,128]{3,2,1,0:T(8,128)(2,1)S(1)}, bf16[1,96,8,128]{3,2,1,0:T(8,128)(2,1)}, u32[]{:S(2)}) copy-start(bf16[1,96,8,128]{3,2,1,0:T(8,128)(2,1)} %param.6) | copy-start | bytes 589828
  1.9 13.0 %collective-permute-start = (f32[48,8,128]{2,1,0:T(8,128)S(1)}, f32[48,8,128]{2,1,0:T(8,128)S(1)}, u32[]{:S(2)}, u32[]{:S(2)}) collective-permute-start(f32[48,8,128]{2,1,0:T(8,128)S(1)} %get-tuple-element.34), channel_id=1, source_target_pairs={{0,31},{1,2},{2,1},{3,4},{4,3},{5,6},{6,5},{7,8},{8,7},{9,10},{10,... | collective-permute-start | bytes 589832 | tf_op jit(solution)/shard_map/ppermute | solution.py:279
  10.0 7.3 %collective-permute-start.1 = (f32[48,8,128]{2,1,0:T(8,128)S(1)}, f32[48,8,128]{2,1,0:T(8,128)S(1)}, u32[]{:S(2)}, u32[]{:S(2)}) collective-permute-start(f32[48,8,128]{2,1,0:T(8,128)S(1)} %get-tuple-element.35), channel_id=1, source_target_pairs={{0,1},{1,0},{2,3},{3,2},{4,5},{5,4},{6,7},{7,6},{8,9},{9,8},{10,11... | collective-permute-start | bytes 589832 | tf_op jit(solution)/shard_map/ppermute | solution.py:280
  22.6 40.3 %copy-start.1 = (f32[1,96,8,128]{3,2,1,0:T(8,128)S(1)}, f32[1,96,8,128]{3,2,1,0:T(8,128)}, u32[]{:S(2)}) copy-start(f32[1,96,8,128]{3,2,1,0:T(8,128)} %param.5) | copy-start | bytes 1179652
  57.6 11.3 %collective-permute-start.2 = (f32[48,8,128]{2,1,0:T(8,128)S(1)}, f32[48,8,128]{2,1,0:T(8,128)S(1)}, u32[]{:S(2)}, u32[]{:S(2)}) collective-permute-start(f32[48,8,128]{2,1,0:T(8,128)S(1)} %get-tuple-element.54), channel_id=1, source_target_pairs={{0,31},{1,2},{2,1},{3,4},{4,3},{5,6},{6,5},{7,8},{8,7},{9,10},{10,... | collective-permute-start | bytes 589832 | tf_op jit(solution)/shard_map/ppermute | solution.py:326
  60.9 8.0 %collective-permute-start.3 = (f32[48,8,128]{2,1,0:T(8,128)S(1)}, f32[48,8,128]{2,1,0:T(8,128)S(1)}, u32[]{:S(2)}, u32[]{:S(2)}) collective-permute-start(f32[48,8,128]{2,1,0:T(8,128)S(1)} %get-tuple-element.55), channel_id=1, source_target_pairs={{0,1},{1,0},{2,3},{3,2},{4,5},{5,4},{6,7},{7,6},{8,9},{9,8},{10,11... | collective-permute-start | bytes 589832 | tf_op jit(solution)/shard_map/ppermute | solution.py:327
  81.5 14.6 %all-to-all-start.3 = ((f32[32,1,128]{2,1,0:T(1,128)}), f32[32,1,128]{2,1,0:T(1,128)S(1)}, u32[]{:S(2)}, u32[]{:S(2)}) async-start(f32[32,1,128]{2,1,0:T(1,128)} %broadcast_in_dim.10), calls=%async_computation.3 | async-start | bytes 32768 | tf_op jit(solution)/shard_map/all_to_all | solution.py:355

commit v6 on v5

--- a/solution.py
+++ b/solution.py
@@ -209,10 +209,9 @@
     pack_halves(w[:half_levels], w[half_levels:], near_ref, far_ref, slice(None))
 
 
-def local_kernel(w_ref, x_ref, own_ref, hot_ref, wide_ref, mix_ref, inc_ref, out_ref, ah_ref, al_ref, inc_out):
+def local_kernel(w_ref, x_ref, own_ref, hot_ref, wide_ref, mix_ref, out_ref, ah_ref, al_ref):
     levels, lat, columns = w_ref.shape
     rows = levels * lat
-    inc_out[...] = inc_ref[...]
     mix = mix_ref[...]
     for pair in range(levels // 2):
         both = [wide_ref[pl.ds(level, 1), :] * mix for level in (2 * pair, 2 * pair + 1)]
@@ -237,11 +236,23 @@
     sums_ref[...] = jnp.broadcast_to(row[None], sums_ref.shape)
 
 
-def finish_kernel(cells, got_ref, square_ref, cost_ref):
+def finish_kernel(cells, got_ref, grad_ref, inc_ref, square_hbm, cost_hbm, grad_hbm, inc_hbm, square_ref, cost_ref, sems):
+    copies = [
+        pltpu.make_async_copy(grad_ref, grad_hbm, sems.at[0]),
+        pltpu.make_async_copy(square_ref, square_hbm, sems.at[1]),
+        pltpu.make_async_copy(cost_ref, cost_hbm, sems.at[2]),
+        pltpu.make_async_copy(inc_ref, inc_hbm, sems.at[3]),
+    ]
+    copies[0].start()
+    copies[3].start()
     row = jnp.sum(got_ref[...], axis=0)
     low = lane_is_low(row.shape, row.shape[1] // 2)
     square_ref[...] = jnp.sum(jnp.where(low, row, 0.0), axis=1, keepdims=True) / cells
     cost_ref[...] = jnp.sum(jnp.where(low, 0.0, row), axis=1, keepdims=True) / cells
+    copies[1].start()
+    copies[2].start()
+    for copy in copies:
+        copy.wait()
 
 
 def per_device(tiles, control, members, obs_weight, innovation, scale_index):
@@ -325,15 +336,15 @@
     )(member, misfit)
     far = lax.ppermute(far, "tile", far_pairs)
     near = lax.ppermute(near, "tile", near_pairs)
-    inner, ah, al, inc = pl.pallas_call(
+    inner, ah, al = pl.pallas_call(
         local_kernel,
-        out_shape=(field, square, square, jax.ShapeDtypeStruct(inc.shape, f32)),
-        in_specs=vmem(7),
-        out_specs=tuple(vmem(4)),
+        out_shape=(field, square, square),
+        in_specs=vmem(6),
+        out_specs=tuple(vmem(3)),
         compiler_params=params(),
         cost_estimate=pl.CostEstimate(flops=8 * rows * rows * columns, bytes_accessed=4 * 1024 * 1024, transcendentals=0),
         name="local",
-    )(w, x, own, hot, wide, mix, inc)
+    )(w, x, own, hot, wide, mix)
     grad, sums = pl.pallas_call(
         adjoint_kernel,
         out_shape=(field, pltpu.VMEM((groups, 1, columns), f32)),
@@ -344,15 +355,16 @@
     )(far, near, inner, halo, hot, ah, al, sums)
     sums = jnp.sum(lax.all_to_all(sums, "member", 0, 0), axis=0)
     sums = jnp.broadcast_to(sums[None], (tiles,) + sums.shape)
-    one = jax.ShapeDtypeStruct((1, 1), f32)
-    square_mean, cost = pl.pallas_call(
+    one = pltpu.HBM((1, 1), f32)
+    square_mean, cost, grad, inc = pl.pallas_call(
         functools.partial(finish_kernel, cells),
-        out_shape=(one, one),
-        in_specs=vmem(1),
-        out_specs=tuple(vmem(2)),
+        out_shape=(one, one, pltpu.HBM(grad.shape, f32), pltpu.HBM(inc.shape, f32)),
+        in_specs=vmem(3),
+        out_specs=tuple(hbm * 4),
+        scratch_shapes=[pltpu.VMEM((1, 1), f32), pltpu.VMEM((1, 1), f32), pltpu.SemaphoreType.DMA((4,))],
         compiler_params=params(),
         name="finish",
-    )(lax.all_to_all(sums, "tile", 0, 0))
+    )(lax.all_to_all(sums, "tile", 0, 0), grad, inc)
     return inc, grad[None], cost.reshape(()), square_mean.reshape(())
 
 

time: 97.2 us -> 96.8 us (level)
  blocking collectives: 49.5 us -> 64.1 us
  waiting for transfers between devices: 14.5 us -> 7.3 us
  starting transfers between devices: 21.5 us -> 15.3 us
  local copies, waits for them, and re-layouts: 1.38 us -> 0.02 us
    all_to_all x0 -> x1, blocking collectives: none -> 14.6 us  [per_device(): lax.all_to_all(sums, 'tile', 0, 0)]
    all_to_all x1 -> x0, waiting for transfers between devices: 7.68 us -> none  [per_device(): lax.all_to_all(sums, 'tile', 0, 0)]
    all_to_all x1 -> x0, starting transfers between devices: 6.19 us -> none  [per_device(): lax.all_to_all(sums, 'tile', 0, 0)]
  transfers between devices with their start and end apart: 5 -> 4, of which waited for: 3 -> 2; matrix products, arithmetic and copies ran while one was open for 1% -> 0% of each run, Pallas kernels for 5% -> 4%
where the time goes in v6:
time: 96.8 us; the launch traced here: 96.3 us
  blocking collectives  64.1 us (66%)
  starting transfers between devices  15.3 us (16%)
  Pallas kernels  8.88 us (9%)
  waiting for transfers between devices  7.3 us (8%)
    all_to_all x1, blocking collectives, per_device(): got = lax.all_to_all(both, 'member', 0, 0, axis_index_groups=chips)  19 us
    all_to_all x1, blocking collectives, per_device(): lax.all_to_all(sums, 'tile', 0, 0)  14.6 us
    ppermute x2, starting transfers between devices, per_device(): far = lax.ppermute(far, 'tile', far_pairs)  11.4 us
    all_to_all x1, blocking collectives, per_device(): lax.all_to_all(misfit_share, 'member', 0, 0, axis_index_groups=chips)  11.3 us
    all_to_all x1, blocking collectives, per_device(): sums = jnp.sum(lax.all_to_all(sums, 'member', 0, 0), axis=0)  10.6 us
    ppermute x2, waiting for transfers between devices, per_device(): far = lax.ppermute(far, 'tile', far_pairs)  4.85 us
    all_gather x1, blocking collectives, per_device(): misfit = lax.all_gather(misfit_mine, 'member', axis_index_groups=cores)  4.56 us
    all_gather x1, blocking collectives, per_device(): sent = lax.all_gather(other, 'member', axis_index_groups=cores)  4.01 us
  transfers between devices with their start and end apart: 4, of which 2 were waited for; matrix products, arithmetic and copies ran while one was open for 0% of the time, Pallas kernels for 4%

profile of v6, /device:TPU:1, one launch (start us, length us, event | category | flops | bytes accessed | tf_op | source)
XLA Modules:
  0.0 96.3 jit_solution(1417246399742354165)
XLA Ops:
  0.6 0.0 copy-start
  0.6 1.2 %pack_control.1 = (f32[48,8,128]{2,1,0:T(8,128)S(1)}, f32[48,8,128]{2,1,0:T(8,128)S(1)}, f32[96,8,128]{2,1,0:T(8,128)S(1)}) custom-call(f32[96,8,128]{2,1,0:T(8,128)} %bitcast.11), custom_call_target="tpu_custom_call" | custom-call | tf_op jit(solution)/shard_map/pack_control/pallas_call | solution.py:281
  1.9 8.1 %collective-permute-start = (f32[48,8,128]{2,1,0:T(8,128)S(1)}, f32[48,8,128]{2,1,0:T(8,128)S(1)}, u32[]{:S(2)}, u32[]{:S(2)}) collective-permute-start(f32[48,8,128]{2,1,0:T(8,128)S(1)} %get-tuple-element.35), channel_id=1, source_target_pairs={{0,31},{1,2},{2,1},{3,4},{4,3},{5,6},{6,5},{7,8},{8,7},{9,10},{10,... | collective-permute-start | bytes 589832 | tf_op jit(solution)/shard_map/ppermute | solution.py:290
  10.0 1.9 %collective-permute-start.1 = (f32[48,8,128]{2,1,0:T(8,128)S(1)}, f32[48,8,128]{2,1,0:T(8,128)S(1)}, u32[]{:S(2)}, u32[]{:S(2)}) collective-permute-start(f32[48,8,128]{2,1,0:T(8,128)S(1)} %get-tuple-element.36), channel_id=1, source_target_pairs={{0,1},{1,0},{2,3},{3,2},{4,5},{5,4},{6,7},{7,6},{8,9},{9,8},{10,11... | collective-permute-start | bytes 589832 | tf_op jit(solution)/shard_map/ppermute | solution.py:291
  11.9 2.9 %operators.1 = (bf16[768,768]{1,0:T(8,128)(2,1)S(1)}, bf16[768,768]{1,0:T(8,128)(2,1)S(1)}, f32[96,768]{1,0:T(8,128)S(1)}, f32[8,768]{1,0:T(8,128)S(1)}, bf16[51...) custom-call(s32[96]{0:T(128)} %classes_hbm.1, ...), custom_call_target="tpu_custom_call" | custom-call | flops 452984832 | bytes 6291456 | tf_op jit(solution)/shard_map/operators/pallas_call | solution.py:292
  14.9 0.0 collective-permute-done.far_ref
  14.9 2.4 %collective-permute-done.1.near_ref = f32[48,8,128]{2,1,0:T(8,128)S(1)} collective-permute-done((f32[48,8,128]{2,1,0:T(8,128)S(1)}, f32[48,8,128]{2,1,0:T(8,128)S(1)}, u32[]{:S(2)}, u32[]{:S(2)}) %collective-permute-start.1) | collective-permute-done | bytes 196640 | tf_op jit(solution)/shard_map/ppermute | solution.py:291
  17.3 0.0 copy-done
  17.3 1.2 %forward.1 = (f32[8,6,8,128]{3,2,1,0:T(8,128)S(1)}, f32[8,6,8,128]{3,2,1,0:T(8,128)S(1)}) custom-call(f32[48,8,128]{2,1,0:T(8,128)S(1)} %collective-permute-done.far_ref, f32[48,8,128]{2,1,0:T(8,128)S(1)} %collective-permute-done.1.near_ref, f32[768,128]{1,0:T(8,128)S(1)} %get-tuple-element.38.y_ref, bf16[768,768]{1,0:T(8,128)(2,1)S(1)} %get-tuple-element.39.fh_ref, ...), custom_call_target="tpu_custom_call" | custom-call | tf_op jit(solution)/shard_map/forward/pallas_call | solution.py:308
  18.6 4.0 %all-gather = f32[16,6,8,128]{3,2,1,0:T(8,128)S(1)} all-gather(f32[8,6,8,128]{3,2,1,0:T(8,128)S(1)} %get-tuple-element.44), channel_id=2, replica_groups={{0,32},{64,96},{128,160},{192,224},{256,288},{320,352},{384,416},{448,4..., dimensions={0}, use_global_device_ids=true | all-gather | bytes 589824 | tf_op jit(solution)/shard_map/all_gather | solution.py:316
  22.6 0.0 copy-start.1
  22.6 19.0 %all_to_all.20.got_ref = f32[8,6,8,128]{3,2,1,0:T(8,128)S(1)} all-to-all(f32[8,6,8,128]{3,2,1,0:T(8,128)S(1)} %add_cores.1), channel_id=1, replica_groups={{0,64,128,192,256,320,384,448},{32,96,160,224,288,352,416,480},{1,65,12..., dimensions={0} | all-to-all | bytes 393216 | tf_op jit(solution)/shard_map/all_to_all | solution.py:318
  41.6 11.3 %all_to_all.21 = f32[8,6,8,128]{3,2,1,0:T(8,128)S(1)} all-to-all(f32[8,6,8,128]{3,2,1,0:T(8,128)S(1)} %get-tuple-element.48), channel_id=1, replica_groups={{0,64,128,192,256,320,384,448},{32,96,160,224,288,352,416,480},{1,65,12..., dimensions={0} | all-to-all | bytes 393216 | tf_op jit(solution)/shard_map/all_to_all | solution.py:327
  52.9 4.6 %all-gather.1 = f32[16,6,8,128]{3,2,1,0:T(8,128)S(1)} all-gather(f32[8,6,8,128]{3,2,1,0:T(8,128)S(1)} %all_to_all.21), channel_id=3, replica_groups={{0,32},{64,96},{128,160},{192,224},{256,288},{320,352},{384,416},{448,4..., dimensions={0}, use_global_device_ids=true | all-gather | bytes 589824 | tf_op jit(solution)/shard_map/all_gather | solution.py:328
  57.5 0.1 weighted.1
  57.6 3.3 %collective-permute-start.2 = (f32[48,8,128]{2,1,0:T(8,128)S(1)}, f32[48,8,128]{2,1,0:T(8,128)S(1)}, u32[]{:S(2)}, u32[]{:S(2)}) collective-permute-start(f32[48,8,128]{2,1,0:T(8,128)S(1)} %get-tuple-element.49), channel_id=1, source_target_pairs={{0,31},{1,2},{2,1},{3,4},{4,3},{5,6},{6,5},{7,8},{8,7},{9,10},{10,... | collective-permute-start | bytes 589832 | tf_op jit(solution)/shard_map/ppermute | solution.py:337
  61.0 1.9 %collective-permute-start.3 = (f32[48,8,128]{2,1,0:T(8,128)S(1)}, f32[48,8,128]{2,1,0:T(8,128)S(1)}, u32[]{:S(2)}, u32[]{:S(2)}) collective-permute-start(f32[48,8,128]{2,1,0:T(8,128)S(1)} %get-tuple-element.50), channel_id=1, source_target_pairs={{0,1},{1,0},{2,3},{3,2},{4,5},{5,4},{6,7},{7,6},{8,9},{9,8},{10,11... | collective-permute-start | bytes 589832 | tf_op jit(solution)/shard_map/ppermute | solution.py:338
  62.9 0.0 copy-done.1
  62.9 1.2 %local.1 = (f32[96,8,128]{2,1,0:T(8,128)S(1)}, bf16[768,768]{1,0:T(8,128)(2,1)S(1)}, bf16[768,768]{1,0:T(8,128)(2,1)S(1)}) custom-call(f32[96,8,128]{2,1,0:T(8,128)S(1)} %get-tuple-element.51.w_ref, f32[96,8,128]{2,1,0:T(8,128)S(1)} %bitcast.12, bf16[512,256]{1,0:T(8,128)(2,1)S(1)} %get-tuple-element.52.own_ref, ...), custom_call_target="tpu_custom_call" | custom-call | flops 603979776 | bytes 4194304 | tf_op jit(solution)/shard_map/local/pallas_call | solution.py:339
  64.1 4.8 %collective-permute-done.2.far_ref = f32[48,8,128]{2,1,0:T(8,128)S(1)} collective-permute-done((f32[48,8,128]{2,1,0:T(8,128)S(1)}, f32[48,8,128]{2,1,0:T(8,128)S(1)}, u32[]{:S(2)}, u32[]{:S(2)}) %collective-permute-start.2) | collective-permute-done | bytes 196640 | tf_op jit(solution)/shard_map/ppermute | solution.py:337
  69.0 0.0 collective-permute-done.3.near_ref
  69.0 1.3 %adjoint.1 = (f32[96,8,128]{2,1,0:T(8,128)S(1)}, f32[16,1,128]{2,1,0:T(1,128)S(1)}) custom-call(f32[48,8,128]{2,1,0:T(8,128)S(1)} %collective-permute-done.2.far_ref, f32[48,8,128]{2,1,0:T(8,128)S(1)} %collective-permute-done.3.near_ref, f32[96,8,128]{2,1,0:T(8,128)S(1)} %get-tuple-element.55.part_ref, bf16[512,256]{1,0:T(8,128)(2,1)S(1)} %get-tuple-element.41.halo_ref, ...), custom_call_target="tpu_custom_call" | custom-call | tf_op jit(solution)/shard_map/adjoint/pallas_call | solution.py:348
  70.3 10.6 %all_to_all.22 = f32[16,1,128]{2,1,0:T(1,128)S(1)} all-to-all(f32[16,1,128]{2,1,0:T(1,128)S(1)} %get-tuple-element.59), channel_id=1, replica_groups=mesh['member'=16,'tile'=32] {'member'}, dimensions={0} | all-to-all | bytes 16384 | tf_op jit(solution)/shard_map/all_to_all | solution.py:356
  80.9 14.6 %all_to_all.23.got_ref = f32[32,1,128]{2,1,0:T(1,128)S(1)} all-to-all(f32[32,1,128]{2,1,0:T(1,128)S(1)} %broadcast_in_dim.4), channel_id=1, replica_groups=mesh['member'=16,'tile'=32] {'tile'}, dimensions={0} | all-to-all | bytes 32768 | tf_op jit(solution)/shard_map/all_to_all | solution.py:367
  95.5 0.8 finish.1
  (4 shorter events, 0.1 us)
Async XLA Ops:
  0.6 16.7 %copy-start = (bf16[1,96,8,128]{3,2,1,0:T(8,128)(2,1)S(1)}, bf16[1,96,8,128]{3,2,1,0:T(8,128)(2,1)}, u32[]{:S(2)}) copy-start(bf16[1,96,8,128]{3,2,1,0:T(8,128)(2,1)} %param.6) | copy-start | bytes 589828
  1.9 13.0 %collective-permute-start = (f32[48,8,128]{2,1,0:T(8,128)S(1)}, f32[48,8,128]{2,1,0:T(8,128)S(1)}, u32[]{:S(2)}, u32[]{:S(2)}) collective-permute-start(f32[48,8,128]{2,1,0:T(8,128)S(1)} %get-tuple-element.35), channel_id=1, source_target_pairs={{0,31},{1,2},{2,1},{3,4},{4,3},{5,6},{6,5},{7,8},{8,7},{9,10},{10,... | collective-permute-start | bytes 589832 | tf_op jit(solution)/shard_map/ppermute | solution.py:290
  10.0 7.3 %collective-permute-start.1 = (f32[48,8,128]{2,1,0:T(8,128)S(1)}, f32[48,8,128]{2,1,0:T(8,128)S(1)}, u32[]{:S(2)}, u32[]{:S(2)}) collective-permute-start(f32[48,8,128]{2,1,0:T(8,128)S(1)} %get-tuple-element.36), channel_id=1, source_target_pairs={{0,1},{1,0},{2,3},{3,2},{4,5},{5,4},{6,7},{7,6},{8,9},{9,8},{10,11... | collective-permute-start | bytes 589832 | tf_op jit(solution)/shard_map/ppermute | solution.py:291
  22.6 40.3 %copy-start.1 = (f32[1,96,8,128]{3,2,1,0:T(8,128)S(1)}, f32[1,96,8,128]{3,2,1,0:T(8,128)}, u32[]{:S(2)}) copy-start(f32[1,96,8,128]{3,2,1,0:T(8,128)} %param.5) | copy-start | bytes 1179652
  57.6 11.3 %collective-permute-start.2 = (f32[48,8,128]{2,1,0:T(8,128)S(1)}, f32[48,8,128]{2,1,0:T(8,128)S(1)}, u32[]{:S(2)}, u32[]{:S(2)}) collective-permute-start(f32[48,8,128]{2,1,0:T(8,128)S(1)} %get-tuple-element.49), channel_id=1, source_target_pairs={{0,31},{1,2},{2,1},{3,4},{4,3},{5,6},{6,5},{7,8},{8,7},{9,10},{10,... | collective-permute-start | bytes 589832 | tf_op jit(solution)/shard_map/ppermute | solution.py:337
  61.0 8.0 %collective-permute-start.3 = (f32[48,8,128]{2,1,0:T(8,128)S(1)}, f32[48,8,128]{2,1,0:T(8,128)S(1)}, u32[]{:S(2)}, u32[]{:S(2)}) collective-permute-start(f32[48,8,128]{2,1,0:T(8,128)S(1)} %get-tuple-element.50), channel_id=1, source_target_pairs={{0,1},{1,0},{2,3},{3,2},{4,5},{5,4},{6,7},{7,6},{8,9},{9,8},{10,11... | collective-permute-start | bytes 589832 | tf_op jit(solution)/shard_map/ppermute | solution.py:338

commit v7 on v6

--- a/solution.py
+++ b/solution.py
@@ -97,8 +97,9 @@
 
 
 def operators_kernel(
-    classes_hbm, x_ref, weight_hbm, innovation_hbm,
-    fh_ref, fl_ref, wide_ref, mix_ref, own_ref, halo_ref, hot_ref, y_ref, sum_ref, weight_ref, innovation_ref,
+    inverse,
+    classes_hbm, x_ref, m_ref, weight_hbm, innovation_hbm,
+    fh_ref, fl_ref, wide_ref, mix_ref, own_ref, halo_ref, hot_ref, y_ref, scaled_ref, sum_ref, weight_ref, innovation_ref,
     classes, class_ref, class_rows_ref, sems,
 ):
     levels, lat, columns = x_ref.shape
@@ -170,16 +171,18 @@
             both.append(wide_ref[pl.ds(level, 1), :] * pattern)
         at = pl.ds(2 * pair * lat, 2 * lat)
         fh_ref[at, :], fl_ref[at, :] = split(jnp.concatenate(both, axis=0))
-    y_ref[...] = class_product(left_product(fh_ref[...], fl_ref[...], x), hot_ref, own_ref[...])
+    scaled = m_ref[...].astype(f32) * inverse
+    scaled_ref[...] = scaled
+    y_ref[...] = scaled.reshape(rows, columns) * class_product(left_product(fh_ref[...], fl_ref[...], x), hot_ref, own_ref[...])
     weight_copy.wait()
     innovation_copy.wait()
 
 
-def forward_kernel(inverse, far_ref, near_ref, y_ref, fh_ref, flo_ref, halo_ref, hot_ref, m_ref, mine_ref, other_ref):
+def forward_kernel(far_ref, near_ref, y_ref, fh_ref, flo_ref, halo_ref, hot_ref, m_ref, mine_ref, other_ref):
     levels, lat, columns = m_ref.shape
     halo = left_product(fh_ref[...], flo_ref[...], unpack_halves(near_ref[...], far_ref[...]))
-    alpha = y_ref[...] + class_product(halo, hot_ref, halo_ref[...])
-    term = m_ref[...].astype(f32) * alpha.reshape(levels, lat, columns) * inverse
+    edge = class_product(halo, hot_ref, halo_ref[...])
+    term = y_ref[...].reshape(levels, lat, columns) + m_ref[...] * edge.reshape(levels, lat, columns)
     chips, share = mine_ref.shape[:2]
     term = term.reshape(chips, 2, share, lat, columns)
     even = lax.axis_index("member") % 2 == 0
@@ -200,10 +203,10 @@
     sum_ref[...] = sum_in[...] + jnp.sum(cost.reshape(-1, cost.shape[2]), axis=0, keepdims=True)
 
 
-def weight_kernel(inverse, m_ref, both_ref, w_ref, far_ref, near_ref):
+def weight_kernel(m_ref, both_ref, w_ref, far_ref, near_ref):
     levels, lat, columns = m_ref.shape
     misfit = jnp.stack([both_ref[0], both_ref[1]], axis=1)
-    w = m_ref[...].astype(f32) * misfit.reshape(levels, lat, columns) * inverse
+    w = m_ref[...] * misfit.reshape(levels, lat, columns)
     w_ref[...] = w
     half_levels = near_ref.shape[0]
     pack_halves(w[:half_levels], w[half_levels:], near_ref, far_ref, slice(None))
@@ -289,11 +292,11 @@
     )(x_hbm)
     far = lax.ppermute(far, "tile", far_pairs)
     near = lax.ppermute(near, "tile", near_pairs)
-    fh, fl, wide, mix, own, halo, hot, y, half_sum, weight_share, innovation_share = pl.pallas_call(
-        operators_kernel,
-        out_shape=(square, square, pltpu.VMEM((levels, rows), f32), pltpu.VMEM((lat, rows), f32), band, band, pltpu.VMEM((CLASSES, rows, columns), bf16), pltpu.VMEM((rows, columns), f32), line, part, part),
-        in_specs=hbm + vmem(1) + hbm * 2,
-        out_specs=tuple(vmem(11)),
+    fh, fl, wide, mix, own, halo, hot, y, scaled, half_sum, weight_share, innovation_share = pl.pallas_call(
+        functools.partial(operators_kernel, inverse),
+        out_shape=(square, square, pltpu.VMEM((levels, rows), f32), pltpu.VMEM((lat, rows), f32), band, band, pltpu.VMEM((CLASSES, rows, columns), bf16), pltpu.VMEM((rows, columns), f32), field, line, part, part),
+        in_specs=hbm + vmem(2) + hbm * 2,
+        out_specs=tuple(vmem(12)),
         scratch_shapes=[
             pltpu.SMEM((levels,), jnp.int32),
             pltpu.VMEM((levels, columns), f32),
@@ -303,16 +306,16 @@
         compiler_params=params(),
         cost_estimate=pl.CostEstimate(flops=6 * rows * rows * columns, bytes_accessed=6 * 1024 * 1024, transcendentals=300000),
         name="operators",
-    )(classes, x_near, weight_hbm, innovation_hbm)
+    )(classes, x_near, member, weight_hbm, innovation_hbm)
     half_term = pltpu.VMEM((groups // 2, share, lat, columns), f32)
     mine, other = pl.pallas_call(
-        functools.partial(forward_kernel, inverse),
+        forward_kernel,
         out_shape=(half_term, half_term),
         in_specs=vmem(8),
         out_specs=tuple(vmem(2)),
         compiler_params=params(),
         name="forward",
-    )(far, near, y, fh, fl, halo, hot, member)
+    )(far, near, y, fh, fl, halo, hot, scaled)
     sent = lax.all_gather(other, "member", axis_index_groups=cores)
     both = pl.pallas_call(add_kernel, out_shape=half_term, in_specs=vmem(2), out_specs=vmem(1)[0], compiler_params=params(), name="add_cores")(mine, sent)
     got = lax.all_to_all(both, "member", 0, 0, axis_index_groups=chips)
@@ -327,13 +330,13 @@
     misfit_mine = lax.all_to_all(misfit_share, "member", 0, 0, axis_index_groups=chips)
     misfit = lax.all_gather(misfit_mine, "member", axis_index_groups=cores)
     w, far, near = pl.pallas_call(
-        functools.partial(weight_kernel, inverse),
+        weight_kernel,
         out_shape=(field, half_pack, half_pack),
         in_specs=vmem(2),
         out_specs=tuple(vmem(3)),
         compiler_params=params(),
         name="weighted",
-    )(member, misfit)
+    )(scaled, misfit)
     far = lax.ppermute(far, "tile", far_pairs)
     near = lax.ppermute(near, "tile", near_pairs)
     inner, ah, al = pl.pallas_call(

time: 96.8 us -> 96.8 us (level)
  no operation moved by 1% of the time
where the time goes in v7:
time: 96.8 us; the launch traced here: 96.3 us
  blocking collectives  64.1 us (66%)
  starting transfers between devices  15.3 us (16%)
  Pallas kernels  8.82 us (9%)
  waiting for transfers between devices  6.38 us (7%)
    all_to_all x1, blocking collectives, per_device(): got = lax.all_to_all(both, 'member', 0, 0, axis_index_groups=chips)  19 us
    all_to_all x1, blocking collectives, per_device(): lax.all_to_all(sums, 'tile', 0, 0)  14.6 us
    ppermute x2, starting transfers between devices, per_device(): far = lax.ppermute(far, 'tile', far_pairs)  11.4 us
    all_to_all x1, blocking collectives, per_device(): lax.all_to_all(misfit_share, 'member', 0, 0, axis_index_groups=chips)  11.3 us
    all_to_all x1, blocking collectives, per_device(): sums = jnp.sum(lax.all_to_all(sums, 'member', 0, 0), axis=0)  10.6 us
    ppermute x2, waiting for transfers between devices, per_device(): far = lax.ppermute(far, 'tile', far_pairs)  4.85 us
    all_gather x1, blocking collectives, per_device(): misfit = lax.all_gather(misfit_mine, 'member', axis_index_groups=cores)  4.56 us
    all_gather x1, blocking collectives, per_device(): sent = lax.all_gather(other, 'member', axis_index_groups=cores)  4.01 us
  transfers between devices with their start and end apart: 4, of which 2 were waited for; matrix products, arithmetic and copies ran while one was open for 0% of the time, Pallas kernels for 4%

profile of v7, /device:TPU:1, one launch (start us, length us, event | category | flops | bytes accessed | tf_op | source)
XLA Modules:
  0.0 96.3 jit_solution(7684217082610543684)
XLA Ops:
  0.6 1.2 %pack_control.1 = (f32[48,8,128]{2,1,0:T(8,128)S(1)}, f32[48,8,128]{2,1,0:T(8,128)S(1)}, f32[96,8,128]{2,1,0:T(8,128)S(1)}) custom-call(f32[96,8,128]{2,1,0:T(8,128)} %bitcast.9), custom_call_target="tpu_custom_call" | custom-call | tf_op jit(solution)/shard_map/pack_control/pallas_call | solution.py:284
  1.8 8.1 %collective-permute-start = (f32[48,8,128]{2,1,0:T(8,128)S(1)}, f32[48,8,128]{2,1,0:T(8,128)S(1)}, u32[]{:S(2)}, u32[]{:S(2)}) collective-permute-start(f32[48,8,128]{2,1,0:T(8,128)S(1)} %get-tuple-element.38), channel_id=1, source_target_pairs={{0,31},{1,2},{2,1},{3,4},{4,3},{5,6},{6,5},{7,8},{8,7},{9,10},{10,... | collective-permute-start | bytes 589832 | tf_op jit(solution)/shard_map/ppermute | solution.py:293
  9.9 1.9 %collective-permute-start.1 = (f32[48,8,128]{2,1,0:T(8,128)S(1)}, f32[48,8,128]{2,1,0:T(8,128)S(1)}, u32[]{:S(2)}, u32[]{:S(2)}) collective-permute-start(f32[48,8,128]{2,1,0:T(8,128)S(1)} %get-tuple-element.39), channel_id=1, source_target_pairs={{0,1},{1,0},{2,3},{3,2},{4,5},{5,4},{6,7},{7,6},{8,9},{9,8},{10,11... | collective-permute-start | bytes 589832 | tf_op jit(solution)/shard_map/ppermute | solution.py:294
  11.9 0.0 copy-start.1
  11.9 0.9 copy-done.1
  12.8 2.9 %operators.1 = (bf16[768,768]{1,0:T(8,128)(2,1)S(1)}, bf16[768,768]{1,0:T(8,128)(2,1)S(1)}, f32[96,768]{1,0:T(8,128)S(1)}, f32[8,768]{1,0:T(8,128)S(1)}, bf16[51...) custom-call(s32[96]{0:T(128)} %classes_hbm.1, ...), custom_call_target="tpu_custom_call" | custom-call | flops 452984832 | bytes 6291456 | tf_op jit(solution)/shard_map/operators/pallas_call | solution.py:295
  15.7 0.0 collective-permute-done.far_ref
  15.7 1.5 %collective-permute-done.1.near_ref = f32[48,8,128]{2,1,0:T(8,128)S(1)} collective-permute-done((f32[48,8,128]{2,1,0:T(8,128)S(1)}, f32[48,8,128]{2,1,0:T(8,128)S(1)}, u32[]{:S(2)}, u32[]{:S(2)}) %collective-permute-start.1) | collective-permute-done | bytes 196640 | tf_op jit(solution)/shard_map/ppermute | solution.py:294
  17.3 1.2 %forward.1 = (f32[8,6,8,128]{3,2,1,0:T(8,128)S(1)}, f32[8,6,8,128]{3,2,1,0:T(8,128)S(1)}) custom-call(f32[48,8,128]{2,1,0:T(8,128)S(1)} %collective-permute-done.far_ref, f32[48,8,128]{2,1,0:T(8,128)S(1)} %collective-permute-done.1.near_ref, f32[768,128]{1,0:T(8,128)S(1)} %get-tuple-element.40.y_ref, bf16[768,768]{1,0:T(8,128)(2,1)S(1)} %get-tuple-element.41.fh_ref, ...), custom_call_target="tpu_custom_call" | custom-call | tf_op jit(solution)/shard_map/forward/pallas_call | solution.py:311
  18.5 4.0 %all-gather = f32[16,6,8,128]{3,2,1,0:T(8,128)S(1)} all-gather(f32[8,6,8,128]{3,2,1,0:T(8,128)S(1)} %get-tuple-element.46), channel_id=2, replica_groups={{0,32},{64,96},{128,160},{192,224},{256,288},{320,352},{384,416},{448,4..., dimensions={0}, use_global_device_ids=true | all-gather | bytes 589824 | tf_op jit(solution)/shard_map/all_gather | solution.py:319
  22.6 0.0 copy-start
  22.6 19.0 %all_to_all.20.got_ref = f32[8,6,8,128]{3,2,1,0:T(8,128)S(1)} all-to-all(f32[8,6,8,128]{3,2,1,0:T(8,128)S(1)} %add_cores.1), channel_id=1, replica_groups={{0,64,128,192,256,320,384,448},{32,96,160,224,288,352,416,480},{1,65,12..., dimensions={0} | all-to-all | bytes 393216 | tf_op jit(solution)/shard_map/all_to_all | solution.py:321
  41.6 11.3 %all_to_all.21 = f32[8,6,8,128]{3,2,1,0:T(8,128)S(1)} all-to-all(f32[8,6,8,128]{3,2,1,0:T(8,128)S(1)} %get-tuple-element.50), channel_id=1, replica_groups={{0,64,128,192,256,320,384,448},{32,96,160,224,288,352,416,480},{1,65,12..., dimensions={0} | all-to-all | bytes 393216 | tf_op jit(solution)/shard_map/all_to_all | solution.py:330
  52.9 4.6 %all-gather.1 = f32[16,6,8,128]{3,2,1,0:T(8,128)S(1)} all-gather(f32[8,6,8,128]{3,2,1,0:T(8,128)S(1)} %all_to_all.21), channel_id=3, replica_groups={{0,32},{64,96},{128,160},{192,224},{256,288},{320,352},{384,416},{448,4..., dimensions={0}, use_global_device_ids=true | all-gather | bytes 589824 | tf_op jit(solution)/shard_map/all_gather | solution.py:331
  57.4 0.1 weighted.1
  57.6 3.3 %collective-permute-start.2 = (f32[48,8,128]{2,1,0:T(8,128)S(1)}, f32[48,8,128]{2,1,0:T(8,128)S(1)}, u32[]{:S(2)}, u32[]{:S(2)}) collective-permute-start(f32[48,8,128]{2,1,0:T(8,128)S(1)} %get-tuple-element.51), channel_id=1, source_target_pairs={{0,31},{1,2},{2,1},{3,4},{4,3},{5,6},{6,5},{7,8},{8,7},{9,10},{10,... | collective-permute-start | bytes 589832 | tf_op jit(solution)/shard_map/ppermute | solution.py:340
  60.9 1.9 %collective-permute-start.3 = (f32[48,8,128]{2,1,0:T(8,128)S(1)}, f32[48,8,128]{2,1,0:T(8,128)S(1)}, u32[]{:S(2)}, u32[]{:S(2)}) collective-permute-start(f32[48,8,128]{2,1,0:T(8,128)S(1)} %get-tuple-element.52), channel_id=1, source_target_pairs={{0,1},{1,0},{2,3},{3,2},{4,5},{5,4},{6,7},{7,6},{8,9},{9,8},{10,11... | collective-permute-start | bytes 589832 | tf_op jit(solution)/shard_map/ppermute | solution.py:341
  62.8 0.0 copy-done
  62.8 1.2 %local.1 = (f32[96,8,128]{2,1,0:T(8,128)S(1)}, bf16[768,768]{1,0:T(8,128)(2,1)S(1)}, bf16[768,768]{1,0:T(8,128)(2,1)S(1)}) custom-call(f32[96,8,128]{2,1,0:T(8,128)S(1)} %get-tuple-element.53.w_ref, f32[96,8,128]{2,1,0:T(8,128)S(1)} %bitcast.10, bf16[512,256]{1,0:T(8,128)(2,1)S(1)} %get-tuple-element.54.own_ref, ...), custom_call_target="tpu_custom_call" | custom-call | flops 603979776 | bytes 4194304 | tf_op jit(solution)/shard_map/local/pallas_call | solution.py:342
  64.1 4.8 %collective-permute-done.2.far_ref = f32[48,8,128]{2,1,0:T(8,128)S(1)} collective-permute-done((f32[48,8,128]{2,1,0:T(8,128)S(1)}, f32[48,8,128]{2,1,0:T(8,128)S(1)}, u32[]{:S(2)}, u32[]{:S(2)}) %collective-permute-start.2) | collective-permute-done | bytes 196640 | tf_op jit(solution)/shard_map/ppermute | solution.py:340
  68.9 0.0 collective-permute-done.3.near_ref
  68.9 1.3 %adjoint.1 = (f32[96,8,128]{2,1,0:T(8,128)S(1)}, f32[16,1,128]{2,1,0:T(1,128)S(1)}) custom-call(f32[48,8,128]{2,1,0:T(8,128)S(1)} %collective-permute-done.2.far_ref, f32[48,8,128]{2,1,0:T(8,128)S(1)} %collective-permute-done.3.near_ref, f32[96,8,128]{2,1,0:T(8,128)S(1)} %get-tuple-element.57.part_ref, bf16[512,256]{1,0:T(8,128)(2,1)S(1)} %get-tuple-element.43.halo_ref, ...), custom_call_target="tpu_custom_call" | custom-call | tf_op jit(solution)/shard_map/adjoint/pallas_call | solution.py:351
  70.2 10.6 %all_to_all.22 = f32[16,1,128]{2,1,0:T(1,128)S(1)} all-to-all(f32[16,1,128]{2,1,0:T(1,128)S(1)} %get-tuple-element.61), channel_id=1, replica_groups=mesh['member'=16,'tile'=32] {'member'}, dimensions={0} | all-to-all | bytes 16384 | tf_op jit(solution)/shard_map/all_to_all | solution.py:359
  80.9 14.6 %all_to_all.23.got_ref = f32[32,1,128]{2,1,0:T(1,128)S(1)} all-to-all(f32[32,1,128]{2,1,0:T(1,128)S(1)} %broadcast_in_dim.4), channel_id=1, replica_groups=mesh['member'=16,'tile'=32] {'tile'}, dimensions={0} | all-to-all | bytes 32768 | tf_op jit(solution)/shard_map/all_to_all | solution.py:370
  95.5 0.8 finish.1
  (4 shorter events, 0.1 us)
Async XLA Ops:
  1.8 13.9 %collective-permute-start = (f32[48,8,128]{2,1,0:T(8,128)S(1)}, f32[48,8,128]{2,1,0:T(8,128)S(1)}, u32[]{:S(2)}, u32[]{:S(2)}) collective-permute-start(f32[48,8,128]{2,1,0:T(8,128)S(1)} %get-tuple-element.38), channel_id=1, source_target_pairs={{0,31},{1,2},{2,1},{3,4},{4,3},{5,6},{6,5},{7,8},{8,7},{9,10},{10,... | collective-permute-start | bytes 589832 | tf_op jit(solution)/shard_map/ppermute | solution.py:293
  9.9 7.3 %collective-permute-start.1 = (f32[48,8,128]{2,1,0:T(8,128)S(1)}, f32[48,8,128]{2,1,0:T(8,128)S(1)}, u32[]{:S(2)}, u32[]{:S(2)}) collective-permute-start(f32[48,8,128]{2,1,0:T(8,128)S(1)} %get-tuple-element.39), channel_id=1, source_target_pairs={{0,1},{1,0},{2,3},{3,2},{4,5},{5,4},{6,7},{7,6},{8,9},{9,8},{10,11... | collective-permute-start | bytes 589832 | tf_op jit(solution)/shard_map/ppermute | solution.py:294
  11.9 0.9 copy-start.1
  22.6 40.3 %copy-start = (f32[1,96,8,128]{3,2,1,0:T(8,128)S(1)}, f32[1,96,8,128]{3,2,1,0:T(8,128)}, u32[]{:S(2)}) copy-start(f32[1,96,8,128]{3,2,1,0:T(8,128)} %param.5) | copy-start | bytes 1179652
  57.6 11.3 %collective-permute-start.2 = (f32[48,8,128]{2,1,0:T(8,128)S(1)}, f32[48,8,128]{2,1,0:T(8,128)S(1)}, u32[]{:S(2)}, u32[]{:S(2)}) collective-permute-start(f32[48,8,128]{2,1,0:T(8,128)S(1)} %get-tuple-element.51), channel_id=1, source_target_pairs={{0,31},{1,2},{2,1},{3,4},{4,3},{5,6},{6,5},{7,8},{8,7},{9,10},{10,... | collective-permute-start | bytes 589832 | tf_op jit(solution)/shard_map/ppermute | solution.py:340
  60.9 8.0 %collective-permute-start.3 = (f32[48,8,128]{2,1,0:T(8,128)S(1)}, f32[48,8,128]{2,1,0:T(8,128)S(1)}, u32[]{:S(2)}, u32[]{:S(2)}) collective-permute-start(f32[48,8,128]{2,1,0:T(8,128)S(1)} %get-tuple-element.52), channel_id=1, source_target_pairs={{0,1},{1,0},{2,3},{3,2},{4,5},{5,4},{6,7},{7,6},{8,9},{9,8},{10,11... | collective-permute-start | bytes 589832 | tf_op jit(solution)/shard_map/ppermute | solution.py:341
